TPU v7x, 128 devices: a whole 4x4x4 slice. The times are simulated.
128 devices in a mesh: section: 2 (over core), dp: 64 (over x, y, z).
Axes of the slice: x: 4, y: 4, z: 4, core: 2. Of those that a mesh axis runs over, the one named last changes fastest.
Arguments:
- ends: bfloat16 [2, 3, 4096, 896], P('section', None, 'dp'), may hold values from -9 to 9
- segment_ids: int32 [3, 4096], replicated, may hold values from 0 to 3, as said below
- valid_blocks: int32 [3, 32], replicated, may hold values from 0 to 1, as said below
- qkv_weight: bfloat16 [2, 896, 1152], P('section', 'dp'), may hold values from -0.1875 to 0.1875
- qkv_bias: bfloat16 [2, 1152], P('section'), may hold values from -3 to 3
- out_weight: bfloat16 [2, 896, 896], P('section', 'dp'), may hold values from -2 to 2
- gate_up_weight: bfloat16 [2, 896, 9728], P('section', 'dp'), may hold values from -0.1875 to 0.1875
- down_weight: bfloat16 [2, 896, 4864], P('section', 'dp'), may hold values from -0.078125 to 0.078125
- norm_gains: bfloat16 [2, 2, 896], P('section'), may hold values from 0.5 to 1.5
Outputs:
- boundary: bfloat16 [2, 3, 4096, 896], P('section', None, 'dp')
- qkv_weight_grad: float32 [2, 896, 1152], P('section', 'dp')
- qkv_bias_grad: float32 [2, 1152], P('section')
- out_weight_grad: float32 [2, 896, 896], P('section', 'dp')
- gate_up_weight_grad: float32 [2, 896, 9728], P('section', 'dp')
- down_weight_grad: float32 [2, 896, 4864], P('section', 'dp')
- norm_gains_grad: float32 [2, 2, 896], P('section')
- rms_stats: float32 [2, 3, 3], P('section')
Inputs may be any that keep to these rules, and one draw needn't show every extreme that they name: `segment_ids`: along each micro-batch the ids never fall; in one micro-batch, drawn from the seed, all tokens form one document. `valid_blocks`: in each micro-batch the valid blocks form a prefix of 16 blocks or more; every block of the single-document micro-batch is valid.
All inputs are finite; a program needn't handle non-finite values.
Results may differ from a plain program's by a relative error of at most 0.013.
Values may be sent and summed in bfloat16 or wider, within the bound.
A program may use at most 320 MiB of HBM per device.

v0:
```python
import math

import jax
import jax.numpy as jnp
from jax import lax
from jax.sharding import PartitionSpec as P

HEADS = 14
KV_HEADS = 2
HEAD = 64
FF = 4864
BLOCK = 128


EPS = 1e-06
THETA = 1000000.0
MASKED = -1e30


def passed_along(block, axis, distance):
    devices = range(lax.axis_size(axis))
    route = [(i - distance, i) for i in devices if i - distance in devices]
    return lax.ppermute(block, axis, route)


def matmul(left, right):
    return jnp.dot(left, right, preferred_element_type=jnp.float32)


def contract_last(left, right):
    return lax.dot_general(
        left, right, (((1,), (1,)), ((), ())), preferred_element_type=jnp.float32
    )


def contract_first(left, right):
    return lax.dot_general(
        left, right, (((0,), (0,)), ((), ())), preferred_element_type=jnp.float32
    )


def normalize(features, gain_vec):
    scale_rows = lax.rsqrt(jnp.mean(features * features, axis=-1, keepdims=True) + EPS)
    return (features * scale_rows * gain_vec, scale_rows)


def norm_back(grad_in, features, scale_rows, gain_vec):
    scaled = grad_in * gain_vec
    grad_out = scale_rows * scaled - features * scale_rows**3 * jnp.mean(
        scaled * features, axis=-1, keepdims=True
    )
    return (grad_out, jnp.sum(grad_in * features * scale_rows, axis=0))


def rotate(heads_in, cosine_rows, sine_rows):
    half_size = heads_in.shape[-1] // 2
    first_half = heads_in[..., :half_size]
    second_half = heads_in[..., half_size:]
    cos_part = cosine_rows[:, None, :]
    sin_part = sine_rows[:, None, :]
    return jnp.concatenate(
        [
            first_half * cos_part - second_half * sin_part,
            second_half * cos_part + first_half * sin_part,
        ],
        axis=-1,
    )


def weight_builder(operands):
    (
        normed_all,
        grad_proj_all,
        grad_branch_all,
        attended_all,
        normed_two_all,
        grad_gu_all,
        grad_mlp_all,
        hidden_all,
    ) = operands
    return jnp.concatenate(
        [
            contract_first(normed_all, grad_proj_all),
            contract_first(grad_branch_all, attended_all),
            contract_first(normed_two_all, grad_gu_all),
            contract_first(grad_mlp_all, hidden_all),
        ],
        axis=1,
    )


def shards(
    ends,
    segment_ids,
    valid_blocks,
    qkv_weight,
    qkv_bias,
    out_weight,
    gate_up_weight,
    down_weight,
    norm_gains,
):
    section_index = lax.axis_index("section")
    shard_index = lax.axis_index("dp")
    inputs = ends[0]
    batches, tokens, model_width = inputs.shape
    seq_len = segment_ids.shape[1]
    groups = HEADS // KV_HEADS
    head_total = HEADS * HEAD
    kv_total = KV_HEADS * HEAD
    qkv_total = head_total + 2 * kv_total
    softmax_scale = 1.0 / math.sqrt(HEAD)
    bias_vec = qkv_bias[0].astype(jnp.float32)
    gain_rows = norm_gains[0].astype(jnp.float32)
    local_weights = (qkv_weight[0], out_weight[0], gate_up_weight[0], down_weight[0])
    gathered = (
        lax.all_gather(local_weights[0], "dp", axis=0, tiled=True),
        lax.all_gather(local_weights[1], "dp", axis=0, tiled=True),
        lax.all_gather(local_weights[2], "dp", axis=0, tiled=True),
        lax.all_gather(local_weights[3], "dp", axis=0, tiled=True),
    )
    key_valid = jnp.repeat(valid_blocks, BLOCK, axis=1)
    key_pos = jnp.arange(seq_len, dtype=jnp.int32)
    query_pos = shard_index * tokens + jnp.arange(tokens, dtype=jnp.int32)
    frequency = THETA ** (-jnp.arange(HEAD // 2, dtype=jnp.float32) * 2.0 / HEAD)
    angles = query_pos.astype(jnp.float32)[:, None] * frequency[None, :]
    cosine_rows = jnp.cos(angles)
    sine_rows = jnp.sin(angles)

    def allowed_pairs(batch_index):
        segment_row = segment_ids[batch_index]
        valid_row = key_valid[batch_index]
        local_segment = lax.dynamic_slice_in_dim(segment_row, shard_index * tokens, tokens)
        local_valid = lax.dynamic_slice_in_dim(valid_row, shard_index * tokens, tokens)
        same_doc = local_segment[:, None] == segment_row[None, :]
        causal = key_pos[None, :] <= query_pos[:, None]
        usable = (valid_row[None, :] > 0) | (key_pos[None, :] == query_pos[:, None])
        return (same_doc & causal & usable, local_valid)

    def scores_of(grouped, all_keys, allowed):
        key_heads = all_keys.reshape(seq_len, KV_HEADS, HEAD)
        raw_scores = (
            jnp.einsum("qngd,knd->ngqk", grouped, key_heads, preferred_element_type=jnp.float32)
            * softmax_scale
        )
        return jnp.where(allowed[None, None], raw_scores, MASKED)

    zeros_rows = jnp.zeros((tokens, model_width), jnp.bfloat16)
    received = zeros_rows
    outputs = []
    saved_all = []
    squares_all = []
    for step_num in range(batches + 1):
        batch_index = jnp.clip(step_num - section_index, 0, batches - 1)
        first_in = inputs[min(step_num, batches - 1)]
        hidden_in = jnp.where(section_index == 0, first_in, received).astype(jnp.float32)
        forward_w_qkv, forward_w_out, forward_w_gate_up, forward_w_down = gathered
        forward_allowed, forward_local_valid = allowed_pairs(batch_index)
        forward_normed, forward_scale_one = normalize(hidden_in, gain_rows[0])
        forward_normed = forward_normed.astype(jnp.bfloat16)
        projected = matmul(forward_normed, forward_w_qkv) + bias_vec
        forward_queries = rotate(
            projected[:, :head_total].reshape(tokens, HEADS, HEAD), cosine_rows, sine_rows
        ).astype(jnp.bfloat16)
        forward_key_local = rotate(
            projected[:, head_total : head_total + kv_total].reshape(tokens, KV_HEADS, HEAD),
            cosine_rows,
            sine_rows,
        )
        forward_key_local = forward_key_local.astype(jnp.bfloat16).reshape(tokens, kv_total)
        forward_value_local = projected[:, head_total + kv_total :].astype(jnp.bfloat16)
        forward_all_keys = lax.all_gather(forward_key_local, "dp", axis=0, tiled=True)
        forward_all_values = lax.all_gather(forward_value_local, "dp", axis=0, tiled=True)
        forward_grouped = forward_queries.reshape(tokens, KV_HEADS, groups, HEAD)
        forward_scores = scores_of(forward_grouped, forward_all_keys, forward_allowed)
        row_max = jnp.max(forward_scores, axis=-1, keepdims=True)
        exponents = jnp.exp(forward_scores - row_max)
        row_total = jnp.sum(exponents, axis=-1, keepdims=True)
        forward_prob_table = exponents / row_total
        forward_log_total = row_max + jnp.log(row_total)
        mixed = jnp.einsum(
            "ngqk,knd->qngd",
            forward_prob_table.astype(jnp.bfloat16),
            forward_all_values.reshape(seq_len, KV_HEADS, HEAD),
            preferred_element_type=jnp.float32,
        )
        forward_attended = mixed.reshape(tokens, head_total).astype(jnp.bfloat16)
        branch = contract_last(forward_attended, forward_w_out)
        forward_middle = hidden_in + branch
        forward_normed_two, forward_scale_two = normalize(forward_middle, gain_rows[1])
        forward_normed_two = forward_normed_two.astype(jnp.bfloat16)
        forward_gate_up = matmul(forward_normed_two, forward_w_gate_up)
        forward_hidden = (jax.nn.silu(forward_gate_up[:, :FF]) * forward_gate_up[:, FF:]).astype(
            jnp.bfloat16
        )
        mlp_out = contract_last(forward_hidden, forward_w_down)
        output = forward_middle + mlp_out
        valid_weight = forward_local_valid.astype(jnp.float32)[:, None]
        squares = jnp.stack(
            [
                jnp.sum(hidden_in * hidden_in * valid_weight),
                jnp.sum(branch * branch * valid_weight),
                jnp.sum(mlp_out * mlp_out * valid_weight),
            ]
        )
        forward_saved_state = (
            hidden_in,
            forward_scale_one,
            forward_normed,
            forward_queries,
            forward_key_local,
            forward_value_local,
            forward_all_keys,
            forward_all_values,
            forward_log_total,
            forward_attended,
            forward_middle,
            forward_scale_two,
            forward_normed_two,
            forward_gate_up,
            forward_hidden,
            batch_index,
        )
        output, saved_state, squares = (output, forward_saved_state, squares)
        outputs.append(output.astype(jnp.bfloat16))
        saved_all.append(saved_state)
        squares_all.append(squares)
        if step_num < batches:
            received = passed_along(output.astype(jnp.bfloat16), "section", 1)
    back_weights = (
        lax.all_gather(local_weights[0], "dp", axis=0, tiled=True),
        lax.all_gather(local_weights[1], "dp", axis=0, tiled=True),
        lax.all_gather(local_weights[2], "dp", axis=0, tiled=True),
        lax.all_gather(local_weights[3], "dp", axis=0, tiled=True),
    )
    coming = zeros_rows
    grads_by_step = [None] * (batches + 1)
    input_grads = []
    gain_sum = jnp.zeros((2, model_width), jnp.float32)
    bias_sum = jnp.zeros((head_total + 2 * kv_total,), jnp.float32)
    for back_step in range(batches + 1):
        step_num = batches - back_step
        if back_step < batches:
            cot_rows = inputs[batches - 1 - back_step]
        else:
            cot_rows = zeros_rows
        grad_in = jnp.where(section_index == 1, cot_rows, coming).astype(jnp.float32)
        (
            backward_hidden_in,
            scale_one,
            normed,
            queries,
            key_local,
            value_local,
            kept_keys,
            kept_values,
            log_total,
            attended,
            middle,
            scale_two,
            normed_two,
            gate_up,
            hidden,
            backward_batch_index,
        ) = saved_all[step_num]
        w_qkv, w_out, w_gate_up, w_down = back_weights
        backward_allowed = allowed_pairs(backward_batch_index)[0]
        grad_mlp = grad_in.astype(jnp.bfloat16)
        grad_hidden = matmul(grad_mlp, w_down)
        gate_part = gate_up[:, :FF]
        up_part = gate_up[:, FF:]
        sigmoid_gate = jax.nn.sigmoid(gate_part)
        grad_gate = grad_hidden * up_part * sigmoid_gate * (1.0 + gate_part * (1.0 - sigmoid_gate))
        grad_up = grad_hidden * gate_part * sigmoid_gate
        grad_gate_up = jnp.concatenate([grad_gate, grad_up], axis=1).astype(jnp.bfloat16)
        grad_normed_two = contract_last(grad_gate_up, w_gate_up)
        grad_middle, gain_two = norm_back(grad_normed_two, middle, scale_two, gain_rows[1])
        grad_middle = grad_middle + grad_in
        grad_branch = grad_middle.astype(jnp.bfloat16)
        grad_attended = matmul(grad_branch, w_out).astype(jnp.bfloat16)
        backward_grouped = queries.reshape(tokens, KV_HEADS, groups, HEAD)
        scores = scores_of(backward_grouped, kept_keys, backward_allowed)
        prob_table = jnp.exp(scores - log_total)
        value_heads = kept_values.reshape(seq_len, KV_HEADS, HEAD)
        grad_heads = grad_attended.reshape(tokens, KV_HEADS, groups, HEAD)
        grad_probs = jnp.einsum(
            "qngd,knd->ngqk", grad_heads, value_heads, preferred_element_type=jnp.float32
        )
        row_inner = jnp.sum(prob_table * grad_probs, axis=-1, keepdims=True)
        grad_scores = (prob_table * (grad_probs - row_inner)).astype(jnp.bfloat16)
        grad_queries = (
            jnp.einsum(
                "ngqk,knd->qngd",
                grad_scores,
                kept_keys.reshape(seq_len, KV_HEADS, HEAD),
                preferred_element_type=jnp.float32,
            )
            * softmax_scale
        )
        grad_keys = (
            jnp.einsum(
                "ngqk,qngd->knd", grad_scores, backward_grouped, preferred_element_type=jnp.float32
            )
            * softmax_scale
        )
        grad_values = jnp.einsum(
            "ngqk,qngd->knd",
            prob_table.astype(jnp.bfloat16),
            grad_heads,
            preferred_element_type=jnp.float32,
        )
        key_terms = jnp.concatenate(
            [grad_keys.reshape(seq_len, kv_total), grad_values.reshape(seq_len, kv_total)], axis=1
        )
        own_keys = lax.psum_scatter(key_terms, "dp", scatter_dimension=0, tiled=True)
        grad_key_rot = own_keys[:, :kv_total].reshape(tokens, KV_HEADS, HEAD)
        grad_value_local = own_keys[:, kv_total:]
        grad_projected = jnp.concatenate(
            [
                rotate(grad_queries.reshape(tokens, HEADS, HEAD), cosine_rows, -sine_rows).reshape(
                    tokens, head_total
                ),
                rotate(grad_key_rot, cosine_rows, -sine_rows).reshape(tokens, kv_total),
                grad_value_local,
            ],
            axis=1,
        ).astype(jnp.bfloat16)
        grad_bias = jnp.sum(grad_projected.astype(jnp.float32), axis=0)
        grad_normed = contract_last(grad_projected, w_qkv)
        grad_input, gain_one = norm_back(grad_normed, backward_hidden_in, scale_one, gain_rows[0])
        grad_input = grad_input + grad_middle
        products = (
            normed,
            grad_projected,
            grad_branch,
            attended,
            normed_two,
            grad_gate_up,
            grad_mlp,
            hidden,
        )
        grad_input, products, smalls = (
            grad_input,
            products,
            (jnp.stack([gain_one, gain_two]), grad_bias),
        )
        grads_by_step[step_num] = products
        gain_sum = gain_sum + smalls[0]
        bias_sum = bias_sum + smalls[1]
        input_grads.append(grad_input)
        if back_step < batches:
            coming = passed_along(grad_input.astype(jnp.bfloat16), "section", -1)

    def select_steps(members):
        stacked = jnp.stack(members)
        chosen = lax.dynamic_slice_in_dim(stacked, section_index, batches, 0)
        return chosen.reshape((batches * chosen.shape[1],) + chosen.shape[2:])

    operands = tuple(
        (
            select_steps([grads_by_step[index_num][member] for index_num in range(batches + 1)])
            for member in range(8)
        )
    )
    summed = lax.psum_scatter(weight_builder(operands), "dp", scatter_dimension=0, tiled=True)
    grad_qkv_w = summed[:, :qkv_total]
    grad_out_w = summed[:, qkv_total : qkv_total + head_total]
    grad_gu_w = summed[:, qkv_total + head_total : qkv_total + head_total + 2 * FF]
    grad_down_w = summed[:, qkv_total + head_total + 2 * FF :]
    squares_pick = lax.dynamic_slice_in_dim(jnp.stack(squares_all), section_index, batches, 0)
    total_squares, gain_grad, bias_grad = lax.psum((squares_pick, gain_sum, bias_sum), "dp")
    valid_counts = jnp.sum(valid_blocks, axis=1).astype(jnp.float32) * BLOCK * model_width
    rms_values = jnp.sqrt(total_squares / valid_counts[:, None])
    grad_stack = jnp.stack(input_grads[::-1][:batches]).astype(jnp.bfloat16)
    out_stack = jnp.stack(outputs[1:])
    boundary = jnp.where(section_index == 0, grad_stack, out_stack)[None]
    return (
        boundary,
        grad_qkv_w[None],
        bias_grad[None],
        grad_out_w[None],
        grad_gu_w[None],
        grad_down_w[None],
        gain_grad[None],
        rms_values[None],
    )


def solution(mesh):
    in_specs = (
        P("section", None, "dp", None),
        P(),
        P(),
        P("section", "dp", None),
        P("section", None),
        P("section", "dp", None),
        P("section", "dp", None),
        P("section", "dp", None),
        P("section", None, None),
    )
    out_specs = (
        P("section", None, "dp", None),
        P("section", "dp", None),
        P("section", None),
        P("section", "dp", None),
        P("section", "dp", None),
        P("section", "dp", None),
        P("section", None, None),
        P("section", None, None),
    )
    return jax.shard_map(shards, mesh=mesh, in_specs=in_specs, out_specs=out_specs, check_vma=False)
```

profile of v0, /device:TPU:1, one launch (start us, length us, event | category | flops | bytes accessed | tf_op | source)
XLA Modules:
  0.0 3309.8 jit_solution(15159623778127314429)
XLA Ops:
  14.0 68.4 %all-gather.33.cloned.1.call-done = bf16[1,896,1152]{2,0,1:T(2,128)(2,1)} async-done(((bf16[1,14,1152]{2,0,1:T(2,128)(2,1)}), bf16[1,896,1152]{2,0,1:T(2,128)(2,1)}) %all-gather.33.cloned.1.call-update) | async-done | bytes 2064400 | tf_op jit(solution)/shard_map/all_gather | solution.py:117
  93.2 57.6 %all-gather.35.cloned.1.call-done = bf16[1,896,896]{2,0,1:T(2,128)(2,1)} async-done(((bf16[1,14,896]{2,0,1:T(2,128)(2,1)}), bf16[1,896,896]{2,0,1:T(2,128)(2,1)}) %all-gather.35.cloned.1.call-update) | async-done | bytes 1605648 | tf_op jit(solution)/shard_map/all_gather | solution.py:118
  159.7 54.6 %all-gather.17.cloned.1.call-done = bf16[4096,128]{1,0:T(8,128)(2,1)} async-done(((bf16[64,128]{1,0:T(8,128)(2,1)}), bf16[4096,128]{1,0:T(8,128)(2,1)}) %all-gather.17.cloned.1.call-update) | async-done | bytes 1048592 | tf_op jit(solution)/shard_map/all_gather | solution.py:172
  217.0 62.0 %all-gather.19.cloned.1.call-done = bf16[4096,128]{1,0:T(8,128)(2,1)} async-done(((bf16[64,128]{1,0:T(8,128)(2,1)}), bf16[4096,128]{1,0:T(8,128)(2,1)}) %all-gather.19.cloned.1.call-update) | async-done | bytes 1048592 | tf_op jit(solution)/shard_map/all_gather | solution.py:173
  281.3 9.0 fusion.298
  290.3 7.6 fusion.28
  298.0 8.7 fusion.130
  309.8 78.1 %all-gather.39.cloned.1.call-done = bf16[1,896,4864]{2,0,1:T(2,128)(2,1)} async-done(((bf16[1,14,4864]{2,0,1:T(2,128)(2,1)}), bf16[1,896,4864]{2,0,1:T(2,128)(2,1)}) %all-gather.39.cloned.1.call-update) | async-done | bytes 8716304 | tf_op jit(solution)/shard_map/all_gather | solution.py:120
  387.9 11.5 copy.270
  399.3 156.9 %all-gather.37.cloned.1.call-done = bf16[1,896,9728]{2,0,1:T(2,128)(2,1)} async-done(((bf16[1,14,9728]{2,0,1:T(2,128)(2,1)}), bf16[1,896,9728]{2,0,1:T(2,128)(2,1)}) %all-gather.37.cloned.1.call-update) | async-done | bytes 17432592 | tf_op jit(solution)/shard_map/all_gather | solution.py:119
  556.3 15.7 copy.269
  598.2 55.7 %all-gather.21.cloned.1.call-done = bf16[4096,128]{1,0:T(8,128)(2,1)} async-done(((bf16[64,128]{1,0:T(8,128)(2,1)}), bf16[4096,128]{1,0:T(8,128)(2,1)}) %all-gather.21.cloned.1.call-update) | async-done | bytes 1048592 | tf_op jit(solution)/shard_map/all_gather | solution.py:172
  656.3 8.9 fusion.299
  665.2 7.3 fusion.29
  672.5 46.4 %all-gather.23.cloned.1.call-done = bf16[4096,128]{1,0:T(8,128)(2,1)} async-done(((bf16[64,128]{1,0:T(8,128)(2,1)}), bf16[4096,128]{1,0:T(8,128)(2,1)}) %all-gather.23.cloned.1.call-update) | async-done | bytes 1048592 | tf_op jit(solution)/shard_map/all_gather | solution.py:173
  721.5 8.9 fusion.129
  735.7 7.8 multiply_reduce_fusion.5
  754.3 56.4 %all-gather.25.cloned.1.call-done = bf16[4096,128]{1,0:T(8,128)(2,1)} async-done(((bf16[64,128]{1,0:T(8,128)(2,1)}), bf16[4096,128]{1,0:T(8,128)(2,1)}) %all-gather.25.cloned.1.call-update) | async-done | bytes 1048592 | tf_op jit(solution)/shard_map/all_gather | solution.py:172
  813.3 9.0 fusion.300
  822.3 7.3 fusion.30
  829.6 45.8 %all-gather.27.cloned.1.call-done = bf16[4096,128]{1,0:T(8,128)(2,1)} async-done(((bf16[64,128]{1,0:T(8,128)(2,1)}), bf16[4096,128]{1,0:T(8,128)(2,1)}) %all-gather.27.cloned.1.call-update) | async-done | bytes 1048592 | tf_op jit(solution)/shard_map/all_gather | solution.py:173
  877.7 8.9 fusion.128
  887.5 7.4 fusion.10
  906.0 58.0 %all-gather.29.cloned.1.call-done = bf16[4096,128]{1,0:T(8,128)(2,1)} async-done(((bf16[64,128]{1,0:T(8,128)(2,1)}), bf16[4096,128]{1,0:T(8,128)(2,1)}) %all-gather.29.cloned.1.call-update) | async-done | bytes 1048592 | tf_op jit(solution)/shard_map/all_gather | solution.py:172
  965.5 6.5 fusion.301
  972.0 7.3 fusion.31
  979.3 49.4 %all-gather.31.cloned.1.call-done = bf16[4096,128]{1,0:T(8,128)(2,1)} async-done(((bf16[64,128]{1,0:T(8,128)(2,1)}), bf16[4096,128]{1,0:T(8,128)(2,1)}) %all-gather.31.cloned.1.call-update) | async-done | bytes 1048592 | tf_op jit(solution)/shard_map/all_gather | solution.py:173
  1030.3 8.9 fusion.127
  1040.0 7.6 fusion.8
  1049.9 12.6 multiply_reduce_fusion.11
  1062.5 6.3 fusion.36
  1070.9 13.9 fusion.25
  1088.5 7.5 fusion.27
  1109.3 6.2 convolution_multiply_fusion.3
  1121.2 294.2 %reduce-scatter.5.cloned.1.call-done = f32[64,256]{1,0:T(8,128)} async-done(((f32[4096,256]{1,0:T(8,128)}), f32[64,256]{1,0:T(8,128)}) %reduce-scatter.5.cloned.1.call-update) | async-done | bytes 65552 | tf_op jit(solution)/shard_map/reduce_scatter | solution.py:315
  1419.6 52.3 %collective-permute-start.3 = (bf16[64,896]{1,0:T(8,128)(2,1)S(1)}, bf16[64,896]{1,0:T(8,128)(2,1)S(1)}, u32[]{:S(2)}, u32[]{:S(2)}) collective-permute-start(bf16[64,896]{1,0:T(8,128)(2,1)S(1)} %get-tuple-element.160), channel_id=1, source_target_pairs={{64,0},{65,1},{66,2},{67,3},{68,4},{69,5},{70,6},{71,7},{72,8},{73... | collective-permute-start | bytes 344072 | tf_op jit(solution)/shard_map/ppermute | solution.py:23
  1472.9 6.7 multiply_convert_fusion.6
  1479.6 12.3 multiply_reduce_fusion.10
  1494.9 13.8 fusion.22
  1508.7 9.2 fusion.54
  1517.9 7.7 fusion.24
  1539.4 6.5 convolution_multiply_fusion.2
  1551.6 290.7 %reduce-scatter.7.cloned.1.call-done = f32[64,256]{1,0:T(8,128)} async-done(((f32[4096,256]{1,0:T(8,128)}), f32[64,256]{1,0:T(8,128)}) %reduce-scatter.7.cloned.1.call-update) | async-done | bytes 65552 | tf_op jit(solution)/shard_map/reduce_scatter | solution.py:315
  1847.5 52.2 %collective-permute-start.4 = (bf16[64,896]{1,0:T(8,128)(2,1)S(1)}, bf16[64,896]{1,0:T(8,128)(2,1)S(1)}, u32[]{:S(2)}, u32[]{:S(2)}) collective-permute-start(bf16[64,896]{1,0:T(8,128)(2,1)S(1)} %get-tuple-element.162), channel_id=1, source_target_pairs={{64,0},{65,1},{66,2},{67,3},{68,4},{69,5},{70,6},{71,7},{72,8},{73... | collective-permute-start | bytes 344072 | tf_op jit(solution)/shard_map/ppermute | solution.py:23
  1900.5 6.7 multiply_convert_fusion.4
  1907.2 13.0 multiply_reduce_fusion.9
  1924.1 13.8 fusion.19
  1937.9 9.2 fusion.56
  1947.1 7.8 fusion.21
  1969.1 6.5 convolution_multiply_fusion.1
  1981.1 290.7 %reduce-scatter.9.cloned.1.call-done = f32[64,256]{1,0:T(8,128)} async-done(((f32[4096,256]{1,0:T(8,128)}), f32[64,256]{1,0:T(8,128)}) %reduce-scatter.9.cloned.1.call-update) | async-done | bytes 65552 | tf_op jit(solution)/shard_map/reduce_scatter | solution.py:315
  2277.7 52.5 %collective-permute-start.5 = (bf16[64,896]{1,0:T(8,128)(2,1)S(1)}, bf16[64,896]{1,0:T(8,128)(2,1)S(1)}, u32[]{:S(2)}, u32[]{:S(2)}) collective-permute-start(bf16[64,896]{1,0:T(8,128)(2,1)S(1)} %get-tuple-element.164), channel_id=1, source_target_pairs={{64,0},{65,1},{66,2},{67,3},{68,4},{69,5},{70,6},{71,7},{72,8},{73... | collective-permute-start | bytes 344072 | tf_op jit(solution)/shard_map/ppermute | solution.py:23
  2331.0 6.7 multiply_convert_fusion.2
  2337.7 13.0 multiply_reduce_fusion.8
  2354.6 13.7 fusion.16
  2368.3 9.1 fusion.58
  2377.5 7.7 fusion.18
  2421.7 6.6 convolution_multiply_fusion
  2440.1 8.7 convolution_bitcast_fusion.1
  2449.0 15.1 convolution_bitcast_fusion
  2464.1 237.9 %reduce-scatter.11.cloned.1.call-done = f32[64,256]{1,0:T(8,128)} async-done(((f32[4096,256]{1,0:T(8,128)}), f32[64,256]{1,0:T(8,128)}) %reduce-scatter.11.cloned.1.call-update) | async-done | bytes 65552 | tf_op jit(solution)/shard_map/reduce_scatter | solution.py:315
  2708.3 38.4 %pad_maximum_fusion = f32[896,16640]{1,0:T(8,128)} fusion(f32[896,4864]{1,0:T(8,128)} %convolution_bitcast_fusion.1, f32[896,9728]{1,0:T(8,128)} %convolution_bitcast_fusion, f32[896,896]{1,0:T(8,128)} %convolution_bitcast_fusion.7, f32[896,1152]{1,0:T(8,128)} %convolution_bitcast_fusion.6), kind=kLoop, calls=%fused_computation | loop fusion | flops 44728320 | bytes 119275520 | tf_op jit(solution)/shard_map/concatenate | solution.py:81
  2773.5 296.6 %all-reduce.1 = (f32[1,1152]{1,0:T(1,128)}, f32[1,2,896]{2,1,0:T(2,128)}, f32[3,3]{1,0:T(4,128)S(1)}) all-reduce(f32[1,1152]{1,0:T(1,128)S(1)} %broadcast_in_dim.75, f32[1,2,896]{2,1,0:T(2,128)S(1)} %fusion.266, f32[3,3]{1,0:T(4,128)S(1)} %constant_dynamic-slice_fusion), channel_id=1, replica_groups=mesh['section'=2,'dp'=64] {'dp'}, use_global_device_ids=true, to_apply=%region_37.38 | all-reduce | flops 2953 | bytes 23624 | tf_op jit(solution)/shard_map/psum | solution.py:371
  3073.9 220.9 %all-reduce.4.cloned.1.call-done = f32[896,16640]{1,0:T(8,128)} async-done(((f32[896,16640]{1,0:T(8,128)}), f32[896,16640]{1,0:T(8,128)}) %all-reduce.4.cloned.1.call-update) | async-done | bytes 59637776
  (656 shorter events, 288.1 us)
Async XLA Ops:
  7.2 75.3 %all-gather.33.cloned.1.call-start = ((), (), s32[]{:S(2)}) async-start(), calls=%async_computation.16 | async-start | bytes 4193280 | tf_op jit(solution)/shard_map/all_gather | solution.py:117
  8.7 142.1 %all-gather.35.cloned.1.call-start = ((), (), s32[]{:S(2)}) async-start(), calls=%async_computation.17 | async-start | bytes 3261440 | tf_op jit(solution)/shard_map/all_gather | solution.py:118
  10.2 204.1 %all-gather.17.cloned.1.call-start = ((), (), s32[]{:S(2)}) async-start(), calls=%async_computation.4 | async-start | bytes 1064960 | tf_op jit(solution)/shard_map/all_gather | solution.py:172
  13.2 73.4 %copy-start.137 = (f32[64]{0:T(128)}, f32[64]{0:T(128)S(1)}, u32[]{:S(2)}) copy-start(f32[64]{0:T(128)S(1)} %get-tuple-element.181) | copy-start | bytes 772
  14.0 74.5 %copy-start.98 = (bf16[1,14,4864]{2,1,0:T(8,128)(2,1)S(1)}, bf16[1,14,4864]{2,1,0:T(8,128)(2,1)}, u32[]{:S(2)}) copy-start(bf16[1,14,4864]{2,1,0:T(8,128)(2,1)} %param.16) | copy-start | bytes 408580
  14.0 75.5 %copy-start.93 = (bf16[1,14,9728]{2,1,0:T(8,128)(2,1)S(1)}, bf16[1,14,9728]{2,1,0:T(8,128)(2,1)}, u32[]{:S(2)}) copy-start(bf16[1,14,9728]{2,1,0:T(8,128)(2,1)} %param.15) | copy-start | bytes 817156
  14.0 76.8 %copy-start.135 = (s32[3,32]{1,0:T(4,128)S(1)}, s32[3,32]{1,0:T(4,128)}, u32[]{:S(2)}) copy-start(s32[3,32]{1,0:T(4,128)} %param.11) | copy-start | bytes 1156
  85.0 818.1 %copy-start.1 = (bf16[1,896,1152]{2,1,0:T(8,128)(2,1)}, bf16[1,896,1152]{2,1,0:T(8,128)(2,1)S(1)}, u32[]{:S(2)}) copy-start(bf16[1,896,1152]{2,1,0:T(8,128)(2,1)S(1)} %copy.267) | copy-start | bytes 6193156
  87.8 191.2 %all-gather.19.cloned.1.call-start = ((), (), s32[]{:S(2)}) async-start(), calls=%async_computation.5 | async-start | bytes 1064960 | tf_op jit(solution)/shard_map/all_gather | solution.py:173
  88.5 299.4 %all-gather.39.cloned.1.call-start = ((), (), s32[]{:S(2)}) async-start(), calls=%async_computation.19 | async-start | bytes 17704960 | tf_op jit(solution)/shard_map/all_gather | solution.py:120
  89.5 466.8 %all-gather.37.cloned.1.call-start = ((), (), s32[]{:S(2)}) async-start(), calls=%async_computation.18 | async-start | bytes 35409920 | tf_op jit(solution)/shard_map/all_gather | solution.py:119
  90.8 563.2 %all-gather.21.cloned.1.call-start = ((), (), s32[]{:S(2)}) async-start(), calls=%async_computation.6 | async-start | bytes 1064960 | tf_op jit(solution)/shard_map/all_gather | solution.py:172
  91.8 488.9 %copy-start.143 = (f32[64]{0:T(128)}, f32[64]{0:T(128)S(1)}, u32[]{:S(2)}) copy-start(f32[64]{0:T(128)S(1)} %get-tuple-element.165) | copy-start | bytes 772
  91.8 643.8 %copy-start.144 = (f32[64]{0:T(128)}, f32[64]{0:T(128)S(1)}, u32[]{:S(2)}) copy-start(f32[64]{0:T(128)S(1)} %get-tuple-element.168) | copy-start | bytes 772
  91.8 803.1 %copy-start.145 = (f32[64]{0:T(128)}, f32[64]{0:T(128)S(1)}, u32[]{:S(2)}) copy-start(f32[64]{0:T(128)S(1)} %get-tuple-element.167) | copy-start | bytes 772
  309.1 271.6 %copy-start.22 = (f32[64,896]{1,0:T(8,128)}, f32[64,896]{1,0:T(8,128)S(1)}, u32[]{:S(2)}) copy-start(f32[64,896]{1,0:T(8,128)S(1)} %get-tuple-element.98) | copy-start | bytes 688132
  309.8 262.2 %copy-start.131 = (f32[64]{0:T(128)}, f32[64]{0:T(128)S(1)}, u32[]{:S(2)}) copy-start(f32[64]{0:T(128)S(1)} %get-tuple-element.183) | copy-start | bytes 772
  586.0 3.2 collective-permute-start
  590.3 140.2 %copy-start.28 = (bf16[64,896]{1,0:T(8,128)(2,1)}, bf16[64,896]{1,0:T(8,128)(2,1)S(1)}, u32[]{:S(2)}) copy-start(bf16[64,896]{1,0:T(8,128)(2,1)S(1)} %get-tuple-element.96) | copy-start | bytes 344068
  592.5 126.4 %all-gather.23.cloned.1.call-start = ((), (), s32[]{:S(2)}) async-start(), calls=%async_computation.7 | async-start | bytes 1064960 | tf_op jit(solution)/shard_map/all_gather | solution.py:173
  593.3 217.4 %all-gather.25.cloned.1.call-start = ((), (), s32[]{:S(2)}) async-start(), calls=%async_computation.8 | async-start | bytes 1064960 | tf_op jit(solution)/shard_map/all_gather | solution.py:172
  743.5 4.6 collective-permute-start.1
  749.1 137.6 %copy-start.30 = (bf16[64,896]{1,0:T(8,128)(2,1)}, bf16[64,896]{1,0:T(8,128)(2,1)S(1)}, u32[]{:S(2)}) copy-start(bf16[64,896]{1,0:T(8,128)(2,1)S(1)} %get-tuple-element.92) | copy-start | bytes 344068
  751.4 124.0 %all-gather.27.cloned.1.call-start = ((), (), s32[]{:S(2)}) async-start(), calls=%async_computation.9 | async-start | bytes 1064960 | tf_op jit(solution)/shard_map/all_gather | solution.py:173
  752.1 211.9 %all-gather.29.cloned.1.call-start = ((), (), s32[]{:S(2)}) async-start(), calls=%async_computation.10 | async-start | bytes 1064960 | tf_op jit(solution)/shard_map/all_gather | solution.py:172
  754.2 68.1 %copy-start.49 = (bf16[64,14,32]{2,0,1:T(8,128)(2,1)}, bf16[64,14,32]{2,0,1:T(8,128)(2,1)S(1)}, u32[]{:S(2)}) copy-start(bf16[64,14,32]{2,0,1:T(8,128)(2,1)S(1)} %copy.200) | copy-start | bytes 172036
  822.3 72.6 %slice-start.21 = ((s8[8716288]{0:T(1024)(128)(4,1)}), s8[327680]{0:T(1024)(128)(4,1)S(1)}, s32[]{:S(2)}) async-start(s8[8716288]{0:T(1024)(128)(4,1)} %bitcast.513), calls=%async_computation.42 | async-start | bytes 655360
  898.3 4.6 collective-permute-start.2
  904.7 124.0 %all-gather.31.cloned.1.call-start = ((), (), s32[]{:S(2)}) async-start(), calls=%async_computation.11 | async-start | bytes 1064960 | tf_op jit(solution)/shard_map/all_gather | solution.py:173
  905.4 510.0 %reduce-scatter.5.cloned.1.call-start = ((), (), s32[]{:S(2)}) async-start(), calls=%async_computation.12 | async-start | bytes 4259840 | tf_op jit(solution)/shard_map/reduce_scatter | solution.py:315
  972.0 75.5 %slice-start.24 = ((s8[8716288]{0:T(1024)(128)(4,1)}), s8[327680]{0:T(1024)(128)(4,1)S(1)}, s32[]{:S(2)}) async-start(s8[8716288]{0:T(1024)(128)(4,1)} %bitcast.515), calls=%async_computation.45 | async-start | bytes 655360
  1108.2 734.2 %reduce-scatter.7.cloned.1.call-start = ((), (), s32[]{:S(2)}) async-start(), calls=%async_computation.13 | async-start | bytes 4259840 | tf_op jit(solution)/shard_map/reduce_scatter | solution.py:315
  1115.5 301.9 %copy-start.2 = (bf16[1,896,1152]{2,1,0:T(8,128)(2,1)S(1)}, bf16[1,896,1152]{2,1,0:T(8,128)(2,1)}, u32[]{:S(2)}) copy-start(bf16[1,896,1152]{2,1,0:T(8,128)(2,1)} %copy-done.1) | copy-start | bytes 6193156
  1115.5 303.3 %copy-start.54 = (f32[64,896]{1,0:T(8,128)S(1)}, f32[64,896]{1,0:T(8,128)}, u32[]{:S(2)}) copy-start(f32[64,896]{1,0:T(8,128)} %copy-done.53) | copy-start | bytes 688132
  1121.0 358.6 %copy-start.38 = (bf16[64,14,64]{2,1,0:T(8,128)(2,1)}, bf16[64,14,64]{2,1,0:T(8,128)(2,1)S(1)}, u32[]{:S(2)}) copy-start(bf16[64,14,64]{2,1,0:T(8,128)(2,1)S(1)} %maximum_convert_fusion) | copy-start | bytes 344068
  1121.2 358.4 %copy-start.63 = (bf16[64,896]{1,0:T(8,128)(2,1)}, bf16[64,896]{1,0:T(8,128)(2,1)S(1)}, u32[]{:S(2)}) copy-start(bf16[64,896]{1,0:T(8,128)(2,1)S(1)} %reshape.1432) | copy-start | bytes 344068
  1419.6 53.2 %collective-permute-start.3 = (bf16[64,896]{1,0:T(8,128)(2,1)S(1)}, bf16[64,896]{1,0:T(8,128)(2,1)S(1)}, u32[]{:S(2)}, u32[]{:S(2)}) collective-permute-start(bf16[64,896]{1,0:T(8,128)(2,1)S(1)} %get-tuple-element.160), channel_id=1, source_target_pairs={{64,0},{65,1},{66,2},{67,3},{68,4},{69,5},{70,6},{71,7},{72,8},{73... | collective-permute-start | bytes 344072 | tf_op jit(solution)/shard_map/ppermute | solution.py:23
  1539.4 732.4 %reduce-scatter.9.cloned.1.call-start = ((), (), s32[]{:S(2)}) async-start(), calls=%async_computation.14 | async-start | bytes 4259840 | tf_op jit(solution)/shard_map/reduce_scatter | solution.py:315
  1546.0 298.4 %copy-start.31 = (bf16[64,896]{1,0:T(8,128)(2,1)S(1)}, bf16[64,896]{1,0:T(8,128)(2,1)}, u32[]{:S(2)}) copy-start(bf16[64,896]{1,0:T(8,128)(2,1)} %copy-done.30) | copy-start | bytes 344068
  1546.0 298.4 %copy-start.142 = (f32[64]{0:T(128)S(1)}, f32[64]{0:T(128)}, u32[]{:S(2)}) copy-start(f32[64]{0:T(128)} %copy-done.141) | copy-start | bytes 772
  1546.0 298.4 %copy-start.146 = (f32[64]{0:T(128)S(1)}, f32[64]{0:T(128)}, u32[]{:S(2)}) copy-start(f32[64]{0:T(128)} %copy-done.145) | copy-start | bytes 772
  1546.8 352.9 %copy-start.122 = (f32[2,7,64]{2,1,0:T(8,128)S(1)}, f32[2,7,64]{2,1,0:T(8,128)}, u32[]{:S(2)}) copy-start(f32[2,7,64]{2,1,0:T(8,128)} %copy-done.121) | copy-start | bytes 10756
  1546.8 352.9 %copy-start.126 = (f32[2,7,64]{2,1,0:T(8,128)S(1)}, f32[2,7,64]{2,1,0:T(8,128)}, u32[]{:S(2)}) copy-start(f32[2,7,64]{2,1,0:T(8,128)} %copy-done.125) | copy-start | bytes 10756
  1551.6 348.9 %copy-start.65 = (bf16[64,896]{1,0:T(8,128)(2,1)}, bf16[64,896]{1,0:T(8,128)(2,1)S(1)}, u32[]{:S(2)}) copy-start(bf16[64,896]{1,0:T(8,128)(2,1)S(1)} %reshape.1439) | copy-start | bytes 344068
  1847.5 52.9 %collective-permute-start.4 = (bf16[64,896]{1,0:T(8,128)(2,1)S(1)}, bf16[64,896]{1,0:T(8,128)(2,1)S(1)}, u32[]{:S(2)}, u32[]{:S(2)}) collective-permute-start(bf16[64,896]{1,0:T(8,128)(2,1)S(1)} %get-tuple-element.162), channel_id=1, source_target_pairs={{64,0},{65,1},{66,2},{67,3},{68,4},{69,5},{70,6},{71,7},{72,8},{73... | collective-permute-start | bytes 344072 | tf_op jit(solution)/shard_map/ppermute | solution.py:23
  1969.0 733.0 %reduce-scatter.11.cloned.1.call-start = ((), (), s32[]{:S(2)}) async-start(), calls=%async_computation.15 | async-start | bytes 4259840 | tf_op jit(solution)/shard_map/reduce_scatter | solution.py:315
  1975.6 298.2 %copy-start.29 = (bf16[64,896]{1,0:T(8,128)(2,1)S(1)}, bf16[64,896]{1,0:T(8,128)(2,1)}, u32[]{:S(2)}) copy-start(bf16[64,896]{1,0:T(8,128)(2,1)} %copy-done.28) | copy-start | bytes 344068
  1976.3 353.9 %copy-start.120 = (f32[2,7,64]{2,1,0:T(8,128)S(1)}, f32[2,7,64]{2,1,0:T(8,128)}, u32[]{:S(2)}) copy-start(f32[2,7,64]{2,1,0:T(8,128)} %copy-done.119) | copy-start | bytes 10756
  1980.9 356.7 %copy-start.41 = (bf16[64,14,64]{2,1,0:T(8,128)(2,1)}, bf16[64,14,64]{2,1,0:T(8,128)(2,1)S(1)}, u32[]{:S(2)}) copy-start(bf16[64,14,64]{2,1,0:T(8,128)(2,1)S(1)} %maximum_convert_fusion.2) | copy-start | bytes 344068
  1981.1 349.1 %copy-start.67 = (bf16[64,896]{1,0:T(8,128)(2,1)}, bf16[64,896]{1,0:T(8,128)(2,1)S(1)}, u32[]{:S(2)}) copy-start(bf16[64,896]{1,0:T(8,128)(2,1)S(1)} %reshape.1446) | copy-start | bytes 344068
  2277.7 53.2 %collective-permute-start.5 = (bf16[64,896]{1,0:T(8,128)(2,1)S(1)}, bf16[64,896]{1,0:T(8,128)(2,1)S(1)}, u32[]{:S(2)}, u32[]{:S(2)}) collective-permute-start(bf16[64,896]{1,0:T(8,128)(2,1)S(1)} %get-tuple-element.164), channel_id=1, source_target_pairs={{64,0},{65,1},{66,2},{67,3},{68,4},{69,5},{70,6},{71,7},{72,8},{73... | collective-permute-start | bytes 344072 | tf_op jit(solution)/shard_map/ppermute | solution.py:23
  2399.4 895.5 %all-reduce.4.cloned.1.call-start = ((), (), s32[]{:S(2)}) async-start(), calls=%async_computation.20 | async-start | bytes 119275520
  2448.9 255.1 %copy-start.111 = (bf16[1,64,896]{2,1,0:T(8,128)(2,1)S(1)}, bf16[1,64,896]{2,1,0:T(8,128)(2,1)}, u32[]{:S(2)}) copy-start(bf16[1,64,896]{2,1,0:T(8,128)(2,1)} %fusion.239) | copy-start | bytes 344068
  2448.9 255.1 %copy-start.112 = (bf16[1,64,896]{2,1,0:T(8,128)(2,1)S(1)}, bf16[1,64,896]{2,1,0:T(8,128)(2,1)}, u32[]{:S(2)}) copy-start(bf16[1,64,896]{2,1,0:T(8,128)(2,1)} %concatenate.306) | copy-start | bytes 344068
  2448.9 255.1 %copy-start.113 = (bf16[1,64,896]{2,1,0:T(8,128)(2,1)S(1)}, bf16[1,64,896]{2,1,0:T(8,128)(2,1)}, u32[]{:S(2)}) copy-start(bf16[1,64,896]{2,1,0:T(8,128)(2,1)} %concatenate.302) | copy-start | bytes 344068
  2448.9 255.1 %copy-start.114 = (bf16[1,64,896]{2,1,0:T(8,128)(2,1)S(1)}, bf16[1,64,896]{2,1,0:T(8,128)(2,1)}, u32[]{:S(2)}) copy-start(bf16[1,64,896]{2,1,0:T(8,128)(2,1)} %concatenate.298) | copy-start | bytes 344068
  2449.0 255.1 %copy-start.115 = (bf16[1,64,896]{2,1,0:T(8,128)(2,1)S(1)}, bf16[1,64,896]{2,1,0:T(8,128)(2,1)}, u32[]{:S(2)}) copy-start(bf16[1,64,896]{2,1,0:T(8,128)(2,1)} %concatenate.294) | copy-start | bytes 344068
  2449.0 255.0 %copy-start.117 = (bf16[1,64,896]{2,1,0:T(8,128)(2,1)S(1)}, bf16[1,64,896]{2,1,0:T(8,128)(2,1)}, u32[]{:S(2)}) copy-start(bf16[1,64,896]{2,1,0:T(8,128)(2,1)} %get-tuple-element.159) | copy-start | bytes 344068
  2449.0 255.0 %copy-start.129 = (bf16[1,64,128]{2,1,0:T(8,128)(2,1)S(1)}, bf16[1,64,128]{2,1,0:T(8,128)(2,1)}, u32[]{:S(2)}) copy-start(bf16[1,64,128]{2,1,0:T(8,128)(2,1)} %slice_bitcast_fusion) | copy-start | bytes 49156
  2449.0 255.0 %copy-start.130 = (bf16[1,64,128]{2,1,0:T(8,128)(2,1)S(1)}, bf16[1,64,128]{2,1,0:T(8,128)(2,1)}, u32[]{:S(2)}) copy-start(bf16[1,64,128]{2,1,0:T(8,128)(2,1)} %slice_bitcast_fusion.2) | copy-start | bytes 49156
  2746.8 324.6 %copy-start.58 = (f32[64,896]{1,0:T(8,128)S(1)}, f32[64,896]{1,0:T(8,128)}, u32[]{:S(2)}) copy-start(f32[64,896]{1,0:T(8,128)} %copy-done.57) | copy-start | bytes 688132
  2746.8 325.2 %copy-start.85 = (bf16[1,1,64,896]{3,2,1,0:T(8,128)(2,1)S(1)}, bf16[1,1,64,896]{3,2,1,0:T(8,128)(2,1)}, u32[]{:S(2)}) copy-start(bf16[1,1,64,896]{3,2,1,0:T(8,128)(2,1)} %get-tuple-element.139) | copy-start | bytes 344068
  2746.9 325.2 %copy-start.87 = (bf16[64,896]{1,0:T(8,128)(2,1)S(1)}, bf16[64,896]{1,0:T(8,128)(2,1)}, u32[]{:S(2)}) copy-start(bf16[64,896]{1,0:T(8,128)(2,1)} %copy-done.86) | copy-start | bytes 344068
  2758.2 313.9 %copy-start.89 = (bf16[64,896]{1,0:T(8,128)(2,1)S(1)}, bf16[64,896]{1,0:T(8,128)(2,1)}, u32[]{:S(2)}) copy-start(bf16[64,896]{1,0:T(8,128)(2,1)} %copy-done.88) | copy-start | bytes 344068
  (135 other events, 2023.6 us)
Sparse Core Ops, SparseCore 0:
  11.4 71.0 all-gather.32
  85.9 64.8 all-gather.34
  153.7 60.5 all-gather.16
  217.6 61.4 all-gather.18
  282.3 105.5 all-gather.38
  391.1 165.0 all-gather.36
  592.6 61.2 all-gather.20
  657.4 61.4 all-gather.22
  751.5 59.1 all-gather.24
  814.0 61.4 all-gather.26
  904.8 59.1 all-gather.28
  967.3 61.4 all-gather.30
  1108.3 307.1 reduce-scatter.4
  1539.5 302.7 reduce-scatter.6
  1969.1 302.6 reduce-scatter.8
  2399.5 302.4 reduce-scatter.10
  2747.0 547.8 all-reduce.3
where the time goes:
time: 3320 us; the launch traced here: 3310 us
  waiting for transfers between devices  2130 us (64%)
  matrix products  362 us (11%)
  blocking collectives  297 us (9%)
  other arithmetic  178 us (5%)
  starting transfers between devices  162 us (5%)
  local copies, waits for them, and re-layouts  161 us (5%)
    reduce_scatter x4, waiting for transfers between devices, shards(): lax.psum_scatter(key_terms, 'dp', scatter_dimension=0, tiled=True)  1110 us
    psum x1, blocking collectives, shards(): lax.psum((squares_pick, gain_sum, bias_sum), 'dp')  297 us
    all_gather x4, waiting for transfers between devices, shards(): lax.all_gather(forward_key_local, 'dp', axis=0, tiled=True)  225 us
    unnamed x18, waiting for transfers between devices  221 us
    all_gather x4, waiting for transfers between devices, shards(): lax.all_gather(forward_value_local, 'dp', axis=0, tiled=True)  204 us
    ppermute x6, starting transfers between devices, passed_along(): return lax.ppermute(block, axis, route)  161 us
    all_gather x1, waiting for transfers between devices, shards(): lax.all_gather(local_weights[2], 'dp', axis=0, tiled=True)  157 us
    dot_general x16, matrix products, contract_last(): lax.dot_general(left, right, (((1,), (1,)), ((), ())), preferred_element_...  84.2 us
  transfers between devices with their start and end apart: 23, of which 22 were waited for; matrix products, arithmetic and copies ran while one was open for 8% of the time, Pallas kernels for 0%

commit v1 on v0

v1 whole, which is shorter than its diff:
```python
import functools
import math

import jax
import jax.numpy as jnp
from jax import lax
from jax.experimental import pallas as pl
from jax.experimental.pallas import tpu as pltpu
from jax.sharding import PartitionSpec as P

MESH = pl.DeviceIdType.MESH
EPS = 1e-06
THETA = 1000000.0
MASKED = -1e30

MB = 3
T = 64
R = MB * T
D = 896
DP = 1024
FFH = 2432
QS = 512
C_UP, C_DOWN, C_QK, C_VO, C = FFH, 2 * FFH, 3 * FFH, 3 * FFH + QS, 3 * FFH + 2 * QS
KB = 512
SEQ = 4096
MIB = 1024 * 1024

THIRDS = ((0, 22 * 128), (22 * 128, 22 * 128), (44 * 128, 21 * 128))
ORDERS = (("z", "y", "x"), ("y", "x", "z"), ("x", "z", "y"))
FF_CHUNKS = ((0, 512), (512, 512), (1024, 512), (1536, 512), (2048, 384))


def position():
    chip = lax.axis_index("dp")
    return {"x": chip // 16, "y": (chip // 4) % 4, "z": chip % 4}


def moved(place, axis, distance):
    other = dict(place)
    other[axis] = (place[axis] + distance + 4) % 4
    return other


def chip_id(place):
    return {"dp": place["x"] * 16 + place["y"] * 4 + place["z"]}


def other_core():
    return {"section": 1 - lax.axis_index("section")}


def meet(place, core=False, chips=True, far=False):
    barrier = pltpu.get_barrier_semaphore()
    count = 0
    if chips:
        for axis in "xyz":
            for distance in (1, -1, 2) if far else (1, -1):
                pl.semaphore_signal(
                    barrier,
                    inc=1,
                    device_id=chip_id(moved(place, axis, distance)),
                    device_id_type=MESH,
                )
                count += 1
    if core:
        pl.semaphore_signal(barrier, inc=1, device_id=other_core(), device_id_type=MESH)
        count += 1
    pl.semaphore_wait(barrier, count)


def send(src, dst, send_sem, recv_sem, device):
    return pltpu.make_async_remote_copy(
        src, dst, send_sem, recv_sem, device_id=device, device_id_type=MESH
    )


def cube(done, place):
    return tuple(slice(None) if axis in done else place[axis] for axis in "xyz")


def gather_stages(view, place, send_sems, recv_sems):
    pending = []

    def copy(j, phase, k, whose, part, distance):
        ref = view(cube(ORDERS[j][:phase], whose), j, part)
        return send(
            ref,
            ref,
            send_sems.at[j, phase, k],
            recv_sems.at[j, phase, k],
            chip_id(moved(place, ORDERS[j][phase], distance)),
        )

    def first(phase):
        for j in range(3):
            for k, distance in ((0, 1), (1, -1)):
                one = copy(j, phase, k, place, None, distance)
                one.start()
                pending.append(one)

    def second(phase):
        for j in range(3):
            for k, distance in ((0, 1), (1, -1)):
                whose = moved(place, ORDERS[j][phase], -distance)
                copy(j, phase, k, whose, None, distance).wait_recv()
                one = copy(j, phase, 2 + k, whose, k, distance)
                one.start()
                pending.append(one)

    def third(phase):
        for j in range(3):
            for k, distance in ((0, 1), (1, -1)):
                whose = moved(place, ORDERS[j][phase], 2)
                copy(j, phase, 2 + k, whose, k, distance).wait_recv()

    def finish():
        for one in pending:
            one.wait_send()

    stages = []
    for phase in range(3):
        stages.append(functools.partial(first, phase))
        stages.append(functools.partial(second, phase))
        stages.append(functools.partial(third, phase))
    stages.append(finish)
    return stages


def scatter_stages(view, halves, wholes, place, send_sems, recv_sems, width, final):
    pending = []

    def chips_of(j, phase, whose):
        order = ORDERS[j][::-1]
        return cube(order[phase + 1 :], whose)

    def axis_of(j, phase):
        return ORDERS[j][::-1][phase]

    def add(dst, *terms):
        dst[...] = sum(term[...].astype(jnp.float32) for term in terms).astype(dst.dtype)

    def half_copy(j, phase, k, distance):
        src = view(chips_of(j, phase, moved(place, axis_of(j, phase), 2)), j, k)
        return send(
            src,
            halves[phase](j, k),
            send_sems.at[j, phase, k],
            recv_sems.at[j, phase, k],
            chip_id(moved(place, axis_of(j, phase), distance)),
        )

    def whole_copy(j, phase, k, distance):
        src = view(chips_of(j, phase, moved(place, axis_of(j, phase), distance)), j, None)
        return send(
            src,
            wholes[phase](j, k, None),
            send_sems.at[j, phase, 2 + k],
            recv_sems.at[j, phase, 2 + k],
            chip_id(moved(place, axis_of(j, phase), distance)),
        )

    def first(phase):
        for j in range(3):
            for k, distance in ((0, 1), (1, -1)):
                one = half_copy(j, phase, k, distance)
                one.start()
                pending.append(one)

    def second(phase):
        for j in range(3):
            for k, distance in ((0, 1), (1, -1)):
                half_copy(j, phase, k, distance).wait_recv()
                mine = view(chips_of(j, phase, moved(place, axis_of(j, phase), distance)), j, k)
                add(mine, mine, halves[phase](j, k))
                one = whole_copy(j, phase, k, distance)
                one.start()
                pending.append(one)

    def third(phase):
        for j in range(3):
            for k, distance in ((0, 1), (1, -1)):
                whole_copy(j, phase, k, distance).wait_recv()
            mine = view(chips_of(j, phase, place), j, None)
            if phase < 2:
                add(mine, mine, wholes[phase](j, 0, None), wholes[phase](j, 1, None))
            else:
                final(j, mine, wholes[phase](j, 0, None), wholes[phase](j, 1, None))

    def finish():
        for one in pending:
            one.wait_send()

    stages = []
    for phase in range(3):
        stages.append(functools.partial(first, phase))
        stages.append(functools.partial(second, phase))
        stages.append(functools.partial(third, phase))
    stages.append(finish)
    return stages


def weight_view(ref):
    def view(chips, j, part):
        start, size = THIRDS[j]
        if part is not None:
            half = size // 256 * 128
            start, size = (start, half) if part == 0 else (start + half, size - half)
        return ref.at[tuple(chips) + (slice(None), pl.ds(start, size))]

    return view


def token_view(ref):
    def view(chips, j, part):
        rows = slice(None) if part is None else pl.ds(part * 32, 32)
        return ref.at[tuple(chips) + (j, rows, slice(None))]

    return view


def params(collective_id=None, vmem=56):
    if collective_id is None:
        return pltpu.CompilerParams(vmem_limit_bytes=vmem * MIB)
    return pltpu.CompilerParams(
        collective_id=collective_id, has_side_effects=True, vmem_limit_bytes=vmem * MIB
    )


ANY = pl.BlockSpec(memory_space=pl.ANY)
VMEM = pl.BlockSpec(memory_space=pltpu.VMEM)
SMEM = pl.BlockSpec(memory_space=pltpu.SMEM)
DMA = pltpu.SemaphoreType.DMA


def shape(dims, dtype):
    return jax.ShapeDtypeStruct(dims, dtype)


def nn(left, right):
    return jnp.dot(left, right, preferred_element_type=jnp.float32)


def nt(left, right):
    return lax.dot_general(
        left, right, (((1,), (1,)), ((), ())), preferred_element_type=jnp.float32
    )


def tn(left, right):
    return lax.dot_general(
        left, right, (((0,), (0,)), ((), ())), preferred_element_type=jnp.float32
    )


def gather_weights_kernel(mine, theirs, ends, small, w, ends_all, small_all, lsem, xs, xr, ss, rs):
    place = position()
    core = lax.axis_index("section")
    meet(place, core=True)
    here = (place["x"], place["y"], place["z"])
    own = w.at[(core,) + here]
    locals_ = [
        pltpu.make_async_copy(mine, own, lsem.at[0]),
        pltpu.make_async_copy(ends, ends_all.at[core], lsem.at[1]),
        pltpu.make_async_copy(small, small_all.at[core], lsem.at[2]),
    ]
    swaps = [
        send(theirs, own, xs.at[0], xr.at[0], other_core()),
        send(ends, ends_all.at[core], xs.at[1], xr.at[1], other_core()),
        send(small, small_all.at[core], xs.at[2], xr.at[2], other_core()),
    ]
    arrivals = [
        send(theirs, w.at[(1 - core,) + here], xs.at[0], xr.at[0], other_core()),
        send(ends, ends_all.at[1 - core], xs.at[1], xr.at[1], other_core()),
        send(small, small_all.at[1 - core], xs.at[2], xr.at[2], other_core()),
    ]
    for one in locals_ + swaps:
        one.start()
    for one in locals_:
        one.wait()
    for one in arrivals:
        one.wait_recv()
    stages = [
        gather_stages(weight_view(w.at[layer]), place, ss.at[layer], rs.at[layer])
        for layer in range(2)
    ]
    for step in zip(*stages):
        for stage in step:
            stage()
    for one in swaps:
        one.wait_send()


def gather_weights(mine, theirs, ends, small):
    return pl.pallas_call(
        gather_weights_kernel,
        out_shape=(
            shape((2, 4, 4, 4, 16, C), jnp.bfloat16),
            shape((2,) + ends.shape, ends.dtype),
            shape((2,) + small.shape, small.dtype),
        ),
        in_specs=[ANY] * 4,
        out_specs=(ANY,) * 3,
        scratch_shapes=[DMA((3,)), DMA((3,)), DMA((3,)), DMA((2, 3, 3, 4)), DMA((2, 3, 3, 4))],
        compiler_params=params(0),
        name="gather_weights",
    )(mine, theirs, ends, small)


def gather_tokens_kernel(own, everything, lsem, ss, rs):
    place = position()
    meet(place)
    local = pltpu.make_async_copy(
        own, everything.at[place["x"], place["y"], place["z"]], lsem
    )
    local.start()
    local.wait()
    for stage in gather_stages(token_view(everything), place, ss, rs):
        stage()


def gather_tokens(own):
    return pl.pallas_call(
        gather_tokens_kernel,
        out_shape=shape((4, 4, 4) + own.shape, own.dtype),
        in_specs=[ANY],
        out_specs=ANY,
        scratch_shapes=[DMA, DMA((3, 3, 4)), DMA((3, 3, 4))],
        compiler_params=params(1),
        name="gather_keys_values",
    )(own)


def scatter_tokens_kernel(terms, out, buf, h0, h1, h2, w0, w1, w2, lsem, ss, rs):
    place = position()
    meet(place)
    load = pltpu.make_async_copy(terms, buf, lsem)
    load.start()
    load.wait()
    halves = [lambda j, k, ref=ref: ref.at[j, k] for ref in (h0, h1, h2)]
    wholes = [lambda j, k, part, ref=ref: ref.at[j, k] for ref in (w0, w1, w2)]

    def final(j, mine, left, right):
        out[j] = (
            mine[...].astype(jnp.float32)
            + left[...].astype(jnp.float32)
            + right[...].astype(jnp.float32)
        )

    for stage in scatter_stages(
        token_view(buf), halves, wholes, place, ss, rs, None, final
    ):
        stage()


def scatter_tokens(terms):
    kv = jnp.bfloat16
    return pl.pallas_call(
        scatter_tokens_kernel,
        out_shape=shape((MB, T, 128), jnp.float32),
        in_specs=[ANY],
        out_specs=VMEM,
        scratch_shapes=[
            pltpu.VMEM((4, 4, 4, MB, T, 128), kv),
            pltpu.VMEM((3, 2, 4, 4, T // 2, 128), kv),
            pltpu.VMEM((3, 2, 4, T // 2, 128), kv),
            pltpu.VMEM((3, 2, T // 2, 128), kv),
            pltpu.VMEM((3, 2, 4, 4, T, 128), kv),
            pltpu.VMEM((3, 2, 4, T, 128), kv),
            pltpu.VMEM((3, 2, T, 128), kv),
            DMA,
            DMA((3, 3, 4)),
            DMA((3, 3, 4)),
        ],
        compiler_params=params(2),
        name="scatter_key_value_grads",
    )(terms)


def pair_mask(base, bounds):
    keys = base + lax.broadcasted_iota(jnp.int32, (KB, 128), 0)
    start, end, own = bounds[0:1, :], bounds[1:2, :], bounds[2:3, :]
    allowed = ((keys >= start) & (keys < end)) | (keys == own)
    bias = jnp.where(allowed, 0.0, MASKED)
    return jnp.concatenate([bias] * 4, axis=1)


def attend_kernel(blocks, qt, kv, bounds, out, lse):
    batch = pl.program_id(0)
    queries = qt[0]

    def step(index, carry):
        top, total, mixed = carry
        rows = kv[pl.ds(index * (KB // T), KB // T), 0].reshape(KB, 128)
        scores = nn(rows, queries) + pair_mask(index * KB, bounds[0])
        new_top = jnp.maximum(top, jnp.max(scores, axis=0, keepdims=True))
        shrink = jnp.exp(top - new_top)
        probs = jnp.exp(scores - new_top)
        total = total * shrink + jnp.sum(probs, axis=0, keepdims=True)
        mixed = mixed * shrink + tn(rows, probs.astype(jnp.bfloat16))
        return new_top, total, mixed

    top, total, mixed = lax.fori_loop(
        blocks[batch, 0],
        blocks[batch, 1],
        step,
        (
            jnp.full((1, QS), MASKED, jnp.float32),
            jnp.zeros((1, QS), jnp.float32),
            jnp.zeros((128, QS), jnp.float32),
        ),
    )
    out[0] = (mixed / total)[64:, :]
    lse[0] = jnp.broadcast_to(top + jnp.log(total), (8, QS))


def attend(blocks, qt, kv, bounds):
    return pl.pallas_call(
        attend_kernel,
        grid=(MB,),
        out_shape=(shape((MB, 64, QS), jnp.float32), shape((MB, 8, QS), jnp.float32)),
        in_specs=[
            SMEM,
            pl.BlockSpec((1, 128, QS), lambda m: (m, 0, 0)),
            pl.BlockSpec((64, 1, T, 128), lambda m: (0, m, 0, 0)),
            pl.BlockSpec((1, 8, 128), lambda m: (m, 0, 0)),
        ],
        out_specs=(
            pl.BlockSpec((1, 64, QS), lambda m: (m, 0, 0)),
            pl.BlockSpec((1, 8, QS), lambda m: (m, 0, 0)),
        ),
        compiler_params=params(),
        name="attention",
    )(blocks, qt, kv, bounds)


def attend_back_kernel(blocks, qt, dot_, kv, bounds, out, lse, dqt, dkv):
    batch = pl.program_id(0)
    queries, grads = qt[0], dot_[0]
    log_total = lse[0, 0:1, :]
    inner = jnp.sum(out[0] * grads[64:, :].astype(jnp.float32), axis=0, keepdims=True)
    dkv[...] = jnp.zeros_like(dkv)

    def step(index, total):
        chips = pl.ds(index * (KB // T), KB // T)
        rows = kv[chips, 0].reshape(KB, 128)
        scores = nn(rows, queries) + pair_mask(index * KB, bounds[0])
        probs = jnp.exp(scores - log_total)
        slopes = (probs * (nn(rows, grads) - inner)).astype(jnp.bfloat16)
        both = nt(slopes, queries) + nt(probs.astype(jnp.bfloat16), grads)
        dkv[chips, 0] = both.astype(jnp.bfloat16).reshape(KB // T, T, 128)
        return total + tn(rows, slopes)

    total = lax.fori_loop(
        blocks[batch, 0], blocks[batch, 1], step, jnp.zeros((128, QS), jnp.float32)
    )
    dqt[0] = total[:64, :] * (1.0 / 8.0)


def attend_back(blocks, qt, dot_, kv, bounds, out, lse):
    return pl.pallas_call(
        attend_back_kernel,
        grid=(MB,),
        out_shape=(
            shape((MB, 64, QS), jnp.float32),
            shape((64, MB, T, 128), jnp.bfloat16),
        ),
        in_specs=[
            SMEM,
            pl.BlockSpec((1, 128, QS), lambda m: (m, 0, 0)),
            pl.BlockSpec((1, 128, QS), lambda m: (m, 0, 0)),
            pl.BlockSpec((64, 1, T, 128), lambda m: (0, m, 0, 0)),
            pl.BlockSpec((1, 8, 128), lambda m: (m, 0, 0)),
            pl.BlockSpec((1, 64, QS), lambda m: (m, 0, 0)),
            pl.BlockSpec((1, 8, QS), lambda m: (m, 0, 0)),
        ],
        out_specs=(
            pl.BlockSpec((1, 64, QS), lambda m: (m, 0, 0)),
            pl.BlockSpec((64, 1, T, 128), lambda m: (0, m, 0, 0)),
        ),
        compiler_params=params(),
        name="attention_back",
    )(blocks, qt, dot_, kv, bounds, out, lse)


def mean_of(values):
    return jnp.sum(values, axis=-1, keepdims=True) * (1.0 / D)


def turn(values, cosine, sine):
    lane = lax.broadcasted_iota(jnp.int32, values.shape, 1) % 64
    swapped = jnp.where(lane < 32, pltpu.roll(values, QS - 32, 1), pltpu.roll(values, 32, 1))
    return values * cosine + swapped * sine


def tiled(table):
    wide = jnp.concatenate([table] * 4, axis=1)
    return jnp.concatenate([wide] * MB, axis=0)


def project_kernel(layer, x, gains, bias, cosine, sine, w, n1, qk, v, wbuf, sem):
    load = pltpu.make_async_copy(w.at[layer, :, :, pl.ds(C_QK, 2 * QS)], wbuf, sem)
    load.start()
    rows = x[...].astype(jnp.float32)
    normed = (rows * lax.rsqrt(mean_of(rows * rows) + EPS) * gains[0:1, :]).astype(jnp.bfloat16)
    n1[...] = normed
    load.wait()
    weights = wbuf[...].reshape(DP, 2 * QS)
    projected = nn(normed, weights[:, : QS + 128]) + bias[0:1, : QS + 128]
    turned = turn(projected[:, :QS], tiled(cosine[...]), tiled(sine[...]))
    qk[...] = turned.astype(jnp.bfloat16)
    v[...] = projected[:, QS:].astype(jnp.bfloat16)


def project(layer, x, gains, bias, cosine, sine, w):
    return pl.pallas_call(
        functools.partial(project_kernel, layer),
        out_shape=(
            shape((R, DP), jnp.bfloat16),
            shape((R, QS), jnp.bfloat16),
            shape((R, 128), jnp.bfloat16),
        ),
        in_specs=[VMEM] * 5 + [ANY],
        out_specs=(VMEM,) * 3,
        scratch_shapes=[pltpu.VMEM((64, 16, 2 * QS), jnp.bfloat16), DMA],
        compiler_params=params(),
        name="project",
    )(x, gains, bias, cosine, sine, w)


def mlp_kernel(
    layer, x, attended, gains, w, xo, mid, n2, gu, hid, sq, wbuf, mine, theirs, wsem, xs, xr
):
    meet(position(), core=True, chips=False)

    def load(index, start, size):
        cols = pl.ds(start, size)
        return pltpu.make_async_copy(
            w.at[layer, :, :, cols], wbuf.at[:, :, cols], wsem.at[index]
        )

    loads = [load(0, C_VO, QS)]
    for index, (start, size) in enumerate(FF_CHUNKS):
        for part in range(3):
            loads.append(load(1 + 3 * index + part, part * FFH + start, size))
    for one in loads:
        one.start()

    def weights(start, size):
        return wbuf[:, :, pl.ds(start, size)].reshape(DP, size)

    def swap(slot):
        return send(
            mine.at[slot], theirs.at[slot], xs.at[slot], xr.at[slot], other_core()
        )

    loads[0].wait()
    mine[0] = nt(attended[...], weights(C_VO, QS))
    one = swap(0)
    one.start()
    one.wait()
    branch = mine[0] + theirs[0]
    rows = x[...].astype(jnp.float32)
    middle = rows + branch
    mid[...] = middle
    normed = (middle * lax.rsqrt(mean_of(middle * middle) + EPS) * gains[1:2, :]).astype(
        jnp.bfloat16
    )
    n2[...] = normed
    total = jnp.zeros((R, DP), jnp.float32)
    for index, (start, size) in enumerate(FF_CHUNKS):
        for part in range(3):
            loads[1 + 3 * index + part].wait()
        gate = nn(normed, weights(start, size))
        up = nn(normed, weights(C_UP + start, size))
        gu[:, pl.ds(start, size)] = gate
        gu[:, pl.ds(C_UP + start, size)] = up
        hidden = (gate * jax.nn.sigmoid(gate) * up).astype(jnp.bfloat16)
        hid[:, pl.ds(start, size)] = hidden
        total = total + nt(hidden, weights(C_DOWN + start, size))
    mine[1] = total
    two = swap(1)
    two.start()
    two.wait()
    out = mine[1] + theirs[1]
    xo[...] = (middle + out).astype(jnp.bfloat16)
    row = lax.broadcasted_iota(jnp.int32, (8, 128), 0)
    lane = lax.broadcasted_iota(jnp.int32, (8, 128), 1)
    sums = jnp.zeros((8, 128), jnp.float32)
    for kind, values in enumerate((rows, branch, out)):
        squares = jnp.sum(values * values, axis=1, keepdims=True)
        for batch in range(MB):
            one = jnp.sum(squares[batch * T : (batch + 1) * T], axis=0, keepdims=True)
            sums = jnp.where((row == batch) & (lane == kind), one, sums)
    sq[...] = sums


def mlp(layer, x, attended, gains, w):
    return pl.pallas_call(
        functools.partial(mlp_kernel, layer),
        out_shape=(
            shape((R, DP), jnp.bfloat16),
            shape((R, DP), jnp.float32),
            shape((R, DP), jnp.bfloat16),
            shape((R, 2 * FFH), jnp.float32),
            shape((R, FFH), jnp.bfloat16),
            shape((8, 128), jnp.float32),
        ),
        in_specs=[VMEM] * 3 + [ANY],
        out_specs=(VMEM,) * 6,
        scratch_shapes=[
            pltpu.VMEM((64, 16, C), jnp.bfloat16),
            pltpu.VMEM((2, R, DP), jnp.float32),
            pltpu.VMEM((2, R, DP), jnp.float32),
            DMA((16,)),
            DMA((2,)),
            DMA((2,)),
        ],
        compiler_params=params(3 + layer),
        name="mlp",
    )(x, attended, gains, w)


def norm_back(grad, rows, gain):
    scale = lax.rsqrt(mean_of(rows * rows) + EPS)
    scaled = grad * gain
    back = scale * scaled - rows * (scale * scale * scale) * mean_of(scaled * rows)
    return back, jnp.sum(grad * rows * scale, axis=0, keepdims=True)


def mlp_back_kernel(
    layer, dout, gu, mid, gains, w, dgu, dmid, da, datt, gain, wbuf, mine, theirs, wsem, xs, xr
):
    meet(position(), core=True, chips=False)

    def load(index, start, size):
        cols = pl.ds(start, size)
        return pltpu.make_async_copy(
            w.at[layer, :, :, cols], wbuf.at[:, :, cols], wsem.at[index]
        )

    loads = []
    for index, (start, size) in enumerate(FF_CHUNKS):
        for part in (2, 0, 1):
            loads.append(load(len(loads), part * FFH + start, size))
    loads.append(load(15, C_VO, QS))
    for one in loads:
        one.start()

    def weights(start, size):
        return wbuf[:, :, pl.ds(start, size)].reshape(DP, size)

    grad_in = dout[...].astype(jnp.float32)
    grad_low = grad_in.astype(jnp.bfloat16)
    total = jnp.zeros((R, DP), jnp.float32)
    for index, (start, size) in enumerate(FF_CHUNKS):
        for part in range(3):
            loads[3 * index + part].wait()
        grad_hidden = nn(grad_low, weights(C_DOWN + start, size))
        gate = gu[:, pl.ds(start, size)]
        up = gu[:, pl.ds(C_UP + start, size)]
        sigma = jax.nn.sigmoid(gate)
        grad_gate = grad_hidden * up * sigma * (1.0 + gate * (1.0 - sigma))
        grad_gate = grad_gate.astype(jnp.bfloat16)
        grad_up = (grad_hidden * gate * sigma).astype(jnp.bfloat16)
        dgu[:, pl.ds(start, size)] = grad_gate
        dgu[:, pl.ds(C_UP + start, size)] = grad_up
        total = total + nt(grad_gate, weights(start, size))
        total = total + nt(grad_up, weights(C_UP + start, size))
    mine[...] = total
    one = send(mine, theirs, xs, xr, other_core())
    one.start()
    one.wait()
    back, gain_row = norm_back(mine[...] + theirs[...], mid[...], gains[1:2, :])
    gain[...] = jnp.broadcast_to(gain_row, (8, DP))
    middle = grad_in + back
    dmid[...] = middle
    low = middle.astype(jnp.bfloat16)
    da[...] = low
    loads[15].wait()
    lane = lax.broadcasted_iota(jnp.int32, (R, QS), 1)
    datt[...] = jnp.where(lane < 64, 0.0, nn(low, weights(C_VO, QS))).astype(jnp.bfloat16)


def mlp_back(layer, dout, gu, mid, gains, w):
    return pl.pallas_call(
        functools.partial(mlp_back_kernel, layer),
        out_shape=(
            shape((R, 2 * FFH), jnp.bfloat16),
            shape((R, DP), jnp.float32),
            shape((R, DP), jnp.bfloat16),
            shape((R, QS), jnp.bfloat16),
            shape((8, DP), jnp.float32),
        ),
        in_specs=[VMEM] * 4 + [ANY],
        out_specs=(VMEM,) * 5,
        scratch_shapes=[
            pltpu.VMEM((64, 16, C), jnp.bfloat16),
            pltpu.VMEM((R, DP), jnp.float32),
            pltpu.VMEM((R, DP), jnp.float32),
            DMA((16,)),
            DMA,
            DMA,
        ],
        compiler_params=params(5 + layer),
        name="mlp_back",
    )(dout, gu, mid, gains, w)


def project_back_kernel(
    layer, dqk, dv, x, dmid, gains, cosine, sine, w, dx, low, vlow, gain, bias,
    wbuf, mine, theirs, wsem, xs, xr,
):
    load = pltpu.make_async_copy(w.at[layer, :, :, pl.ds(C_QK, 2 * QS)], wbuf, wsem)
    load.start()
    meet(position(), core=True, chips=False)
    turned = turn(dqk[...], tiled(cosine[...]), -tiled(sine[...])).astype(jnp.bfloat16)
    low[...] = turned
    values = dv[...].astype(jnp.bfloat16)
    vlow[...] = values
    bias[:, :QS] = jnp.broadcast_to(
        jnp.sum(turned.astype(jnp.float32), axis=0, keepdims=True), (8, QS)
    )
    bias[:, QS:] = jnp.broadcast_to(
        jnp.sum(values.astype(jnp.float32), axis=0, keepdims=True), (8, QS)
    )
    load.wait()
    mine[...] = nt(turned, wbuf[:, :, :QS].reshape(DP, QS)) + nt(
        values, wbuf[:, :, QS:].reshape(DP, QS)
    )
    one = send(mine, theirs, xs, xr, other_core())
    one.start()
    one.wait()
    back, gain_row = norm_back(
        mine[...] + theirs[...], x[...].astype(jnp.float32), gains[0:1, :]
    )
    gain[...] = jnp.broadcast_to(gain_row, (8, DP))
    dx[...] = (dmid[...] + back).astype(jnp.bfloat16)


def project_back(layer, dqk, dv, x, dmid, gains, cosine, sine, w):
    return pl.pallas_call(
        functools.partial(project_back_kernel, layer),
        out_shape=(
            shape((R, DP), jnp.bfloat16),
            shape((R, QS), jnp.bfloat16),
            shape((R, QS), jnp.bfloat16),
            shape((8, DP), jnp.float32),
            shape((8, 2 * QS), jnp.float32),
        ),
        in_specs=[VMEM] * 7 + [ANY],
        out_specs=(VMEM,) * 5,
        scratch_shapes=[
            pltpu.VMEM((64, 16, 2 * QS), jnp.bfloat16),
            pltpu.VMEM((R, DP), jnp.float32),
            pltpu.VMEM((R, DP), jnp.float32),
            DMA,
            DMA,
            DMA,
        ],
        compiler_params=params(7 + layer),
        name="project_back",
    )(dqk, dv, x, dmid, gains, cosine, sine, w)


def weight_grads_kernel(
    sums, n2, dgu, dm, hid, n1, dqk, dv, da, att, small, out, small_out,
    g, h0, h1, h2, w0, w1, w2, sbuf, ss, rs, as_, ar,
):
    place = position()
    meet(place, far=sums)

    def product(start, size, pairs):
        for first in range(0, size, 512):
            wide = min(512, size - first)
            total = sum(
                tn(left[...], right[:, first : first + wide]) for left, right in pairs
            )
            g[:, :, :, :, pl.ds(start + first, wide)] = total.astype(jnp.bfloat16).reshape(
                4, 4, 4, 16, wide
            )

    product(0, 2 * FFH, [(n2, dgu)])
    product(C_DOWN, FFH, [(dm, hid)])
    product(C_QK, QS, [(n1, dqk)])
    product(C_VO, QS, [(n1, dv), (da, att)])

    def spot(j, part):
        size = THIRDS[j][1]
        if part is None:
            return pl.ds(0, size)
        half = size // 256 * 128
        return pl.ds(0, half) if part == 0 else pl.ds(0, size - half)

    halves = [
        lambda j, k, ref=ref: ref.at[(j, k) + (slice(None),) * (ref.ndim - 3) + (spot(j, k),)]
        for ref in (h0, h1, h2)
    ]
    wholes = [
        lambda j, k, part, ref=ref: ref.at[
            (j, k) + (slice(None),) * (ref.ndim - 3) + (spot(j, None),)
        ]
        for ref in (w0, w1, w2)
    ]

    def final(j, mine, left, right):
        out[:, pl.ds(*THIRDS[j])] = (
            mine[...].astype(jnp.float32)
            + left[...].astype(jnp.float32)
            + right[...].astype(jnp.float32)
        )

    stages = scatter_stages(weight_view(g), halves, wholes, place, ss, rs, None, final)
    if sums:
        sbuf[0] = small[...]
        for phase, axis in enumerate("xyz"):
            copies = [
                send(
                    sbuf.at[4 * phase],
                    sbuf.at[4 * phase + k],
                    as_.at[phase, k - 1],
                    ar.at[phase, k - 1],
                    chip_id(moved(place, axis, distance)),
                )
                for k, distance in ((1, 1), (2, -1), (3, 2))
            ]
            for one in copies:
                one.start()
            stages[phase]()
            for one in copies:
                one.wait()
            total = (
                sbuf[4 * phase] + sbuf[4 * phase + 1] + sbuf[4 * phase + 2] + sbuf[4 * phase + 3]
            )
            if phase < 2:
                sbuf[4 * phase + 4] = total
            else:
                small_out[...] = total
        stages = stages[3:]
    else:
        small_out[...] = small[...]
    for stage in stages:
        stage()


def weight_grads(sums, n2, dgu, dm, hid, n1, dqk, dv, da, att, small):
    kind = jnp.bfloat16
    wide = THIRDS[0][1]
    half = THIRDS[0][1] // 2
    return pl.pallas_call(
        functools.partial(weight_grads_kernel, sums),
        out_shape=(shape((16, C), jnp.float32), shape((8, DP), jnp.float32)),
        in_specs=[VMEM] * 10,
        out_specs=(VMEM, VMEM),
        scratch_shapes=[
            pltpu.VMEM((4, 4, 4, 16, C), kind),
            pltpu.VMEM((3, 2, 4, 4, 16, half), kind),
            pltpu.VMEM((3, 2, 4, 16, half), kind),
            pltpu.VMEM((3, 2, 16, half), kind),
            pltpu.VMEM((3, 2, 4, 4, 16, wide), kind),
            pltpu.VMEM((3, 2, 4, 16, wide), kind),
            pltpu.VMEM((3, 2, 16, wide), kind),
            pltpu.VMEM((12, 8, DP), jnp.float32),
            DMA((3, 3, 4)),
            DMA((3, 3, 4)),
            DMA((3, 3)),
            DMA((3, 3)),
        ],
        compiler_params=params(9 + int(sums), vmem=60),
        name="weight_grads",
    )(n2, dgu, dm, hid, n1, dqk, dv, da, att, small)


def shards(
    ends,
    segment_ids,
    valid_blocks,
    qkv_weight,
    qkv_bias,
    out_weight,
    gate_up_weight,
    down_weight,
    norm_gains,
):
    core = lax.axis_index("section")
    chip = lax.axis_index("dp")
    ff = 2 * FFH

    feature = jnp.arange(D, dtype=jnp.int32)
    spread = (
        (feature // 14 * 16 + feature % 14)[:, None] == jnp.arange(DP, dtype=jnp.int32)[None, :]
    ).astype(jnp.bfloat16)

    def widen(rows):
        return nn(rows, spread).astype(jnp.bfloat16)

    def half_of(index):
        pieces = (
            lax.dynamic_slice_in_dim(gate_up_weight[0], index * FFH, FFH, 1),
            lax.dynamic_slice_in_dim(gate_up_weight[0], ff + index * FFH, FFH, 1),
            lax.dynamic_slice_in_dim(down_weight[0], index * FFH, FFH, 1),
            lax.dynamic_slice_in_dim(qkv_weight[0], D + index * 64, 64, 1),
            lax.dynamic_slice_in_dim(qkv_weight[0], index * 448, 448, 1),
            lax.dynamic_slice_in_dim(qkv_weight[0], D + 128 + index * 64, 64, 1),
            lax.dynamic_slice_in_dim(out_weight[0], index * 448, 448, 1),
        )
        return jnp.pad(jnp.concatenate(pieces, axis=1), ((0, 2), (0, 0)))

    small_in = jnp.concatenate(
        [qkv_bias[0], widen(norm_gains[0]).reshape(-1)], axis=0
    )
    small_in = jnp.broadcast_to(small_in[None], (16, small_in.shape[0]))
    small_in = jnp.pad(small_in, ((0, 0), (0, 3328 - small_in.shape[1])))
    w6, ends_all, small_all = gather_weights(
        half_of(core), half_of(1 - core), widen(ends[0].reshape(R, D)), small_in
    )
    w = w6.reshape(2, 64, 16, C)

    def bias_of(layer):
        row = small_all[layer, 0, :1152].astype(jnp.float32)
        pieces = (
            lax.dynamic_slice_in_dim(row, D + core * 64, 64),
            lax.dynamic_slice_in_dim(row, core * 448, 448),
            lax.dynamic_slice_in_dim(row, D + 128 + core * 64, 64),
            jnp.zeros((448,), jnp.float32),
        )
        return jnp.broadcast_to(jnp.concatenate(pieces)[None], (8, 2 * QS))

    def gains_of(layer):
        both = small_all[layer, 0, 1152:3200].astype(jnp.float32).reshape(2, DP)
        return jnp.pad(both, ((0, 6), (0, 0)))

    places = chip * T + jnp.arange(T, dtype=jnp.int32)
    frequency = THETA ** (-jnp.arange(32, dtype=jnp.float32) * 2.0 / 64)
    angles = places.astype(jnp.float32)[:, None] * frequency[None, :]
    cosine = jnp.tile(jnp.cos(angles), (1, 4))
    sine = jnp.sin(angles)
    sine = jnp.tile(jnp.concatenate([-sine, sine], axis=1), (1, 2))

    own_ids = lax.dynamic_slice_in_dim(segment_ids, chip * T, T, 1)
    starts = jnp.sum(
        (segment_ids[:, None, :] < own_ids[:, :, None]).astype(jnp.int32), axis=2
    )
    lengths = jnp.sum(valid_blocks, axis=1) * 128
    finish = jnp.minimum(places[None, :] + 1, lengths[:, None])
    bounds = jnp.stack([starts, finish, jnp.broadcast_to(places[None], (MB, T))], axis=1)
    bounds = jnp.pad(jnp.tile(bounds, (1, 1, 2)), ((0, 0), (0, 5), (0, 0)))
    last = (chip * T + T + KB - 1) // KB
    blocks = jnp.stack([starts[:, 0] // KB, jnp.full((MB,), last, jnp.int32)], axis=1)

    def to_columns(rows):
        turned = rows.reshape(MB, T, 8, 64).transpose(0, 3, 2, 1)
        return turned.at[:, :, 0].set(0).reshape(MB, 64, QS)

    def to_rows(columns):
        return columns.reshape(MB, 64, 8, T).transpose(0, 3, 2, 1).reshape(R, 8, 64)

    saved = []
    x = ends_all[0]
    for layer in range(2):
        gains = gains_of(layer)
        n1, qk, v = project(layer, x, gains, bias_of(layer), cosine, sine, w)
        own = jnp.concatenate([qk[:, :64], v[:, :64]], axis=1).reshape(MB, T, 128)
        kv = gather_tokens(own).reshape(64, MB, T, 128)
        qt = jnp.pad(to_columns(qk) * jnp.bfloat16(0.125), ((0, 0), (0, 64), (0, 0)))
        mixed, lse = attend(blocks, qt, kv, bounds)
        attended = to_rows(mixed).astype(jnp.bfloat16).at[:, 0].set(0).reshape(R, QS)
        xo, mid, n2, gu, hid, sq = mlp(layer, x, attended, gains, w)
        saved.append((x, gains, n1, kv, qt, mixed, lse, attended, mid, n2, gu, hid, sq))
        x = xo
    final_out = x

    dout = ends_all[1]
    grads = [None, None]
    smalls = [None, None]
    for layer in (1, 0):
        x, gains, n1, kv, qt, mixed, lse, attended, mid, n2, gu, hid, sq = saved[layer]
        dgu, dmid, da, datt, gain_two = mlp_back(layer, dout, gu, mid, gains, w)
        dot_ = jnp.pad(to_columns(datt), ((0, 0), (64, 0), (0, 0)))
        dqt, terms = attend_back(blocks, qt, dot_, kv, bounds, mixed, lse)
        own = scatter_tokens(terms.reshape(4, 4, 4, MB, T, 128)).reshape(R, 128)
        dqk = to_rows(dqt).at[:, 0].set(own[:, :64]).reshape(R, QS)
        dv = jnp.pad(own[:, 64:], ((0, 0), (0, QS - 64)))
        dx, dqk_low, dv_low, gain_one, bias_sum = project_back(
            layer, dqk, dv, x, dmid, gains, cosine, sine, w
        )
        valid = lax.dynamic_slice_in_dim(valid_blocks, chip // 2, 1, 1).astype(jnp.float32)
        squares = jnp.where(valid > 0, sq[:MB, :3], 0.0)
        smalls[layer] = jnp.stack(
            [
                gain_one[0],
                gain_two[0],
                bias_sum[0],
                jnp.pad(squares.reshape(-1), (0, DP - 9)),
            ]
        )
        small = jnp.concatenate(smalls, axis=0) if layer == 0 else jnp.zeros((8, DP), jnp.float32)
        grads[layer], small_sum = weight_grads(
            layer == 0, n2, dgu, dout, hid, n1, dqk_low, dv_low, da, attended, small
        )
        dout = dx

    def with_bias(layer):
        return grads[layer].at[14, :QS].set(small_sum[4 * layer + 2, :QS]).at[
            14, QS : 2 * QS
        ].set(small_sum[4 * layer + 2, QS:])

    ready = [with_bias(0), with_bias(1)]
    here = jnp.where(core == 0, ready[0], ready[1])
    away = lax.ppermute(jnp.where(core == 0, ready[1], ready[0]), "section", [(0, 1), (1, 0)])
    lower = jnp.where(core == 0, here, away)
    upper = jnp.where(core == 0, away, here)
    sides = (lower, upper)

    def column(start, size):
        return [side[:14, start : start + size] for side in sides]

    grad_gu = jnp.concatenate(column(0, FFH) + column(C_UP, FFH), axis=1)
    grad_down = jnp.concatenate(column(C_DOWN, FFH), axis=1)
    grad_qkv = jnp.concatenate(
        column(C_QK + 64, 448) + column(C_QK, 64) + column(C_VO, 64), axis=1
    )
    grad_out = jnp.concatenate(column(C_VO + 64, 448), axis=1)
    bias_rows = [side[14] for side in sides]
    grad_bias = jnp.concatenate(
        [row[64:QS] for row in bias_rows]
        + [row[:64] for row in bias_rows]
        + [row[QS : QS + 64] for row in bias_rows]
    )
    own_small = lax.dynamic_slice_in_dim(small_sum, 4 * core, 4, 0)
    grad_gain = own_small[:2].reshape(2, 64, 16)[:, :, :14].reshape(2, D)
    counts = jnp.sum(valid_blocks, axis=1).astype(jnp.float32) * 128 * D
    rms = jnp.sqrt(own_small[3, :9].reshape(MB, 3) / counts[:, None])
    ends_out = jnp.where(core == 0, dout, final_out)
    boundary = nt(ends_out, spread).astype(jnp.bfloat16).reshape(1, MB, T, D)
    return (
        boundary,
        grad_qkv[None],
        grad_bias[None],
        grad_out[None],
        grad_gu[None],
        grad_down[None],
        grad_gain[None],
        rms[None],
    )


def solution(mesh):
    in_specs = (
        P("section", None, "dp", None),
        P(),
        P(),
        P("section", "dp", None),
        P("section", None),
        P("section", "dp", None),
        P("section", "dp", None),
        P("section", "dp", None),
        P("section", None, None),
    )
    out_specs = (
        P("section", None, "dp", None),
        P("section", "dp", None),
        P("section", None),
        P("section", "dp", None),
        P("section", "dp", None),
        P("section", "dp", None),
        P("section", None, None),
        P("section", None, None),
    )
    return jax.shard_map(shards, mesh=mesh, in_specs=in_specs, out_specs=out_specs, check_vma=False)
```

time: 3320 us -> 696 us (0.21)
  waiting for transfers between devices: 2130 us -> 0.01 us
  Pallas kernels: 0 us -> 593 us
  matrix products: 362 us -> 4.08 us
  blocking collectives: 297 us -> 0 us
  other arithmetic: 178 us -> 9.44 us
  starting transfers between devices: 162 us -> 9.05 us
  local copies, waits for them, and re-layouts: 161 us -> 76.5 us
    reduce_scatter x4 -> x0, waiting for transfers between devices: 1110 us -> none  [shards(): lax.psum_scatter(key_terms, 'dp', scatter_dimension=0, tiled=True)]
    all_gather x12 -> x0, waiting for transfers between devices: 789 us -> none  [the longest x4 225 us: shards(): lax.all_gather(forward_key_local, 'dp', axis=0, tiled=True)]
    pallas_call x0 -> x19, Pallas kernels: none -> 593 us  [the longest x2 163 us: weight_grads(): pl.pallas_call(functools.partial(weight_grads_kernel, sums), out_shape=(s...]
    dot_general x60 -> x3, matrix products: 362 us -> 4.08 us  [the longest x2 2.37 us: nn(): return jnp.dot(left, right, preferred_element_type=jnp.float32)]
    psum x1 -> x0, blocking collectives: 297 us -> none  [shards(): lax.psum((squares_pick, gain_sum, bias_sum), 'dp')]
    unnamed x18 -> x0, waiting for transfers between devices: 221 us -> none
    ppermute x6 -> x1, starting transfers between devices: 161 us -> 9.05 us  [shards(): lax.ppermute(jnp.where(core == 0, ready[1], ready[0]), 'section', [(0, 1)...]
    unnamed x376 -> x28, local copies, waits for them, and re-layouts: 67.8 us -> 4.36 us
  transfers between devices with their start and end apart: 23 -> 1, of which waited for: 22 -> 0; matrix products, arithmetic and copies ran while one was open for 8% -> 1% of each run, Pallas kernels for 0% -> 0%
where the time goes in v1:
time: 696 us; the launch traced here: 694 us
  Pallas kernels  593 us (85%)
  local copies, waits for them, and re-layouts  76.5 us (11%)
  other arithmetic  9.44 us (1%)
  starting transfers between devices  9.05 us (1%)
    pallas_call x2, Pallas kernels, weight_grads(): pl.pallas_call(functools.partial(weight_grads_kernel, sums), out_shape=(s...  163 us
    pallas_call x1, Pallas kernels, gather_weights(): pl.pallas_call(gather_weights_kernel, out_shape=(shape((2, 4, 4, 4, 16, C...  158 us
    pallas_call x2, Pallas kernels, scatter_tokens(): pl.pallas_call(scatter_tokens_kernel, out_shape=shape((MB, T, 128), jnp.f...  87.3 us
    pallas_call x2, Pallas kernels, gather_tokens(): pl.pallas_call(gather_tokens_kernel, out_shape=shape((4, 4, 4) + own.shap...  61.5 us
    pallas_call x2, Pallas kernels, mlp(): pl.pallas_call(functools.partial(mlp_kernel, layer), out_shape=(shape((R,...  42.6 us
    pallas_call x2, Pallas kernels, mlp_back(): pl.pallas_call(functools.partial(mlp_back_kernel, layer), out_shape=(shap...  28.2 us
    pallas_call x2, Pallas kernels, project_back(): pl.pallas_call(functools.partial(project_back_kernel, layer), out_shape=(...  22.8 us
  transfers between devices with their start and end apart: 1, of which 0 were waited for; matrix products, arithmetic and copies ran while one was open for 1% of the time, Pallas kernels for 0%

profile of v1, /device:TPU:1, one launch (start us, length us, event | category | flops | bytes accessed | tf_op | source)
XLA Modules:
  0.0 694.0 jit_solution(5168642371200596388)
XLA Ops:
  0.7 1.0 dynamic-slice_bitcast_fusion
  1.7 0.9 dynamic-slice_bitcast_fusion.7
  2.6 0.9 dynamic-slice_bitcast_fusion.6
  3.5 0.8 fusion.28
  4.3 1.0 dynamic-slice_bitcast_fusion.1
  7.0 1.7 fusion.8.ends
  10.1 158.2 %gather_weights.1 = (bf16[2,4,4,4,16,8320]{5,4,3,2,1,0:T(8,128)(2,1)}, bf16[2,192,1024]{2,1,0:T(8,128)(2,1)}, bf16[2,16,3328]{2,1,0:T(8,128)(2,1)}) custom-call(bf16[16,8320]{1,0:T(8,128)(2,1)} %pad.85.mine, bf16[16,8320]{1,0:T(8,128)(2,1)} %pad.86.theirs, bf16[192,1024]{1,0:T(8,128)(2,1)} %fusion.8.ends, bf16[16,3328]{1,0:T(8,128)(2,1)} %pad.88.small), custom_call_target="tpu_custom_call" | custom-call | tf_op jit(solution)/shard_map/gather_weights/pallas_call | solution.py:294
  169.2 0.8 slice_reduce_fusion
  170.1 2.0 slice_bitcast_fusion
  175.1 3.9 project.2
  179.1 0.8 slice.432
  179.9 1.2 reshape.638
  181.1 1.5 pad_maximum_fusion
  182.6 25.3 %gather_keys_values.2 = bf16[4,4,4,3,64,128]{5,4,3,2,1,0:T(8,128)(2,1)} custom-call(bf16[3,64,128]{2,1,0:T(8,128)(2,1)} %bitcast.157), custom_call_target="tpu_custom_call" | custom-call | tf_op jit(solution)/shard_map/gather_keys_values/pallas_call | solution.py:322
  208.4 2.3 scatter.40
  213.9 4.7 attention.2
  218.6 1.0 convert_element_type.106
  220.3 2.2 scatter.41
  222.8 0.8 copy.99.attended.att
  223.6 24.1 %mlp.2 = (bf16[192,1024]{1,0:T(8,128)(2,1)}, f32[192,1024]{1,0:T(8,128)}, bf16[192,1024]{1,0:T(8,128)(2,1)}, f32[192,4864]{1,0:T(8,128)}, bf16[192,2432]{1,0:T(8,128)(2,1)}, /*index=5*/f32[8,128]{1,0:T(8,128)}) custom-call(bf16[192,1024]{1,0:T(8,128)(2,1)} %get-tuple-element.293.x, bf16[192,512]{1,0:T(8,128)(2,1)} %copy.99.attended.att, ...), custom_call_target="tpu_custom_call" | custom-call | tf_op jit(solution)/shard_map/mlp/pallas_call | solution.py:598
  248.9 3.9 project.3
  252.9 0.8 slice.437
  253.7 1.2 reshape.642
  254.9 1.5 pad_maximum_fusion.1
  256.4 36.2 %gather_keys_values.3 = bf16[4,4,4,3,64,128]{5,4,3,2,1,0:T(8,128)(2,1)} custom-call(bf16[3,64,128]{2,1,0:T(8,128)(2,1)} %bitcast.158), custom_call_target="tpu_custom_call" | custom-call | tf_op jit(solution)/shard_map/gather_keys_values/pallas_call | solution.py:322
  293.0 2.0 scatter.44
  295.3 0.8 pad.95.qt
  296.1 4.7 attention.3
  300.9 1.0 convert_element_type.112
  302.5 2.8 scatter.45
  305.6 0.8 copy.104.attended.att
  306.4 18.6 %mlp.3 = (bf16[192,1024]{1,0:T(8,128)(2,1)}, f32[192,1024]{1,0:T(8,128)}, bf16[192,1024]{1,0:T(8,128)(2,1)}, f32[192,4864]{1,0:T(8,128)}, bf16[192,2432]{1,0:T(8,128)(2,1)}, /*index=5*/f32[8,128]{1,0:T(8,128)}) custom-call(bf16[192,1024]{1,0:T(8,128)(2,1)} %get-tuple-element.210.x, bf16[192,512]{1,0:T(8,128)(2,1)} %copy.104.attended.att, ...), custom_call_target="tpu_custom_call" | custom-call | tf_op jit(solution)/shard_map/mlp/pallas_call | solution.py:598
  326.1 14.1 %mlp_back.2 = (bf16[192,4864]{1,0:T(8,128)(2,1)}, f32[192,1024]{1,0:T(8,128)}, bf16[192,1024]{1,0:T(8,128)(2,1)}, bf16[192,512]{1,0:T(8,128)(2,1)}, f32[8,1024]{1,0:T(8,128)}) custom-call(bf16[192,1024]{1,0:T(8,128)(2,1)} %get-tuple-element.292.dout.dm, f32[192,4864]{1,0:T(8,128)} %get-tuple-element.214.gu, f32[192,1024]{1,0:T(8,128)} %get-tuple-element.215.mid, ...), custom_call_target="tpu_custom_call" | custom-call | tf_op jit(solution)/shard_map/mlp_back/pallas_call | solution.py:685
  340.2 1.2 reshape.646
  341.7 2.0 scatter.46
  344.8 6.4 attention_back.2
  351.2 1.2 reshape.648
  352.8 49.0 %scatter_key_value_grads.2 = f32[3,64,128]{2,1,0:T(8,128)} custom-call(bf16[4,4,4,3,64,128]{5,4,3,2,1,0:T(8,128)(2,1)} %bitcast.137), custom_call_target="tpu_custom_call" | custom-call | tf_op jit(solution)/shard_map/scatter_key_value_grads/pallas_call | solution.py:357
  401.8 1.1 fusion.49
  402.8 2.2 scatter.49
  405.4 0.9 copy.109.dqk
  406.4 0.8 pad.97.dv
  407.2 11.8 %project_back.2 = (bf16[192,1024]{1,0:T(8,128)(2,1)}, bf16[192,512]{1,0:T(8,128)(2,1)}, bf16[192,512]{1,0:T(8,128)(2,1)}, f32[8,1024]{1,0:T(8,128)}, f32[8,1024]{1,0:T(8,128)}) custom-call(f32[192,512]{1,0:T(8,128)} %copy.109.dqk, f32[192,512]{1,0:T(8,128)} %pad.97.dv, bf16[192,1024]{1,0:T(8,128)(2,1)} %get-tuple-element.210.x, ...), custom_call_target="tpu_custom_call" | custom-call | tf_op jit(solution)/shard_map/project_back/pallas_call | solution.py:741
  418.9 14.2 %mlp_back.3 = (bf16[192,4864]{1,0:T(8,128)(2,1)}, f32[192,1024]{1,0:T(8,128)}, bf16[192,1024]{1,0:T(8,128)(2,1)}, bf16[192,512]{1,0:T(8,128)(2,1)}, f32[8,1024]{1,0:T(8,128)}) custom-call(bf16[192,1024]{1,0:T(8,128)(2,1)} %get-tuple-element.221.dout.dm, f32[192,4864]{1,0:T(8,128)} %get-tuple-element.222.gu, f32[192,1024]{1,0:T(8,128)} %get-tuple-element.223.mid, ...), custom_call_target="tpu_custom_call" | custom-call | tf_op jit(solution)/shard_map/mlp_back/pallas_call | solution.py:685
  433.1 1.2 reshape.654
  434.7 2.0 scatter.50
  437.7 6.3 attention_back.3
  444.0 1.2 reshape.656
  445.5 38.3 %scatter_key_value_grads.3 = f32[3,64,128]{2,1,0:T(8,128)} custom-call(bf16[4,4,4,3,64,128]{5,4,3,2,1,0:T(8,128)(2,1)} %bitcast.136), custom_call_target="tpu_custom_call" | custom-call | tf_op jit(solution)/shard_map/scatter_key_value_grads/pallas_call | solution.py:357
  483.9 1.1 fusion.48
  484.9 2.4 scatter.51
  487.7 1.0 copy.115.dqk
  488.7 0.8 pad.99.dv
  489.5 11.0 %project_back.3 = (bf16[192,1024]{1,0:T(8,128)(2,1)}, bf16[192,512]{1,0:T(8,128)(2,1)}, bf16[192,512]{1,0:T(8,128)(2,1)}, f32[8,1024]{1,0:T(8,128)}, f32[8,1024]{1,0:T(8,128)}) custom-call(f32[192,512]{1,0:T(8,128)} %copy.115.dqk, f32[192,512]{1,0:T(8,128)} %pad.99.dv, bf16[192,1024]{1,0:T(8,128)(2,1)} %get-tuple-element.293.x, ...), custom_call_target="tpu_custom_call" | custom-call | tf_op jit(solution)/shard_map/project_back/pallas_call | solution.py:741
  505.7 86.0 %weight_grads.2 = (f32[16,8320]{1,0:T(8,128)}, f32[8,1024]{1,0:T(8,128)}) custom-call(bf16[192,1024]{1,0:T(8,128)(2,1)} %get-tuple-element.231.n2, bf16[192,4864]{1,0:T(8,128)(2,1)} %get-tuple-element.232.dgu, bf16[192,1024]{1,0:T(8,128)(2,1)} %get-tuple-element.221.dout.dm, bf16[192,2432]{1,0:T(8,128)(2,1)} %get-tuple-element.233.hid, ...), custom_call_target="tpu_custom_call" | custom-call | tf_op jit(solution)/shard_map/weight_grads/pallas_call | solution.py:849
  591.7 0.8 fusion.50
  592.6 1.8 scatter.54
  595.0 76.6 %weight_grads.3 = (f32[16,8320]{1,0:T(8,128)}, f32[8,1024]{1,0:T(8,128)}) custom-call(bf16[192,1024]{1,0:T(8,128)(2,1)} %get-tuple-element.248.n2, bf16[192,4864]{1,0:T(8,128)(2,1)} %get-tuple-element.249.dgu, bf16[192,1024]{1,0:T(8,128)(2,1)} %get-tuple-element.292.dout.dm, bf16[192,2432]{1,0:T(8,128)(2,1)} %get-tuple-element.250.hid, ...), custom_call_target="tpu_custom_call" | custom-call | tf_op jit(solution)/shard_map/weight_grads/pallas_call | solution.py:849
  671.6 1.4 scatter.56
  673.3 1.4 scatter.59
  674.8 9.1 %collective-permute-start = (f32[16,8320]{1,0:T(8,128)S(1)}, f32[16,8320]{1,0:T(8,128)S(1)}, u32[]{:S(2)}, u32[]{:S(2)}) collective-permute-start(f32[16,8320]{1,0:T(8,128)S(1)} %broadcast_select_fusion.2), channel_id=1, source_target_pairs={{0,64},{64,0},{1,65},{65,1},{2,66},{66,2},{3,67},{67,3},{4,68},{68... | collective-permute-start | bytes 1597448 | tf_op jit(solution)/shard_map/ppermute | solution.py:1009
  686.9 1.7 fusion.7
  689.2 1.0 copy.122
  690.2 1.4 copy.121
  (135 shorter events, 31.6 us)
Async XLA Ops:
  0.6 6.4 copy-start
  0.7 8.0 %copy-start.10 = (bf16[1,2,896]{2,1,0:T(2,128)(2,1)S(1)}, bf16[1,2,896]{2,1,0:T(2,128)(2,1)}, u32[]{:S(2)}) copy-start(bf16[1,2,896]{2,1,0:T(2,128)(2,1)} %param.41) | copy-start | bytes 10756
  0.7 8.7 %copy-start.6 = (bf16[1,1152]{1,0:T(2,128)(2,1)S(1)}, bf16[1,1152]{1,0:T(2,128)(2,1)}, u32[]{:S(2)}) copy-start(bf16[1,1152]{1,0:T(2,128)(2,1)} %param.37) | copy-start | bytes 6916
  179.1 32.7 %copy-start.4 = (s32[3,4096]{1,0:T(4,128)S(1)}, s32[3,4096]{1,0:T(4,128)}, u32[]{:S(2)}) copy-start(s32[3,4096]{1,0:T(4,128)} %param.34) | copy-start | bytes 147460
  179.1 33.3 %copy-start.5 = (s32[3,32]{1,0:T(4,128)S(1)}, s32[3,32]{1,0:T(4,128)}, u32[]{:S(2)}) copy-start(s32[3,32]{1,0:T(4,128)} %param.35) | copy-start | bytes 1156
  306.4 18.8 %copy-start.7 = (f32[8,128]{1,0:T(8,128)S(1)}, f32[8,128]{1,0:T(8,128)}, u32[]{:S(2)}) copy-start(f32[8,128]{1,0:T(8,128)} %get-tuple-element.241) | copy-start | bytes 12292
  591.7 95.2 %copy-start.8 = (bf16[192,1024]{1,0:T(8,128)(2,1)S(1)}, bf16[192,1024]{1,0:T(8,128)(2,1)}, u32[]{:S(2)}) copy-start(bf16[192,1024]{1,0:T(8,128)(2,1)} %get-tuple-element.230) | copy-start | bytes 1179652
  591.7 95.1 %copy-start.9 = (bf16[192,1024]{1,0:T(8,128)(2,1)S(1)}, bf16[192,1024]{1,0:T(8,128)(2,1)}, u32[]{:S(2)}) copy-start(bf16[192,1024]{1,0:T(8,128)(2,1)} %get-tuple-element.229) | copy-start | bytes 1179652
  594.4 78.7 %copy-start.2 = (f32[16,8320]{1,0:T(8,128)S(1)}, f32[16,8320]{1,0:T(8,128)}, u32[]{:S(2)}) copy-start(f32[16,8320]{1,0:T(8,128)} %scatter.54) | copy-start | bytes 1597444
  674.7 13.9 %copy-start.3 = (f32[16,8320]{1,0:T(8,128)S(1)}, f32[16,8320]{1,0:T(8,128)}, u32[]{:S(2)}) copy-start(f32[16,8320]{1,0:T(8,128)} %scatter.59) | copy-start | bytes 1597444
  674.8 13.8 %collective-permute-start = (f32[16,8320]{1,0:T(8,128)S(1)}, f32[16,8320]{1,0:T(8,128)S(1)}, u32[]{:S(2)}, u32[]{:S(2)}) collective-permute-start(f32[16,8320]{1,0:T(8,128)S(1)} %broadcast_select_fusion.2), channel_id=1, source_target_pairs={{0,64},{64,0},{1,65},{65,1},{2,66},{66,2},{3,67},{67,3},{4,68},{68... | collective-permute-start | bytes 1597448 | tf_op jit(solution)/shard_map/ppermute | solution.py:1009
  688.6 5.2 copy-start.1

commit v2 on v1

--- a/solution.py
+++ b/solution.py
@@ -27,6 +27,9 @@
 
 THIRDS = ((0, 22 * 128), (22 * 128, 22 * 128), (44 * 128, 21 * 128))
 ORDERS = (("z", "y", "x"), ("y", "x", "z"), ("x", "z", "y"))
+CM, CA = 3 * FFH, 2 * QS
+M_THIRDS = ((0, FFH), (FFH, FFH), (2 * FFH, FFH))
+A_THIRDS = ((0, 384), (384, 384), (768, 256))
 FF_CHUNKS = ((0, 512), (512, 512), (1024, 512), (1536, 512), (2048, 384))
 
 
@@ -199,9 +202,9 @@
     return stages
 
 
-def weight_view(ref):
+def weight_view(ref, thirds=THIRDS):
     def view(chips, j, part):
-        start, size = THIRDS[j]
+        start, size = thirds[j]
         if part is not None:
             half = size // 256 * 128
             start, size = (start, half) if part == 0 else (start + half, size - half)
@@ -250,84 +253,6 @@
     return lax.dot_general(
         left, right, (((0,), (0,)), ((), ())), preferred_element_type=jnp.float32
     )
-
-
-def gather_weights_kernel(mine, theirs, ends, small, w, ends_all, small_all, lsem, xs, xr, ss, rs):
-    place = position()
-    core = lax.axis_index("section")
-    meet(place, core=True)
-    here = (place["x"], place["y"], place["z"])
-    own = w.at[(core,) + here]
-    locals_ = [
-        pltpu.make_async_copy(mine, own, lsem.at[0]),
-        pltpu.make_async_copy(ends, ends_all.at[core], lsem.at[1]),
-        pltpu.make_async_copy(small, small_all.at[core], lsem.at[2]),
-    ]
-    swaps = [
-        send(theirs, own, xs.at[0], xr.at[0], other_core()),
-        send(ends, ends_all.at[core], xs.at[1], xr.at[1], other_core()),
-        send(small, small_all.at[core], xs.at[2], xr.at[2], other_core()),
-    ]
-    arrivals = [
-        send(theirs, w.at[(1 - core,) + here], xs.at[0], xr.at[0], other_core()),
-        send(ends, ends_all.at[1 - core], xs.at[1], xr.at[1], other_core()),
-        send(small, small_all.at[1 - core], xs.at[2], xr.at[2], other_core()),
-    ]
-    for one in locals_ + swaps:
-        one.start()
-    for one in locals_:
-        one.wait()
-    for one in arrivals:
-        one.wait_recv()
-    stages = [
-        gather_stages(weight_view(w.at[layer]), place, ss.at[layer], rs.at[layer])
-        for layer in range(2)
-    ]
-    for step in zip(*stages):
-        for stage in step:
-            stage()
-    for one in swaps:
-        one.wait_send()
-
-
-def gather_weights(mine, theirs, ends, small):
-    return pl.pallas_call(
-        gather_weights_kernel,
-        out_shape=(
-            shape((2, 4, 4, 4, 16, C), jnp.bfloat16),
-            shape((2,) + ends.shape, ends.dtype),
-            shape((2,) + small.shape, small.dtype),
-        ),
-        in_specs=[ANY] * 4,
-        out_specs=(ANY,) * 3,
-        scratch_shapes=[DMA((3,)), DMA((3,)), DMA((3,)), DMA((2, 3, 3, 4)), DMA((2, 3, 3, 4))],
-        compiler_params=params(0),
-        name="gather_weights",
-    )(mine, theirs, ends, small)
-
-
-def gather_tokens_kernel(own, everything, lsem, ss, rs):
-    place = position()
-    meet(place)
-    local = pltpu.make_async_copy(
-        own, everything.at[place["x"], place["y"], place["z"]], lsem
-    )
-    local.start()
-    local.wait()
-    for stage in gather_stages(token_view(everything), place, ss, rs):
-        stage()
-
-
-def gather_tokens(own):
-    return pl.pallas_call(
-        gather_tokens_kernel,
-        out_shape=shape((4, 4, 4) + own.shape, own.dtype),
-        in_specs=[ANY],
-        out_specs=ANY,
-        scratch_shapes=[DMA, DMA((3, 3, 4)), DMA((3, 3, 4))],
-        compiler_params=params(1),
-        name="gather_keys_values",
-    )(own)
 
 
 def scatter_tokens_kernel(terms, out, buf, h0, h1, h2, w0, w1, w2, lsem, ss, rs):
@@ -382,55 +307,6 @@
     allowed = ((keys >= start) & (keys < end)) | (keys == own)
     bias = jnp.where(allowed, 0.0, MASKED)
     return jnp.concatenate([bias] * 4, axis=1)
-
-
-def attend_kernel(blocks, qt, kv, bounds, out, lse):
-    batch = pl.program_id(0)
-    queries = qt[0]
-
-    def step(index, carry):
-        top, total, mixed = carry
-        rows = kv[pl.ds(index * (KB // T), KB // T), 0].reshape(KB, 128)
-        scores = nn(rows, queries) + pair_mask(index * KB, bounds[0])
-        new_top = jnp.maximum(top, jnp.max(scores, axis=0, keepdims=True))
-        shrink = jnp.exp(top - new_top)
-        probs = jnp.exp(scores - new_top)
-        total = total * shrink + jnp.sum(probs, axis=0, keepdims=True)
-        mixed = mixed * shrink + tn(rows, probs.astype(jnp.bfloat16))
-        return new_top, total, mixed
-
-    top, total, mixed = lax.fori_loop(
-        blocks[batch, 0],
-        blocks[batch, 1],
-        step,
-        (
-            jnp.full((1, QS), MASKED, jnp.float32),
-            jnp.zeros((1, QS), jnp.float32),
-            jnp.zeros((128, QS), jnp.float32),
-        ),
-    )
-    out[0] = (mixed / total)[64:, :]
-    lse[0] = jnp.broadcast_to(top + jnp.log(total), (8, QS))
-
-
-def attend(blocks, qt, kv, bounds):
-    return pl.pallas_call(
-        attend_kernel,
-        grid=(MB,),
-        out_shape=(shape((MB, 64, QS), jnp.float32), shape((MB, 8, QS), jnp.float32)),
-        in_specs=[
-            SMEM,
-            pl.BlockSpec((1, 128, QS), lambda m: (m, 0, 0)),
-            pl.BlockSpec((64, 1, T, 128), lambda m: (0, m, 0, 0)),
-            pl.BlockSpec((1, 8, 128), lambda m: (m, 0, 0)),
-        ],
-        out_specs=(
-            pl.BlockSpec((1, 64, QS), lambda m: (m, 0, 0)),
-            pl.BlockSpec((1, 8, QS), lambda m: (m, 0, 0)),
-        ),
-        compiler_params=params(),
-        name="attention",
-    )(blocks, qt, kv, bounds)
 
 
 def attend_back_kernel(blocks, qt, dot_, kv, bounds, out, lse, dqt, dkv):
@@ -497,127 +373,342 @@
     return jnp.concatenate([wide] * MB, axis=0)
 
 
-def project_kernel(layer, x, gains, bias, cosine, sine, w, n1, qk, v, wbuf, sem):
-    load = pltpu.make_async_copy(w.at[layer, :, :, pl.ds(C_QK, 2 * QS)], wbuf, sem)
-    load.start()
-    rows = x[...].astype(jnp.float32)
-    normed = (rows * lax.rsqrt(mean_of(rows * rows) + EPS) * gains[0:1, :]).astype(jnp.bfloat16)
-    n1[...] = normed
-    load.wait()
-    weights = wbuf[...].reshape(DP, 2 * QS)
-    projected = nn(normed, weights[:, : QS + 128]) + bias[0:1, : QS + 128]
-    turned = turn(projected[:, :QS], tiled(cosine[...]), tiled(sine[...]))
-    qk[...] = turned.astype(jnp.bfloat16)
-    v[...] = projected[:, QS:].astype(jnp.bfloat16)
-
-
-def project(layer, x, gains, bias, cosine, sine, w):
-    return pl.pallas_call(
-        functools.partial(project_kernel, layer),
-        out_shape=(
-            shape((R, DP), jnp.bfloat16),
-            shape((R, QS), jnp.bfloat16),
-            shape((R, 128), jnp.bfloat16),
-        ),
-        in_specs=[VMEM] * 5 + [ANY],
-        out_specs=(VMEM,) * 3,
-        scratch_shapes=[pltpu.VMEM((64, 16, 2 * QS), jnp.bfloat16), DMA],
-        compiler_params=params(),
-        name="project",
-    )(x, gains, bias, cosine, sine, w)
-
-
-def mlp_kernel(
-    layer, x, attended, gains, w, xo, mid, n2, gu, hid, sq, wbuf, mine, theirs, wsem, xs, xr
+def to_columns(rows):
+    turned = rows.T
+    return jnp.concatenate([turned[64 * h : 64 * h + 64] for h in range(8)], axis=1)
+
+
+def to_rows(columns):
+    pairs = []
+    for pair in range(4):
+        turned = columns[:, 128 * pair : 128 * pair + 128].T
+        pairs.append(jnp.concatenate([turned[:64], turned[64:]], axis=1))
+    return jnp.concatenate(pairs, axis=1)
+
+
+def without_first_slot(rows):
+    lane = lax.broadcasted_iota(jnp.int32, rows.shape, 1)
+    return jnp.where(lane < 64, 0.0, rows)
+
+
+def forward_kernel(
+    mat, tat, mml, tml, ends, small, cosine, sine, bounds,
+    wa, wm, kv, gu, cot, gains, n1, qt, mixed, lse, att, mid, n2, hid, xs_, sq,
+    ends_v, small_v, stage_a, stage_m, wat, wml, kvb, gu_v, mine, theirs,
+    lsem, ssem, rsem, a_s, a_r, m_s, m_r, k_s, k_r, osem, wsem, xsem, xrsem,
 ):
-    meet(position(), core=True, chips=False)
-
-    def load(index, start, size):
-        cols = pl.ds(start, size)
-        return pltpu.make_async_copy(
-            w.at[layer, :, :, cols], wbuf.at[:, :, cols], wsem.at[index]
-        )
-
-    loads = [load(0, C_VO, QS)]
+    place = position()
+    core = lax.axis_index("section")
+    chip = lax.axis_index("dp")
+    here = (place["x"], place["y"], place["z"])
+    meet(place, core=True)
+
+    traded = ((mat, tat, stage_a), (mml, tml, stage_m), (ends, ends, ends_v), (small, small, small_v))
+    trades = []
+    for index, (keep, give, dst) in enumerate(traded):
+        local = pltpu.make_async_copy(keep, dst.at[core], lsem.at[index])
+        out = send(give, dst.at[core], ssem.at[index], rsem.at[index], other_core())
+        back = send(give, dst.at[1 - core], ssem.at[index], rsem.at[index], other_core())
+        local.start()
+        out.start()
+        trades.append((local, out, back))
+
+    def arrive(index):
+        local, out, back = trades[index]
+        local.wait()
+        back.wait_recv()
+        out.wait_send()
+
+    arrive(0)
+    into = [
+        pltpu.make_async_copy(stage_a.at[layer], wat.at[(layer,) + here], lsem.at[4 + layer])
+        for layer in range(2)
+    ]
+    for one in into:
+        one.start()
+    for one in into:
+        one.wait()
+    attn = [
+        gather_stages(weight_view(wat.at[layer], A_THIRDS), place, a_s.at[layer], a_r.at[layer])
+        for layer in range(2)
+    ]
+    feed = [
+        gather_stages(weight_view(wml, M_THIRDS), place, m_s.at[0], m_r.at[0]),
+        gather_stages(weight_view(wm.at[1], M_THIRDS), place, m_s.at[1], m_r.at[1]),
+    ]
+    keys = [
+        gather_stages(token_view(kvb.at[layer]), place, k_s.at[layer], k_r.at[layer])
+        for layer in range(2)
+    ]
+    attn[0][0]()
+    arrive(1)
+    into = [
+        pltpu.make_async_copy(stage_m.at[0], wml.at[here], lsem.at[4]),
+        pltpu.make_async_copy(stage_m.at[1], wm.at[(1,) + here], lsem.at[5]),
+    ]
+    for one in into:
+        one.start()
+    for one in into:
+        one.wait()
+    feed[0][0]()
+    attn[0][1]()
+    feed[0][1]()
+    attn[0][2]()
+    attn[0][3]()
+    feed[0][2]()
+    feed[0][3]()
+    attn[0][4]()
+    attn[0][5]()
+    attn[0][6]()
+    attn[0][7]()
+    arrive(2)
+    arrive(3)
+    cot[...] = ends_v[...]
+    for layer in range(2):
+        gains[layer] = small_v[layer, 0:8, :].astype(jnp.float32)
+    attn[0][8]()
+
+    outs = []
+
+    def store(src, dst, index):
+        one = pltpu.make_async_copy(src, dst, osem.at[index])
+        one.start()
+        outs.append(one)
+
+    def rows_of(layer):
+        return ends_v[0] if layer == 0 else xs_[0]
+
+    def project(layer):
+        rows = rows_of(layer).astype(jnp.float32)
+        gain = gains[layer, 2:3, :]
+        bias = jnp.where(core == 0, gains[layer, 0:1, :], gains[layer, 1:2, :])
+        normed = (rows * lax.rsqrt(mean_of(rows * rows) + EPS) * gain).astype(jnp.bfloat16)
+        n1[layer] = normed
+        weights = wat[layer].reshape(DP, CA)
+        projected = nn(normed, weights[:, : QS + 128]) + bias[:, : QS + 128]
+        turned = turn(projected[:, :QS], tiled(cosine[...]), tiled(sine[...]))
+        own = jnp.concatenate([turned[:, :64], projected[:, QS : QS + 64]], axis=1)
+        kvb[(layer,) + here] = own.astype(jnp.bfloat16).reshape(MB, T, 128)
+        heads = without_first_slot(turned).astype(jnp.bfloat16).astype(jnp.float32) * 0.125
+        for batch in range(MB):
+            columns = to_columns(heads[batch * T : (batch + 1) * T]).astype(jnp.bfloat16)
+            qt[layer, batch] = jnp.concatenate([columns, jnp.zeros_like(columns)], axis=0)
+
+    def attend(layer, batch):
+        queries = qt[layer, batch]
+        limits = bounds[batch]
+
+        def step(index, carry):
+            top, total, sums = carry
+            rows = kvb[layer, index // 2, pl.ds(index % 2 * 2, 2), :, batch].reshape(KB, 128)
+            scores = nn(rows, queries) + pair_mask(index * KB, limits)
+            new_top = jnp.maximum(top, jnp.max(scores, axis=0, keepdims=True))
+            shrink = jnp.exp(top - new_top)
+            probs = jnp.exp(scores - new_top)
+            total = total * shrink + jnp.sum(probs, axis=0, keepdims=True)
+            sums = sums * shrink + tn(rows, probs.astype(jnp.bfloat16))
+            return new_top, total, sums
+
+        top, total, sums = lax.fori_loop(
+            0,
+            (chip * T + T + KB - 1) // KB,
+            step,
+            (
+                jnp.full((1, QS), MASKED, jnp.float32),
+                jnp.zeros((1, QS), jnp.float32),
+                jnp.zeros((128, QS), jnp.float32),
+            ),
+        )
+        result = (sums / total)[64:, :]
+        mixed[layer, batch] = result
+        lse[layer, batch] = jnp.broadcast_to(top + jnp.log(total), (8, QS))
+        att[layer, pl.ds(batch * T, T), :] = without_first_slot(to_rows(result)).astype(
+            jnp.bfloat16
+        )
+
+    def swap(slot):
+        return send(mine.at[slot], theirs.at[slot], xsem.at[slot], xrsem.at[slot], other_core())
+
+    def branch_of(layer):
+        mine[0] = nt(att[layer], wat[layer, :, :, :, :, QS:].reshape(DP, QS))
+        one = swap(0)
+        one.start()
+        one.wait()
+        branch = mine[0] + theirs[0]
+        middle = rows_of(layer).astype(jnp.float32) + branch
+        mid[layer] = middle
+        scale = lax.rsqrt(mean_of(middle * middle) + EPS)
+        n2[layer] = (middle * scale * gains[layer, 3:4, :]).astype(jnp.bfloat16)
+        return branch
+
+    def feed_forward(layer, branch, hooks):
+        normed = n2[layer]
+        sums = jnp.zeros((R, DP), jnp.float32)
+        for index, (start, size) in enumerate(FF_CHUNKS):
+            hooks[index]()
+
+            def weights(first, start=start, size=size):
+                return wml[:, :, :, :, pl.ds(first + start, size)].reshape(DP, size)
+
+            gate = nn(normed, weights(0))
+            up = nn(normed, weights(FFH))
+            gu_v[:, pl.ds(start, size)] = gate
+            gu_v[:, pl.ds(FFH + start, size)] = up
+            hidden = (gate * jax.nn.sigmoid(gate) * up).astype(jnp.bfloat16)
+            hid[layer, :, pl.ds(start, size)] = hidden
+            sums = sums + nt(hidden, weights(2 * FFH))
+        store(gu_v, gu.at[layer], 4 + layer)
+        mine[1] = sums
+        one = swap(1)
+        one.start()
+        one.wait()
+        result = mine[1] + theirs[1]
+        middle = mid[layer]
+        xs_[layer] = (middle + result).astype(jnp.bfloat16)
+        rows = rows_of(layer).astype(jnp.float32)
+        row = lax.broadcasted_iota(jnp.int32, (8, 128), 0)
+        lane = lax.broadcasted_iota(jnp.int32, (8, 128), 1)
+        table = jnp.zeros((8, 128), jnp.float32)
+        for kind, values in enumerate((rows, branch, result)):
+            squares = jnp.sum(values * values, axis=1, keepdims=True)
+            for batch in range(MB):
+                one = jnp.sum(squares[batch * T : (batch + 1) * T], axis=0, keepdims=True)
+                table = jnp.where((row == batch) & (lane == kind), one, table)
+        sq[layer] = table
+
+    def nothing():
+        pass
+
+    project(0)
+    keys[0][0]()
+    attn[1][0]()
+    feed[0][4]()
+    keys[0][1]()
+    attn[1][1]()
+    keys[0][2]()
+    keys[0][3]()
+    attn[1][2]()
+    attn[1][3]()
+    feed[0][5]()
+    keys[0][4]()
+    attn[1][4]()
+    keys[0][5]()
+    keys[0][6]()
+    attn[1][5]()
+    attn[1][6]()
+    keys[0][7]()
+    feed[0][6]()
+    feed[1][0]()
+    keys[0][8]()
+    store(kvb.at[0], kv.at[0], 0)
+    attend(0, 0)
+    feed[1][1]()
+    attn[1][7]()
+    attend(0, 1)
+    feed[0][7]()
+    feed[1][2]()
+    feed[1][3]()
+    attend(0, 2)
+    feed[1][4]()
+    attn[1][8]()
+    store(wat, wa, 1)
+    branch = branch_of(0)
+    feed[1][5]()
+    feed[0][8]()
+    feed[1][6]()
+    store(wml, wm.at[0], 2)
+    feed_forward(0, branch, [nothing] * 5)
+    project(1)
+    for stage in keys[1][:8]:
+        stage()
+    feed[1][7]()
+    keys[1][8]()
+    store(kvb.at[1], kv.at[1], 3)
+    for batch in range(MB):
+        attend(1, batch)
+    branch = branch_of(1)
+    feed[1][8]()
+    feed[0][9]()
+    outs[2].wait()
+    outs[3].wait()
+    loads = []
     for index, (start, size) in enumerate(FF_CHUNKS):
         for part in range(3):
-            loads.append(load(1 + 3 * index + part, part * FFH + start, size))
+            cols = pl.ds(part * FFH + start, size)
+            loads.append(
+                pltpu.make_async_copy(
+                    wm.at[1, :, :, :, :, cols],
+                    wml.at[:, :, :, :, cols],
+                    wsem.at[3 * index + part],
+                )
+            )
     for one in loads:
         one.start()
 
-    def weights(start, size):
-        return wbuf[:, :, pl.ds(start, size)].reshape(DP, size)
-
-    def swap(slot):
-        return send(
-            mine.at[slot], theirs.at[slot], xs.at[slot], xr.at[slot], other_core()
-        )
-
-    loads[0].wait()
-    mine[0] = nt(attended[...], weights(C_VO, QS))
-    one = swap(0)
-    one.start()
-    one.wait()
-    branch = mine[0] + theirs[0]
-    rows = x[...].astype(jnp.float32)
-    middle = rows + branch
-    mid[...] = middle
-    normed = (middle * lax.rsqrt(mean_of(middle * middle) + EPS) * gains[1:2, :]).astype(
-        jnp.bfloat16
-    )
-    n2[...] = normed
-    total = jnp.zeros((R, DP), jnp.float32)
-    for index, (start, size) in enumerate(FF_CHUNKS):
-        for part in range(3):
-            loads[1 + 3 * index + part].wait()
-        gate = nn(normed, weights(start, size))
-        up = nn(normed, weights(C_UP + start, size))
-        gu[:, pl.ds(start, size)] = gate
-        gu[:, pl.ds(C_UP + start, size)] = up
-        hidden = (gate * jax.nn.sigmoid(gate) * up).astype(jnp.bfloat16)
-        hid[:, pl.ds(start, size)] = hidden
-        total = total + nt(hidden, weights(C_DOWN + start, size))
-    mine[1] = total
-    two = swap(1)
-    two.start()
-    two.wait()
-    out = mine[1] + theirs[1]
-    xo[...] = (middle + out).astype(jnp.bfloat16)
-    row = lax.broadcasted_iota(jnp.int32, (8, 128), 0)
-    lane = lax.broadcasted_iota(jnp.int32, (8, 128), 1)
-    sums = jnp.zeros((8, 128), jnp.float32)
-    for kind, values in enumerate((rows, branch, out)):
-        squares = jnp.sum(values * values, axis=1, keepdims=True)
-        for batch in range(MB):
-            one = jnp.sum(squares[batch * T : (batch + 1) * T], axis=0, keepdims=True)
-            sums = jnp.where((row == batch) & (lane == kind), one, sums)
-    sq[...] = sums
-
-
-def mlp(layer, x, attended, gains, w):
+    def ready(index):
+        for one in loads[3 * index : 3 * index + 3]:
+            one.wait()
+
+    feed_forward(1, branch, [functools.partial(ready, index) for index in range(5)])
+    for index, one in enumerate(outs):
+        if index not in (2, 3):
+            one.wait()
+    for stages in attn + feed[1:] + keys:
+        stages[9]()
+
+
+def forward(mat, tat, mml, tml, ends, small, cosine, sine, bounds):
+    low, full = jnp.bfloat16, jnp.float32
     return pl.pallas_call(
-        functools.partial(mlp_kernel, layer),
+        forward_kernel,
         out_shape=(
-            shape((R, DP), jnp.bfloat16),
-            shape((R, DP), jnp.float32),
-            shape((R, DP), jnp.bfloat16),
-            shape((R, 2 * FFH), jnp.float32),
-            shape((R, FFH), jnp.bfloat16),
-            shape((8, 128), jnp.float32),
+            shape((2, 4, 4, 4, 16, CA), low),
+            shape((2, 4, 4, 4, 16, CM), low),
+            shape((2, 4, 4, 4, MB, T, 128), low),
+            shape((2, R, 2 * FFH), full),
+            shape((2, R, DP), low),
+            shape((2, 8, DP), full),
+            shape((2, R, DP), low),
+            shape((2, MB, 128, QS), low),
+            shape((2, MB, 64, QS), full),
+            shape((2, MB, 8, QS), full),
+            shape((2, R, QS), low),
+            shape((2, R, DP), full),
+            shape((2, R, DP), low),
+            shape((2, R, FFH), low),
+            shape((2, R, DP), low),
+            shape((2, 8, 128), full),
         ),
-        in_specs=[VMEM] * 3 + [ANY],
-        out_specs=(VMEM,) * 6,
+        in_specs=[ANY] * 6 + [VMEM] * 3,
+        out_specs=(ANY,) * 4 + (VMEM,) * 12,
         scratch_shapes=[
-            pltpu.VMEM((64, 16, C), jnp.bfloat16),
-            pltpu.VMEM((2, R, DP), jnp.float32),
-            pltpu.VMEM((2, R, DP), jnp.float32),
-            DMA((16,)),
+            pltpu.VMEM((2, R, DP), low),
+            pltpu.VMEM((2, 16, DP), low),
+            pltpu.VMEM((2, 16, CA), low),
+            pltpu.VMEM((2, 16, CM), low),
+            pltpu.VMEM((2, 4, 4, 4, 16, CA), low),
+            pltpu.VMEM((4, 4, 4, 16, CM), low),
+            pltpu.VMEM((2, 4, 4, 4, MB, T, 128), low),
+            pltpu.VMEM((R, 2 * FFH), full),
+            pltpu.VMEM((2, R, DP), full),
+            pltpu.VMEM((2, R, DP), full),
+            DMA((6,)),
+            DMA((4,)),
+            DMA((4,)),
+            DMA((2, 3, 3, 4)),
+            DMA((2, 3, 3, 4)),
+            DMA((2, 3, 3, 4)),
+            DMA((2, 3, 3, 4)),
+            DMA((2, 3, 3, 4)),
+            DMA((2, 3, 3, 4)),
+            DMA((6,)),
+            DMA((15,)),
             DMA((2,)),
             DMA((2,)),
         ],
-        compiler_params=params(3 + layer),
-        name="mlp",
-    )(x, attended, gains, w)
+        compiler_params=params(0, vmem=60),
+        name="forward",
+    )(mat, tat, mml, tml, ends, small, cosine, sine, bounds)
 
 
 def norm_back(grad, rows, gain):
@@ -628,21 +719,25 @@
 
 
 def mlp_back_kernel(
-    layer, dout, gu, mid, gains, w, dgu, dmid, da, datt, gain, wbuf, mine, theirs, wsem, xs, xr
+    layer, dout, gu, mid, gains, wa, wm, dgu, dmid, da, datt, gain, wbuf, mine, theirs, wsem, xs, xr
 ):
     meet(position(), core=True, chips=False)
 
     def load(index, start, size):
         cols = pl.ds(start, size)
         return pltpu.make_async_copy(
-            w.at[layer, :, :, cols], wbuf.at[:, :, cols], wsem.at[index]
+            wm.at[layer, :, :, cols], wbuf.at[:, :, cols], wsem.at[index]
         )
 
     loads = []
     for index, (start, size) in enumerate(FF_CHUNKS):
         for part in (2, 0, 1):
             loads.append(load(len(loads), part * FFH + start, size))
-    loads.append(load(15, C_VO, QS))
+    loads.append(
+        pltpu.make_async_copy(
+            wa.at[layer, :, :, pl.ds(QS, QS)], wbuf.at[:, :, pl.ds(CM, QS)], wsem.at[15]
+        )
+    )
     for one in loads:
         one.start()
 
@@ -670,7 +765,7 @@
     one = send(mine, theirs, xs, xr, other_core())
     one.start()
     one.wait()
-    back, gain_row = norm_back(mine[...] + theirs[...], mid[...], gains[1:2, :])
+    back, gain_row = norm_back(mine[...] + theirs[...], mid[...], gains[3:4, :])
     gain[...] = jnp.broadcast_to(gain_row, (8, DP))
     middle = grad_in + back
     dmid[...] = middle
@@ -678,10 +773,10 @@
     da[...] = low
     loads[15].wait()
     lane = lax.broadcasted_iota(jnp.int32, (R, QS), 1)
-    datt[...] = jnp.where(lane < 64, 0.0, nn(low, weights(C_VO, QS))).astype(jnp.bfloat16)
-
-
-def mlp_back(layer, dout, gu, mid, gains, w):
+    datt[...] = jnp.where(lane < 64, 0.0, nn(low, weights(CM, QS))).astype(jnp.bfloat16)
+
+
+def mlp_back(layer, dout, gu, mid, gains, wa, wm):
     return pl.pallas_call(
         functools.partial(mlp_back_kernel, layer),
         out_shape=(
@@ -691,10 +786,10 @@
             shape((R, QS), jnp.bfloat16),
             shape((8, DP), jnp.float32),
         ),
-        in_specs=[VMEM] * 4 + [ANY],
+        in_specs=[VMEM] * 4 + [ANY] * 2,
         out_specs=(VMEM,) * 5,
         scratch_shapes=[
-            pltpu.VMEM((64, 16, C), jnp.bfloat16),
+            pltpu.VMEM((64, 16, CM + QS), jnp.bfloat16),
             pltpu.VMEM((R, DP), jnp.float32),
             pltpu.VMEM((R, DP), jnp.float32),
             DMA((16,)),
@@ -703,14 +798,14 @@
         ],
         compiler_params=params(5 + layer),
         name="mlp_back",
-    )(dout, gu, mid, gains, w)
+    )(dout, gu, mid, gains, wa, wm)
 
 
 def project_back_kernel(
     layer, dqk, dv, x, dmid, gains, cosine, sine, w, dx, low, vlow, gain, bias,
     wbuf, mine, theirs, wsem, xs, xr,
 ):
-    load = pltpu.make_async_copy(w.at[layer, :, :, pl.ds(C_QK, 2 * QS)], wbuf, wsem)
+    load = pltpu.make_async_copy(w.at[layer], wbuf, wsem)
     load.start()
     meet(position(), core=True, chips=False)
     turned = turn(dqk[...], tiled(cosine[...]), -tiled(sine[...])).astype(jnp.bfloat16)
@@ -731,7 +826,7 @@
     one.start()
     one.wait()
     back, gain_row = norm_back(
-        mine[...] + theirs[...], x[...].astype(jnp.float32), gains[0:1, :]
+        mine[...] + theirs[...], x[...].astype(jnp.float32), gains[2:3, :]
     )
     gain[...] = jnp.broadcast_to(gain_row, (8, DP))
     dx[...] = (dmid[...] + back).astype(jnp.bfloat16)
@@ -893,11 +988,16 @@
     def widen(rows):
         return nn(rows, spread).astype(jnp.bfloat16)
 
-    def half_of(index):
+    def feed_half(index):
         pieces = (
             lax.dynamic_slice_in_dim(gate_up_weight[0], index * FFH, FFH, 1),
             lax.dynamic_slice_in_dim(gate_up_weight[0], ff + index * FFH, FFH, 1),
             lax.dynamic_slice_in_dim(down_weight[0], index * FFH, FFH, 1),
+        )
+        return jnp.pad(jnp.concatenate(pieces, axis=1), ((0, 2), (0, 0)))
+
+    def heads_half(index):
+        pieces = (
             lax.dynamic_slice_in_dim(qkv_weight[0], D + index * 64, 64, 1),
             lax.dynamic_slice_in_dim(qkv_weight[0], index * 448, 448, 1),
             lax.dynamic_slice_in_dim(qkv_weight[0], D + 128 + index * 64, 64, 1),
@@ -905,29 +1005,18 @@
         )
         return jnp.pad(jnp.concatenate(pieces, axis=1), ((0, 2), (0, 0)))
 
-    small_in = jnp.concatenate(
-        [qkv_bias[0], widen(norm_gains[0]).reshape(-1)], axis=0
-    )
-    small_in = jnp.broadcast_to(small_in[None], (16, small_in.shape[0]))
-    small_in = jnp.pad(small_in, ((0, 0), (0, 3328 - small_in.shape[1])))
-    w6, ends_all, small_all = gather_weights(
-        half_of(core), half_of(1 - core), widen(ends[0].reshape(R, D)), small_in
-    )
-    w = w6.reshape(2, 64, 16, C)
-
-    def bias_of(layer):
-        row = small_all[layer, 0, :1152].astype(jnp.float32)
+    def bias_half(index):
+        row = qkv_bias[0]
         pieces = (
-            lax.dynamic_slice_in_dim(row, D + core * 64, 64),
-            lax.dynamic_slice_in_dim(row, core * 448, 448),
-            lax.dynamic_slice_in_dim(row, D + 128 + core * 64, 64),
-            jnp.zeros((448,), jnp.float32),
-        )
-        return jnp.broadcast_to(jnp.concatenate(pieces)[None], (8, 2 * QS))
-
-    def gains_of(layer):
-        both = small_all[layer, 0, 1152:3200].astype(jnp.float32).reshape(2, DP)
-        return jnp.pad(both, ((0, 6), (0, 0)))
+            row[D + index * 64 : D + index * 64 + 64],
+            row[index * 448 : index * 448 + 448],
+            row[D + 128 + index * 64 : D + 128 + index * 64 + 64],
+            jnp.zeros((448,), row.dtype),
+        )
+        return jnp.concatenate(pieces)[None]
+
+    small_in = jnp.concatenate([bias_half(0), bias_half(1), widen(norm_gains[0])], axis=0)
+    small_in = jnp.pad(small_in, ((0, 12), (0, 0)))
 
     places = chip * T + jnp.arange(T, dtype=jnp.int32)
     frequency = THETA ** (-jnp.arange(32, dtype=jnp.float32) * 2.0 / 64)
@@ -947,41 +1036,52 @@
     last = (chip * T + T + KB - 1) // KB
     blocks = jnp.stack([starts[:, 0] // KB, jnp.full((MB,), last, jnp.int32)], axis=1)
 
-    def to_columns(rows):
+    (
+        wa, wm, kv_all, gu_all, ends_all, gains_all, n1_all, qt_all, mixed_all, lse_all, att_all,
+        mid_all, n2_all, hid_all, x_all, sq_all,
+    ) = forward(
+        heads_half(core),
+        heads_half(1 - core),
+        feed_half(core),
+        feed_half(1 - core),
+        widen(ends[0].reshape(R, D)),
+        small_in,
+        cosine,
+        sine,
+        bounds,
+    )
+    wa = wa.reshape(2, 64, 16, CA)
+    wm = wm.reshape(2, 64, 16, CM)
+    kv_all = kv_all.reshape(2, 64, MB, T, 128)
+    final_out = x_all[1]
+    dout = ends_all[1]
+
+    def columns_of(rows):
         turned = rows.reshape(MB, T, 8, 64).transpose(0, 3, 2, 1)
         return turned.at[:, :, 0].set(0).reshape(MB, 64, QS)
 
-    def to_rows(columns):
+    def rows_of(columns):
         return columns.reshape(MB, 64, 8, T).transpose(0, 3, 2, 1).reshape(R, 8, 64)
 
-    saved = []
-    x = ends_all[0]
-    for layer in range(2):
-        gains = gains_of(layer)
-        n1, qk, v = project(layer, x, gains, bias_of(layer), cosine, sine, w)
-        own = jnp.concatenate([qk[:, :64], v[:, :64]], axis=1).reshape(MB, T, 128)
-        kv = gather_tokens(own).reshape(64, MB, T, 128)
-        qt = jnp.pad(to_columns(qk) * jnp.bfloat16(0.125), ((0, 0), (0, 64), (0, 0)))
-        mixed, lse = attend(blocks, qt, kv, bounds)
-        attended = to_rows(mixed).astype(jnp.bfloat16).at[:, 0].set(0).reshape(R, QS)
-        xo, mid, n2, gu, hid, sq = mlp(layer, x, attended, gains, w)
-        saved.append((x, gains, n1, kv, qt, mixed, lse, attended, mid, n2, gu, hid, sq))
-        x = xo
-    final_out = x
-
-    dout = ends_all[1]
     grads = [None, None]
     smalls = [None, None]
     for layer in (1, 0):
-        x, gains, n1, kv, qt, mixed, lse, attended, mid, n2, gu, hid, sq = saved[layer]
-        dgu, dmid, da, datt, gain_two = mlp_back(layer, dout, gu, mid, gains, w)
-        dot_ = jnp.pad(to_columns(datt), ((0, 0), (64, 0), (0, 0)))
+        gains, n1, kv, qt, mixed, lse, attended, mid, n2, gu, hid, sq = (
+            member[layer]
+            for member in (
+                gains_all, n1_all, kv_all, qt_all, mixed_all, lse_all, att_all, mid_all, n2_all,
+                gu_all, hid_all, sq_all,
+            )
+        )
+        x = x_all[0] if layer == 1 else ends_all[0]
+        dgu, dmid, da, datt, gain_two = mlp_back(layer, dout, gu, mid, gains, wa, wm)
+        dot_ = jnp.pad(columns_of(datt), ((0, 0), (64, 0), (0, 0)))
         dqt, terms = attend_back(blocks, qt, dot_, kv, bounds, mixed, lse)
         own = scatter_tokens(terms.reshape(4, 4, 4, MB, T, 128)).reshape(R, 128)
-        dqk = to_rows(dqt).at[:, 0].set(own[:, :64]).reshape(R, QS)
+        dqk = rows_of(dqt).at[:, 0].set(own[:, :64]).reshape(R, QS)
         dv = jnp.pad(own[:, 64:], ((0, 0), (0, QS - 64)))
         dx, dqk_low, dv_low, gain_one, bias_sum = project_back(
-            layer, dqk, dv, x, dmid, gains, cosine, sine, w
+            layer, dqk, dv, x, dmid, gains, cosine, sine, wa
         )
         valid = lax.dynamic_slice_in_dim(valid_blocks, chip // 2, 1, 1).astype(jnp.float32)
         squares = jnp.where(valid > 0, sq[:MB, :3], 0.0)

time: 696 us -> 617 us (0.89)
  Pallas kernels: 593 us -> 514 us
    pallas_call x9 -> x1, Pallas kernels: 280 us -> 202 us  [forward(): pl.pallas_call(forward_kernel, out_shape=(shape((2, 4, 4, 4, 16, CA), low...]
    squeeze x1 -> x13, local copies, waits for them, and re-layouts: 2.04 us -> 17.7 us  [the longest x11 16 us: shards(): member[layer]]
    scatter x12 -> x6, local copies, waits for them, and re-layouts: 19.4 us -> 9.86 us  [the longest x4 5.34 us: shards(): dqk = rows_of(dqt).at[:, 0].set(own[:, :64]).reshape(R, QS)]
    slice x3, local copies, waits for them, and re-layouts: 2.46 us -> 9.8 us  [the longest x1 8.1 us: shards(): member[layer]]
where the time goes in v2:
time: 617 us; the launch traced here: 610 us
  Pallas kernels  514 us (83%)
  local copies, waits for them, and re-layouts  74.6 us (12%)
  starting transfers between devices  10.3 us (2%)
    pallas_call x1, Pallas kernels, forward(): pl.pallas_call(forward_kernel, out_shape=(shape((2, 4, 4, 4, 16, CA), low...  202 us
    pallas_call x2, Pallas kernels, weight_grads(): pl.pallas_call(functools.partial(weight_grads_kernel, sums), out_shape=(s...  162 us
    pallas_call x2, Pallas kernels, scatter_tokens(): pl.pallas_call(scatter_tokens_kernel, out_shape=shape((MB, T, 128), jnp.f...  85.3 us
    pallas_call x2, Pallas kernels, mlp_back(): pl.pallas_call(functools.partial(mlp_back_kernel, layer), out_shape=(shap...  28.2 us
    pallas_call x2, Pallas kernels, project_back(): pl.pallas_call(functools.partial(project_back_kernel, layer), out_shape=(...  24.2 us
    squeeze x11, local copies, waits for them, and re-layouts, shards(): member[layer]  16 us
    pallas_call x2, Pallas kernels, attend_back(): pl.pallas_call(attend_back_kernel, grid=(MB,), out_shape=(shape((MB, 64,...  12.7 us
  transfers between devices with their start and end apart: 1, of which 0 were waited for; matrix products, arithmetic and copies ran while one was open for 1% of the time, Pallas kernels for 0%

profile of v2, /device:TPU:1, one launch (start us, length us, event | category | flops | bytes accessed | tf_op | source)
XLA Modules:
  0.0 610.3 jit_solution(3881034235569711168)
XLA Ops:
  0.7 0.9 slice_bitcast_fusion.32
  1.6 0.8 slice_reduce_fusion.1
  2.5 0.8 constant_dynamic-slice_fusion.7
  3.2 1.3 convert_reduce_fusion
  4.6 0.8 reduce_sum.20
  6.6 0.7 tile.30.sine
  8.0 1.4 fusion.10
  9.4 1.7 fusion.8.ends
  12.0 0.9 fusion.20
  12.8 0.7 fusion.36
  13.6 201.8 %forward.1 = (bf16[2,4,4,4,16,1024]{5,4,3,2,1,0:T(8,128)(2,1)}, bf16[2,4,4,4,16,7296]{5,4,3,2,1,0:T(8,128)(2,1)}, bf16[2,4,4,4,3,64,128]{6,5,4,3,2,1,0:T(8,128)(...) custom-call(bf16[16,1024]{1,0:T(8,128)(2,1)} %get-tuple-element.295., ...), custom_call_target="tpu_custom_call" | custom-call | tf_op jit(solution)/shard_map/forward/pallas_call | solution.py:662
  216.5 6.8 %slice_bitcast_fusion = (f32[192,4864]{1,0:T(8,128)}, f32[192,4864]{1,0:T(8,128)}) fusion(f32[2,192,4864]{2,1,0:T(8,128)} %get-tuple-element.149), kind=kLoop, calls=%fused_computation | loop fusion | bytes 14942208 | tf_op jit(solution)/shard_map/squeeze | solution.py:1070
  223.3 1.3 slice_bitcast_fusion.4
  224.6 0.9 slice_bitcast_fusion.10
  226.2 14.1 %mlp_back.2 = (bf16[192,4864]{1,0:T(8,128)(2,1)}, f32[192,1024]{1,0:T(8,128)}, bf16[192,1024]{1,0:T(8,128)(2,1)}, bf16[192,512]{1,0:T(8,128)(2,1)}, f32[8,1024]{1,0:T(8,128)}) custom-call(bf16[192,1024]{1,0:T(8,128)(2,1)} %get-tuple-element.231.dout.dm, f32[192,4864]{1,0:T(8,128)} %get-tuple-element.217.gu, f32[192,1024]{1,0:T(8,128)} %get-tuple-element.225.mid, ...), custom_call_target="tpu_custom_call" | custom-call | tf_op jit(solution)/shard_map/mlp_back/pallas_call | solution.py:780
  240.2 1.2 reshape.486
  241.8 2.5 scatter.26
  244.6 0.8 pad.70.dot_
  245.4 8.1 %fusion.64 = (bf16[1,4,4,4,3,64,128]{6,5,4,3,2,1,0:T(8,128)(2,1)}, bf16[1,4,4,4,3,64,128]{6,5,4,3,2,1,0:T(8,128)(2,1)}) fusion(bf16[2,4,4,4,3,64,128]{6,5,4,3,2,1,0:T(8,128)(2,1)} %get-tuple-element.155), kind=kLoop, calls=%fused_computation.154 | loop fusion | bytes 12582912 | tf_op jit(solution)/shard_map/slice | solution.py:1070
  253.5 1.0 slice_bitcast_fusion.11
  254.5 1.0 slice_bitcast_fusion.15
  256.7 6.4 %attention_back.2 = (f32[3,64,512]{2,1,0:T(8,128)}, bf16[64,3,64,128]{3,2,1,0:T(8,128)(2,1)}) custom-call(s32[3,2]{1,0:T(4,128)} %stack.17.blocks, bf16[3,128,512]{2,1,0:T(8,128)(2,1)} %get-tuple-element.234.qt, bf16[3,128,512]{2,1,0:T(8,128)(2,1)} %pad.70.dot_, bf16[64,3,64,128]{3,2,1,0:T(8,128)(2,1)} %bitcast.157, s32[3,8,128]{2,1,0:T(8,128)} %pad.69.bounds, ...), custom_call_target="tpu_custom_call" | custom-call | tf_op jit(solution)/shard_map/attention_back/pallas_call | solution.py:336
  263.0 1.2 reshape.488
  264.5 48.1 %scatter_key_value_grads.2 = f32[3,64,128]{2,1,0:T(8,128)} custom-call(bf16[4,4,4,3,64,128]{5,4,3,2,1,0:T(8,128)(2,1)} %bitcast.159), custom_call_target="tpu_custom_call" | custom-call | tf_op jit(solution)/shard_map/scatter_key_value_grads/pallas_call | solution.py:282
  312.7 1.1 fusion.72
  313.7 2.2 scatter.29
  316.3 0.9 copy.56.dqk
  317.3 0.8 pad.71.dv
  318.1 0.8 slice_bitcast_fusion.12.x
  318.9 12.1 %project_back.2 = (bf16[192,1024]{1,0:T(8,128)(2,1)}, bf16[192,512]{1,0:T(8,128)(2,1)}, bf16[192,512]{1,0:T(8,128)(2,1)}, f32[8,1024]{1,0:T(8,128)}, f32[8,1024]{1,0:T(8,128)}) custom-call(f32[192,512]{1,0:T(8,128)} %copy.56.dqk, f32[192,512]{1,0:T(8,128)} %pad.71.dv, bf16[192,1024]{1,0:T(8,128)(2,1)} %slice_bitcast_fusion.12.x, ...), custom_call_target="tpu_custom_call" | custom-call | tf_op jit(solution)/shard_map/project_back/pallas_call | solution.py:836
  331.0 14.1 %mlp_back.3 = (bf16[192,4864]{1,0:T(8,128)(2,1)}, f32[192,1024]{1,0:T(8,128)}, bf16[192,1024]{1,0:T(8,128)(2,1)}, bf16[192,512]{1,0:T(8,128)(2,1)}, f32[8,1024]{1,0:T(8,128)}) custom-call(bf16[192,1024]{1,0:T(8,128)(2,1)} %get-tuple-element.162.dout.dm, f32[192,4864]{1,0:T(8,128)} %get-tuple-element.216.gu, f32[192,1024]{1,0:T(8,128)} %get-tuple-element.224.mid, ...), custom_call_target="tpu_custom_call" | custom-call | tf_op jit(solution)/shard_map/mlp_back/pallas_call | solution.py:780
  345.2 1.2 reshape.494
  346.7 2.0 scatter.30
  349.0 0.8 pad.72.dot_
  349.8 6.3 %attention_back.3 = (f32[3,64,512]{2,1,0:T(8,128)}, bf16[64,3,64,128]{3,2,1,0:T(8,128)(2,1)}) custom-call(s32[3,2]{1,0:T(4,128)} %stack.17.blocks, bf16[3,128,512]{2,1,0:T(8,128)(2,1)} %get-tuple-element.235.qt, bf16[3,128,512]{2,1,0:T(8,128)(2,1)} %pad.72.dot_, bf16[64,3,64,128]{3,2,1,0:T(8,128)(2,1)} %bitcast.156, s32[3,8,128]{2,1,0:T(8,128)} %pad.69.bounds, ...), custom_call_target="tpu_custom_call" | custom-call | tf_op jit(solution)/shard_map/attention_back/pallas_call | solution.py:336
  356.1 1.2 reshape.496
  357.7 37.2 %scatter_key_value_grads.3 = f32[3,64,128]{2,1,0:T(8,128)} custom-call(bf16[4,4,4,3,64,128]{5,4,3,2,1,0:T(8,128)(2,1)} %bitcast.158), custom_call_target="tpu_custom_call" | custom-call | tf_op jit(solution)/shard_map/scatter_key_value_grads/pallas_call | solution.py:282
  394.8 1.1 fusion.71
  395.9 2.4 scatter.31
  398.7 0.9 copy.62.dqk
  399.6 0.8 pad.73.dv
  400.4 12.1 %project_back.3 = (bf16[192,1024]{1,0:T(8,128)(2,1)}, bf16[192,512]{1,0:T(8,128)(2,1)}, bf16[192,512]{1,0:T(8,128)(2,1)}, f32[8,1024]{1,0:T(8,128)}, f32[8,1024]{1,0:T(8,128)}) custom-call(f32[192,512]{1,0:T(8,128)} %copy.62.dqk, f32[192,512]{1,0:T(8,128)} %pad.73.dv, bf16[192,1024]{1,0:T(8,128)(2,1)} %get-tuple-element.230.x, ...), custom_call_target="tpu_custom_call" | custom-call | tf_op jit(solution)/shard_map/project_back/pallas_call | solution.py:836
  412.5 0.9 slice.469
  413.4 0.8 slice.471
  414.1 0.8 slice.470
  414.9 0.8 slice.474
  415.7 0.8 slice.476
  416.4 0.8 slice.475
  417.2 1.4 slice_bitcast_fusion.3
  418.6 0.9 slice_bitcast_fusion.8
  419.5 0.9 slice_bitcast_fusion.9
  420.4 0.8 slice_bitcast_fusion.18
  421.9 84.6 %weight_grads.2 = (f32[16,8320]{1,0:T(8,128)}, f32[8,1024]{1,0:T(8,128)}) custom-call(bf16[192,1024]{1,0:T(8,128)(2,1)} %get-tuple-element.228.n2, bf16[192,4864]{1,0:T(8,128)(2,1)} %get-tuple-element.169.dgu, bf16[192,1024]{1,0:T(8,128)(2,1)} %get-tuple-element.162.dout.dm, bf16[192,2432]{1,0:T(8,128)(2,1)} %get-tuple-element.220.hid, ...), custom_call_target="tpu_custom_call" | custom-call | tf_op jit(solution)/shard_map/weight_grads/pallas_call | solution.py:944
  506.5 0.8 fusion.73
  507.3 1.6 scatter.34
  509.5 77.1 %weight_grads.3 = (f32[16,8320]{1,0:T(8,128)}, f32[8,1024]{1,0:T(8,128)}) custom-call(bf16[192,1024]{1,0:T(8,128)(2,1)} %get-tuple-element.229.n2, bf16[192,4864]{1,0:T(8,128)(2,1)} %get-tuple-element.185.dgu, bf16[192,1024]{1,0:T(8,128)(2,1)} %get-tuple-element.231.dout.dm, bf16[192,2432]{1,0:T(8,128)(2,1)} %get-tuple-element.221.hid, ...), custom_call_target="tpu_custom_call" | custom-call | tf_op jit(solution)/shard_map/weight_grads/pallas_call | solution.py:944
  586.7 1.4 scatter.36
  588.3 1.4 scatter.39
  589.8 10.3 %collective-permute-start = (f32[16,8320]{1,0:T(8,128)S(1)}, f32[16,8320]{1,0:T(8,128)S(1)}, u32[]{:S(2)}, u32[]{:S(2)}) collective-permute-start(f32[16,8320]{1,0:T(8,128)S(1)} %broadcast_select_fusion.2), channel_id=1, source_target_pairs={{0,64},{64,0},{1,65},{65,1},{2,66},{66,2},{3,67},{67,3},{4,68},{68... | collective-permute-start | bytes 1597448 | tf_op jit(solution)/shard_map/ppermute | solution.py:1109
  600.1 0.8 constant_dynamic-slice_fusion
  600.9 0.7 broadcast_in_dim_reshape.3
  603.1 1.7 fusion.7
  605.4 1.0 copy.67
  606.4 1.4 copy.66
  (120 shorter events, 14.5 us)
Async XLA Ops:
  0.6 8.7 %copy-start = (bf16[1,3,64,896]{3,2,1,0:T(8,128)(2,1)S(1)}, bf16[1,3,64,896]{3,2,1,0:T(8,128)(2,1)}, u32[]{:S(2)}) copy-start(bf16[1,3,64,896]{3,2,1,0:T(8,128)(2,1)} %param.25) | copy-start | bytes 1032196
  0.7 10.4 %copy-start.15 = (bf16[1,14,4864]{2,1,0:T(8,128)(2,1)S(1)}, bf16[1,14,4864]{2,1,0:T(8,128)(2,1)}, u32[]{:S(2)}) copy-start(bf16[1,14,4864]{2,1,0:T(8,128)(2,1)} %param.32) | copy-start | bytes 408580
  0.7 10.4 %copy-start.18 = (bf16[1,14,1152]{2,1,0:T(8,128)(2,1)S(1)}, bf16[1,14,1152]{2,1,0:T(8,128)(2,1)}, u32[]{:S(2)}) copy-start(bf16[1,14,1152]{2,1,0:T(8,128)(2,1)} %param.28) | copy-start | bytes 96772
  0.7 10.5 %copy-start.19 = (bf16[1,14,896]{2,1,0:T(8,128)(2,1)S(1)}, bf16[1,14,896]{2,1,0:T(8,128)(2,1)}, u32[]{:S(2)}) copy-start(bf16[1,14,896]{2,1,0:T(8,128)(2,1)} %param.30) | copy-start | bytes 75268
  0.7 11.3 %copy-start.12 = (bf16[1,14,9728]{2,1,0:T(8,128)(2,1)S(1)}, bf16[1,14,9728]{2,1,0:T(8,128)(2,1)}, u32[]{:S(2)}) copy-start(bf16[1,14,9728]{2,1,0:T(8,128)(2,1)} %param.31) | copy-start | bytes 817156
  2.5 213.5 %copy-start.20 = (s32[3,32]{1,0:T(4,128)S(1)}, s32[3,32]{1,0:T(4,128)}, u32[]{:S(2)}) copy-start(s32[3,32]{1,0:T(4,128)} %param.27) | copy-start | bytes 1156
  216.5 6.8 %copy-start.5 = (f32[2,192,1024]{2,1,0:T(8,128)S(1)}, f32[2,192,1024]{2,1,0:T(8,128)}, u32[]{:S(2)}) copy-start(f32[2,192,1024]{2,1,0:T(8,128)} %get-tuple-element.150) | copy-start | bytes 4718596
  223.3 1.3 copy-start.10
  223.3 2.3 copy-start.17
  245.4 8.1 %copy-start.9 = (f32[2,3,64,512]{3,2,1,0:T(8,128)S(1)}, f32[2,3,64,512]{3,2,1,0:T(8,128)}, u32[]{:S(2)}) copy-start(f32[2,3,64,512]{3,2,1,0:T(8,128)} %get-tuple-element.156) | copy-start | bytes 2359300
  245.4 9.1 %copy-start.8 = (bf16[2,3,128,512]{3,2,1,0:T(8,128)(2,1)S(1)}, bf16[2,3,128,512]{3,2,1,0:T(8,128)(2,1)}, u32[]{:S(2)}) copy-start(bf16[2,3,128,512]{3,2,1,0:T(8,128)(2,1)} %get-tuple-element.147) | copy-start | bytes 2359300
  245.4 10.0 %copy-start.16 = (f32[2,3,8,512]{3,2,1,0:T(8,128)S(1)}, f32[2,3,8,512]{3,2,1,0:T(8,128)}, u32[]{:S(2)}) copy-start(f32[2,3,8,512]{3,2,1,0:T(8,128)} %get-tuple-element.157) | copy-start | bytes 294916
  264.5 53.5 %copy-start.13 = (bf16[2,192,1024]{2,1,0:T(8,128)(2,1)S(1)}, bf16[2,192,1024]{2,1,0:T(8,128)(2,1)}, u32[]{:S(2)}) copy-start(bf16[2,192,1024]{2,1,0:T(8,128)(2,1)} %get-tuple-element.160) | copy-start | bytes 2359300
  398.7 18.5 %copy-start.4 = (bf16[2,192,2432]{2,1,0:T(8,128)(2,1)S(1)}, bf16[2,192,2432]{2,1,0:T(8,128)(2,1)}, u32[]{:S(2)}) copy-start(bf16[2,192,2432]{2,1,0:T(8,128)(2,1)} %get-tuple-element.170) | copy-start | bytes 5603332
  400.4 18.2 %copy-start.7 = (bf16[2,192,1024]{2,1,0:T(8,128)(2,1)S(1)}, bf16[2,192,1024]{2,1,0:T(8,128)(2,1)}, u32[]{:S(2)}) copy-start(bf16[2,192,1024]{2,1,0:T(8,128)(2,1)} %get-tuple-element.171) | copy-start | bytes 2359300
  412.5 7.0 %copy-start.6 = (bf16[2,192,1024]{2,1,0:T(8,128)(2,1)S(1)}, bf16[2,192,1024]{2,1,0:T(8,128)(2,1)}, u32[]{:S(2)}) copy-start(bf16[2,192,1024]{2,1,0:T(8,128)(2,1)} %get-tuple-element.168) | copy-start | bytes 2359300
  412.5 7.9 %copy-start.11 = (bf16[2,192,512]{2,1,0:T(8,128)(2,1)S(1)}, bf16[2,192,512]{2,1,0:T(8,128)(2,1)}, u32[]{:S(2)}) copy-start(bf16[2,192,512]{2,1,0:T(8,128)(2,1)} %get-tuple-element.175) | copy-start | bytes 1179652
  506.5 96.6 %copy-start.14 = (bf16[2,192,1024]{2,1,0:T(8,128)(2,1)S(1)}, bf16[2,192,1024]{2,1,0:T(8,128)(2,1)}, u32[]{:S(2)}) copy-start(bf16[2,192,1024]{2,1,0:T(8,128)(2,1)} %get-tuple-element.160) | copy-start | bytes 2359300
  508.9 79.1 %copy-start.2 = (f32[16,8320]{1,0:T(8,128)S(1)}, f32[16,8320]{1,0:T(8,128)}, u32[]{:S(2)}) copy-start(f32[16,8320]{1,0:T(8,128)} %scatter.34) | copy-start | bytes 1597444
  589.7 15.1 %copy-start.3 = (f32[16,8320]{1,0:T(8,128)S(1)}, f32[16,8320]{1,0:T(8,128)}, u32[]{:S(2)}) copy-start(f32[16,8320]{1,0:T(8,128)} %scatter.39) | copy-start | bytes 1597444
  589.8 15.0 %collective-permute-start = (f32[16,8320]{1,0:T(8,128)S(1)}, f32[16,8320]{1,0:T(8,128)S(1)}, u32[]{:S(2)}, u32[]{:S(2)}) collective-permute-start(f32[16,8320]{1,0:T(8,128)S(1)} %broadcast_select_fusion.2), channel_id=1, source_target_pairs={{0,64},{64,0},{1,65},{65,1},{2,66},{66,2},{3,67},{67,3},{4,68},{68... | collective-permute-start | bytes 1597448 | tf_op jit(solution)/shard_map/ppermute | solution.py:1109
  604.8 5.2 copy-start.1

commit v3 on v2

--- a/solution.py
+++ b/solution.py
@@ -129,37 +129,27 @@
     return stages
 
 
-def scatter_stages(view, halves, wholes, place, send_sems, recv_sems, width, final):
+def scatter_stages(view, halves, wholes, place, send_sems, recv_sems, final, begin=0):
     pending = []
 
-    def chips_of(j, phase, whose):
-        order = ORDERS[j][::-1]
-        return cube(order[phase + 1 :], whose)
-
-    def axis_of(j, phase):
-        return ORDERS[j][::-1][phase]
-
-    def add(dst, *terms):
-        dst[...] = sum(term[...].astype(jnp.float32) for term in terms).astype(dst.dtype)
-
     def half_copy(j, phase, k, distance):
-        src = view(chips_of(j, phase, moved(place, axis_of(j, phase), 2)), j, k)
+        far = moved(place, back_axis(j, phase), 2)
         return send(
-            src,
+            view(back_chips(j, phase, far), j, k),
             halves[phase](j, k),
             send_sems.at[j, phase, k],
             recv_sems.at[j, phase, k],
-            chip_id(moved(place, axis_of(j, phase), distance)),
+            chip_id(moved(place, back_axis(j, phase), distance)),
         )
 
     def whole_copy(j, phase, k, distance):
-        src = view(chips_of(j, phase, moved(place, axis_of(j, phase), distance)), j, None)
+        near = moved(place, back_axis(j, phase), distance)
         return send(
-            src,
-            wholes[phase](j, k, None),
+            view(back_chips(j, phase, near), j, None),
+            wholes[phase](j, k),
             send_sems.at[j, phase, 2 + k],
             recv_sems.at[j, phase, 2 + k],
-            chip_id(moved(place, axis_of(j, phase), distance)),
+            chip_id(near),
         )
 
     def first(phase):
@@ -173,7 +163,8 @@
         for j in range(3):
             for k, distance in ((0, 1), (1, -1)):
                 half_copy(j, phase, k, distance).wait_recv()
-                mine = view(chips_of(j, phase, moved(place, axis_of(j, phase), distance)), j, k)
+                near = moved(place, back_axis(j, phase), distance)
+                mine = view(back_chips(j, phase, near), j, k)
                 add(mine, mine, halves[phase](j, k))
                 one = whole_copy(j, phase, k, distance)
                 one.start()
@@ -183,23 +174,148 @@
         for j in range(3):
             for k, distance in ((0, 1), (1, -1)):
                 whole_copy(j, phase, k, distance).wait_recv()
-            mine = view(chips_of(j, phase, place), j, None)
+            mine = view(back_chips(j, phase, place), j, None)
             if phase < 2:
-                add(mine, mine, wholes[phase](j, 0, None), wholes[phase](j, 1, None))
+                add(mine, mine, wholes[phase](j, 0), wholes[phase](j, 1))
             else:
-                final(j, mine, wholes[phase](j, 0, None), wholes[phase](j, 1, None))
+                final(j, mine, wholes[phase](j, 0), wholes[phase](j, 1))
 
     def finish():
         for one in pending:
             one.wait_send()
 
     stages = []
-    for phase in range(3):
+    for phase in range(begin, 3):
         stages.append(functools.partial(first, phase))
         stages.append(functools.partial(second, phase))
         stages.append(functools.partial(third, phase))
     stages.append(finish)
     return stages
+
+
+def back_axis(j, phase):
+    return ORDERS[j][2 - phase]
+
+
+def back_chips(j, phase, whose):
+    return cube(ORDERS[j][: 2 - phase], whose)
+
+
+def add(dst, *terms):
+    dst[...] = sum(term[...].astype(jnp.float32) for term in terms).astype(dst.dtype)
+
+
+def half_of(size, part):
+    half = size // 256 * 128
+    return (0, half) if part == 0 else (half, size - half)
+
+
+def scatter_large_stages(
+    source, slab, got_half, got_whole, spare, inner_halves, inner_wholes, place,
+    hs, hr, os_, or_, ws, wr, ls, ss, rs, final,
+):
+    pending = []
+    turns = [(j, k, (1, -1)[k]) for j in range(3) for k in range(2)]
+
+    def half_ref(j, k):
+        return got_half.at[j, k, :, :, :, pl.ds(0, half_of(FFH, k)[1])]
+
+    def whole_ref(j, k, part):
+        return got_whole.at[j, k, :, :, :, pl.ds(*half_of(FFH, part))]
+
+    def near(j, distance):
+        return moved(place, back_axis(j, 0), distance)
+
+    def half_copy(j, k, distance):
+        return send(
+            source(back_chips(j, 0, near(j, 2)), j, k),
+            half_ref(j, k),
+            hs.at[j, k],
+            hr.at[j, k],
+            chip_id(near(j, distance)),
+        )
+
+    def other_copy(j, k, distance):
+        return send(
+            source(back_chips(j, 0, near(j, distance)), j, 1 - k),
+            whole_ref(j, k, 1 - k),
+            os_.at[j, k],
+            or_.at[j, k],
+            chip_id(near(j, distance)),
+        )
+
+    def summed_copy(j, k, distance):
+        return send(
+            half_ref(j, k),
+            whole_ref(j, k, k),
+            ws.at[j, k],
+            wr.at[j, k],
+            chip_id(near(j, distance)),
+        )
+
+    def own_load(index):
+        j, k, distance = turns[index]
+        return pltpu.make_async_copy(
+            source(back_chips(j, 0, near(j, distance)), j, k),
+            spare.at[index % 2, :, :, :, pl.ds(0, half_of(FFH, k)[1])],
+            ls.at[index],
+        )
+
+    def slab_load(j):
+        return pltpu.make_async_copy(
+            source(back_chips(j, 0, place), j, None), slab.at[j], ls.at[6 + j]
+        )
+
+    def first():
+        for j, k, distance in turns:
+            one = half_copy(j, k, distance)
+            one.start()
+            pending.append(one)
+        for j, k, distance in turns:
+            one = other_copy(j, k, distance)
+            one.start()
+            pending.append(one)
+        for j in range(3):
+            slab_load(j).start()
+        own_load(0).start()
+        own_load(1).start()
+
+    def second():
+        for index, (j, k, distance) in enumerate(turns):
+            half_copy(j, k, distance).wait_recv()
+            own_load(index).wait()
+            size = half_of(FFH, k)[1]
+            add(half_ref(j, k), half_ref(j, k), spare.at[index % 2, :, :, :, pl.ds(0, size)])
+            one = summed_copy(j, k, distance)
+            one.start()
+            pending.append(one)
+            if index < 4:
+                own_load(index + 2).start()
+
+    def third():
+        for j in range(3):
+            slab_load(j).wait()
+            for k in range(2):
+                distance = (1, -1)[k]
+                other_copy(j, k, distance).wait_recv()
+                summed_copy(j, k, distance).wait_recv()
+            add(slab.at[j], slab.at[j], got_whole.at[j, 0], got_whole.at[j, 1])
+
+    def view(chips, j, part):
+        rest = tuple(index for axis, index in zip("xyz", chips) if axis != back_axis(j, 0))
+        cols = slice(None) if part is None else pl.ds(*half_of(FFH, part))
+        return slab.at[(j,) + rest + (slice(None), cols)]
+
+    inner = scatter_stages(
+        view, inner_halves, inner_wholes, place, ss, rs, final, begin=1
+    )
+
+    def finish():
+        for one in pending:
+            one.wait_send()
+        inner[-1]()
+
+    return [first, second, third] + inner[:-1] + [finish]
 
 
 def weight_view(ref, thirds=THIRDS):
@@ -255,107 +371,12 @@
     )
 
 
-def scatter_tokens_kernel(terms, out, buf, h0, h1, h2, w0, w1, w2, lsem, ss, rs):
-    place = position()
-    meet(place)
-    load = pltpu.make_async_copy(terms, buf, lsem)
-    load.start()
-    load.wait()
-    halves = [lambda j, k, ref=ref: ref.at[j, k] for ref in (h0, h1, h2)]
-    wholes = [lambda j, k, part, ref=ref: ref.at[j, k] for ref in (w0, w1, w2)]
-
-    def final(j, mine, left, right):
-        out[j] = (
-            mine[...].astype(jnp.float32)
-            + left[...].astype(jnp.float32)
-            + right[...].astype(jnp.float32)
-        )
-
-    for stage in scatter_stages(
-        token_view(buf), halves, wholes, place, ss, rs, None, final
-    ):
-        stage()
-
-
-def scatter_tokens(terms):
-    kv = jnp.bfloat16
-    return pl.pallas_call(
-        scatter_tokens_kernel,
-        out_shape=shape((MB, T, 128), jnp.float32),
-        in_specs=[ANY],
-        out_specs=VMEM,
-        scratch_shapes=[
-            pltpu.VMEM((4, 4, 4, MB, T, 128), kv),
-            pltpu.VMEM((3, 2, 4, 4, T // 2, 128), kv),
-            pltpu.VMEM((3, 2, 4, T // 2, 128), kv),
-            pltpu.VMEM((3, 2, T // 2, 128), kv),
-            pltpu.VMEM((3, 2, 4, 4, T, 128), kv),
-            pltpu.VMEM((3, 2, 4, T, 128), kv),
-            pltpu.VMEM((3, 2, T, 128), kv),
-            DMA,
-            DMA((3, 3, 4)),
-            DMA((3, 3, 4)),
-        ],
-        compiler_params=params(2),
-        name="scatter_key_value_grads",
-    )(terms)
-
-
 def pair_mask(base, bounds):
     keys = base + lax.broadcasted_iota(jnp.int32, (KB, 128), 0)
     start, end, own = bounds[0:1, :], bounds[1:2, :], bounds[2:3, :]
     allowed = ((keys >= start) & (keys < end)) | (keys == own)
     bias = jnp.where(allowed, 0.0, MASKED)
     return jnp.concatenate([bias] * 4, axis=1)
-
-
-def attend_back_kernel(blocks, qt, dot_, kv, bounds, out, lse, dqt, dkv):
-    batch = pl.program_id(0)
-    queries, grads = qt[0], dot_[0]
-    log_total = lse[0, 0:1, :]
-    inner = jnp.sum(out[0] * grads[64:, :].astype(jnp.float32), axis=0, keepdims=True)
-    dkv[...] = jnp.zeros_like(dkv)
-
-    def step(index, total):
-        chips = pl.ds(index * (KB // T), KB // T)
-        rows = kv[chips, 0].reshape(KB, 128)
-        scores = nn(rows, queries) + pair_mask(index * KB, bounds[0])
-        probs = jnp.exp(scores - log_total)
-        slopes = (probs * (nn(rows, grads) - inner)).astype(jnp.bfloat16)
-        both = nt(slopes, queries) + nt(probs.astype(jnp.bfloat16), grads)
-        dkv[chips, 0] = both.astype(jnp.bfloat16).reshape(KB // T, T, 128)
-        return total + tn(rows, slopes)
-
-    total = lax.fori_loop(
-        blocks[batch, 0], blocks[batch, 1], step, jnp.zeros((128, QS), jnp.float32)
-    )
-    dqt[0] = total[:64, :] * (1.0 / 8.0)
-
-
-def attend_back(blocks, qt, dot_, kv, bounds, out, lse):
-    return pl.pallas_call(
-        attend_back_kernel,
-        grid=(MB,),
-        out_shape=(
-            shape((MB, 64, QS), jnp.float32),
-            shape((64, MB, T, 128), jnp.bfloat16),
-        ),
-        in_specs=[
-            SMEM,
-            pl.BlockSpec((1, 128, QS), lambda m: (m, 0, 0)),
-            pl.BlockSpec((1, 128, QS), lambda m: (m, 0, 0)),
-            pl.BlockSpec((64, 1, T, 128), lambda m: (0, m, 0, 0)),
-            pl.BlockSpec((1, 8, 128), lambda m: (m, 0, 0)),
-            pl.BlockSpec((1, 64, QS), lambda m: (m, 0, 0)),
-            pl.BlockSpec((1, 8, QS), lambda m: (m, 0, 0)),
-        ],
-        out_specs=(
-            pl.BlockSpec((1, 64, QS), lambda m: (m, 0, 0)),
-            pl.BlockSpec((64, 1, T, 128), lambda m: (0, m, 0, 0)),
-        ),
-        compiler_params=params(),
-        name="attention_back",
-    )(blocks, qt, dot_, kv, bounds, out, lse)
 
 
 def mean_of(values):
@@ -718,209 +739,286 @@
     return back, jnp.sum(grad * rows * scale, axis=0, keepdims=True)
 
 
-def mlp_back_kernel(
-    layer, dout, gu, mid, gains, wa, wm, dgu, dmid, da, datt, gain, wbuf, mine, theirs, wsem, xs, xr
-):
-    meet(position(), core=True, chips=False)
-
-    def load(index, start, size):
-        cols = pl.ds(start, size)
-        return pltpu.make_async_copy(
-            wm.at[layer, :, :, cols], wbuf.at[:, :, cols], wsem.at[index]
-        )
-
-    loads = []
-    for index, (start, size) in enumerate(FF_CHUNKS):
-        for part in (2, 0, 1):
-            loads.append(load(len(loads), part * FFH + start, size))
-    loads.append(
-        pltpu.make_async_copy(
-            wa.at[layer, :, :, pl.ds(QS, QS)], wbuf.at[:, :, pl.ds(CM, QS)], wsem.at[15]
-        )
-    )
-    for one in loads:
-        one.start()
-
-    def weights(start, size):
-        return wbuf[:, :, pl.ds(start, size)].reshape(DP, size)
-
-    grad_in = dout[...].astype(jnp.float32)
-    grad_low = grad_in.astype(jnp.bfloat16)
-    total = jnp.zeros((R, DP), jnp.float32)
-    for index, (start, size) in enumerate(FF_CHUNKS):
-        for part in range(3):
-            loads[3 * index + part].wait()
-        grad_hidden = nn(grad_low, weights(C_DOWN + start, size))
-        gate = gu[:, pl.ds(start, size)]
-        up = gu[:, pl.ds(C_UP + start, size)]
-        sigma = jax.nn.sigmoid(gate)
-        grad_gate = grad_hidden * up * sigma * (1.0 + gate * (1.0 - sigma))
-        grad_gate = grad_gate.astype(jnp.bfloat16)
-        grad_up = (grad_hidden * gate * sigma).astype(jnp.bfloat16)
-        dgu[:, pl.ds(start, size)] = grad_gate
-        dgu[:, pl.ds(C_UP + start, size)] = grad_up
-        total = total + nt(grad_gate, weights(start, size))
-        total = total + nt(grad_up, weights(C_UP + start, size))
-    mine[...] = total
-    one = send(mine, theirs, xs, xr, other_core())
-    one.start()
-    one.wait()
-    back, gain_row = norm_back(mine[...] + theirs[...], mid[...], gains[3:4, :])
-    gain[...] = jnp.broadcast_to(gain_row, (8, DP))
-    middle = grad_in + back
-    dmid[...] = middle
-    low = middle.astype(jnp.bfloat16)
-    da[...] = low
-    loads[15].wait()
-    lane = lax.broadcasted_iota(jnp.int32, (R, QS), 1)
-    datt[...] = jnp.where(lane < 64, 0.0, nn(low, weights(CM, QS))).astype(jnp.bfloat16)
-
-
-def mlp_back(layer, dout, gu, mid, gains, wa, wm):
-    return pl.pallas_call(
-        functools.partial(mlp_back_kernel, layer),
-        out_shape=(
-            shape((R, 2 * FFH), jnp.bfloat16),
-            shape((R, DP), jnp.float32),
-            shape((R, DP), jnp.bfloat16),
-            shape((R, QS), jnp.bfloat16),
-            shape((8, DP), jnp.float32),
-        ),
-        in_specs=[VMEM] * 4 + [ANY] * 2,
-        out_specs=(VMEM,) * 5,
-        scratch_shapes=[
-            pltpu.VMEM((64, 16, CM + QS), jnp.bfloat16),
-            pltpu.VMEM((R, DP), jnp.float32),
-            pltpu.VMEM((R, DP), jnp.float32),
-            DMA((16,)),
-            DMA,
-            DMA,
-        ],
-        compiler_params=params(5 + layer),
-        name="mlp_back",
-    )(dout, gu, mid, gains, wa, wm)
-
-
-def project_back_kernel(
-    layer, dqk, dv, x, dmid, gains, cosine, sine, w, dx, low, vlow, gain, bias,
-    wbuf, mine, theirs, wsem, xs, xr,
-):
-    load = pltpu.make_async_copy(w.at[layer], wbuf, wsem)
-    load.start()
-    meet(position(), core=True, chips=False)
-    turned = turn(dqk[...], tiled(cosine[...]), -tiled(sine[...])).astype(jnp.bfloat16)
-    low[...] = turned
-    values = dv[...].astype(jnp.bfloat16)
-    vlow[...] = values
-    bias[:, :QS] = jnp.broadcast_to(
-        jnp.sum(turned.astype(jnp.float32), axis=0, keepdims=True), (8, QS)
-    )
-    bias[:, QS:] = jnp.broadcast_to(
-        jnp.sum(values.astype(jnp.float32), axis=0, keepdims=True), (8, QS)
-    )
-    load.wait()
-    mine[...] = nt(turned, wbuf[:, :, :QS].reshape(DP, QS)) + nt(
-        values, wbuf[:, :, QS:].reshape(DP, QS)
-    )
-    one = send(mine, theirs, xs, xr, other_core())
-    one.start()
-    one.wait()
-    back, gain_row = norm_back(
-        mine[...] + theirs[...], x[...].astype(jnp.float32), gains[2:3, :]
-    )
-    gain[...] = jnp.broadcast_to(gain_row, (8, DP))
-    dx[...] = (dmid[...] + back).astype(jnp.bfloat16)
-
-
-def project_back(layer, dqk, dv, x, dmid, gains, cosine, sine, w):
-    return pl.pallas_call(
-        functools.partial(project_back_kernel, layer),
-        out_shape=(
-            shape((R, DP), jnp.bfloat16),
-            shape((R, QS), jnp.bfloat16),
-            shape((R, QS), jnp.bfloat16),
-            shape((8, DP), jnp.float32),
-            shape((8, 2 * QS), jnp.float32),
-        ),
-        in_specs=[VMEM] * 7 + [ANY],
-        out_specs=(VMEM,) * 5,
-        scratch_shapes=[
-            pltpu.VMEM((64, 16, 2 * QS), jnp.bfloat16),
-            pltpu.VMEM((R, DP), jnp.float32),
-            pltpu.VMEM((R, DP), jnp.float32),
-            DMA,
-            DMA,
-            DMA,
-        ],
-        compiler_params=params(7 + layer),
-        name="project_back",
-    )(dqk, dv, x, dmid, gains, cosine, sine, w)
-
-
-def weight_grads_kernel(
-    sums, n2, dgu, dm, hid, n1, dqk, dv, da, att, small, out, small_out,
-    g, h0, h1, h2, w0, w1, w2, sbuf, ss, rs, as_, ar,
+SLOT = 256
+FF_SLOTS = tuple((start, min(SLOT, FFH - start)) for start in range(0, FFH, SLOT))
+A_SLOTS = ((0, 3), (3, 3), (6, 2))
+
+
+def slot_view(pool):
+    def view(chips, j, part):
+        lanes = slice(None) if part is None else pl.ds(part * 128, 128)
+        return pool.at[(pl.ds(*A_SLOTS[j]),) + tuple(chips) + (slice(None), lanes)]
+
+    return view
+
+
+def backward_kernel(
+    wa, wm, kv, gu, cot, x0, x1, gains, n1, qt, mixed, lse, att, mid, n2, squares, cosine, sine,
+    bounds,
+    grads, dx, kept, other, small_out,
+    pool, gbuf, n2t, dmt, wat, mine, theirs, dout, dmid, da, dot_, dqk, low, vlow, kvb, own,
+    kh0, kh1, kh2, kw0, kw1, kw2, slab, got_half, got_whole, spare, mh1, mh2, mw1, mw2,
+    ah0, ah1, ah2, aw0, aw1, aw2, outv, sbuf,
+    lsem, psem, gsem, usem, xsem, xrsem, ks, kr, hs, hr, os_, or_, ws, wr, ls, ms, mr, as_, ar,
+    bs, br, fs, fr, credit,
 ):
     place = position()
-    meet(place, far=sums)
-
-    def product(start, size, pairs):
-        for first in range(0, size, 512):
-            wide = min(512, size - first)
-            total = sum(
-                tn(left[...], right[:, first : first + wide]) for left, right in pairs
+    core = lax.axis_index("section")
+    chip = lax.axis_index("dp")
+    meet(place, core=True, far=True)
+    steps = (chip * T + T + KB - 1) // KB
+
+    def heads_load(layer):
+        return pltpu.make_async_copy(wa.at[layer], wat, lsem.at[2 * layer])
+
+    def keys_load(layer):
+        return pltpu.make_async_copy(kv.at[layer], kvb, lsem.at[2 * layer + 1])
+
+    heads_load(1).start()
+    keys_load(1).start()
+    dout[...] = cot[...].astype(jnp.float32)
+    small = [[None] * 4, [None] * 4]
+    stored = {}
+
+    def swap(slot):
+        return send(mine.at[slot], theirs.at[slot], xsem.at[slot], xrsem.at[slot], other_core())
+
+    def back_feed(layer, hooks):
+        def loads(index):
+            start, size = FF_SLOTS[index]
+            slot = index % 2
+            copies = []
+            for part in range(3):
+                copies.append(
+                    pltpu.make_async_copy(
+                        wm.at[layer, :, :, :, :, pl.ds(part * FFH + start, size)],
+                        pool.at[3 * slot + part, :, :, :, :, pl.ds(0, size)],
+                        psem.at[slot, part],
+                    )
+                )
+            for part in range(2):
+                copies.append(
+                    pltpu.make_async_copy(
+                        gu.at[layer, :, pl.ds(part * FFH + start, size)],
+                        gbuf.at[slot, part, :, pl.ds(0, size)],
+                        usem.at[slot, part],
+                    )
+                )
+            return copies
+
+        for index in range(2):
+            for one in loads(index):
+                one.start()
+        grad_in = dout[...]
+        grad_low = grad_in.astype(jnp.bfloat16)
+        n2t[...] = n2[layer].astype(jnp.float32).T.astype(jnp.bfloat16)
+        dmt[...] = grad_low.astype(jnp.float32).T.astype(jnp.bfloat16)
+        mine[0] = jnp.zeros((R, DP), jnp.float32)
+        for index, (start, size) in enumerate(FF_SLOTS):
+            slot = index % 2
+            hooks.get(index, lambda: None)()
+            for one in loads(index):
+                one.wait()
+
+            def weights(part, slot=slot, size=size):
+                return pool[3 * slot + part, :, :, :, :, :size].reshape(DP, size)
+
+            grad_hidden = nn(grad_low, weights(2))
+            gate = gbuf[slot, 0, :, :size]
+            up = gbuf[slot, 1, :, :size]
+            sigma = jax.nn.sigmoid(gate)
+            hidden = (gate * sigma * up).astype(jnp.bfloat16)
+            grad_gate = grad_hidden * up * sigma * (1.0 + gate * (1.0 - sigma))
+            grad_gate = grad_gate.astype(jnp.bfloat16)
+            grad_up = (grad_hidden * gate * sigma).astype(jnp.bfloat16)
+            mine[0] += nt(grad_gate, weights(0)) + nt(grad_up, weights(1))
+            if index + 2 < len(FF_SLOTS):
+                for one in loads(index + 2):
+                    one.start()
+            products = ((n2t, grad_gate), (n2t, grad_up), (dmt, hidden))
+            for part, (left, right) in enumerate(products):
+                held = 6 + 3 * slot + part
+                if held in stored:
+                    stored.pop(held).wait()
+                pool[held, :, :, :, :, :size] = (
+                    nn(left[...], right).astype(jnp.bfloat16).reshape(4, 4, 4, 16, size)
+                )
+                stored[held] = pltpu.make_async_copy(
+                    pool.at[held, :, :, :, :, pl.ds(0, size)],
+                    grads.at[layer, :, :, :, :, pl.ds(part * FFH + start, size)],
+                    gsem.at[slot, part],
+                )
+                stored[held].start()
+        one = swap(0)
+        one.start()
+        one.wait()
+        back, gain_row = norm_back(mine[0] + theirs[0], mid[layer], gains[layer, 3:4, :])
+        small[layer][1] = gain_row
+        middle = grad_in + back
+        dmid[...] = middle
+        middle_low = middle.astype(jnp.bfloat16)
+        da[layer] = middle_low
+        heads_load(layer).wait()
+        turned = nn(middle_low, wat[:, :, :, :, QS:].reshape(DP, QS))
+        turned = without_first_slot(turned.astype(jnp.bfloat16).astype(jnp.float32))
+        for batch in range(MB):
+            columns = to_columns(turned[batch * T : (batch + 1) * T]).astype(jnp.bfloat16)
+            dot_[batch] = jnp.concatenate([jnp.zeros_like(columns), columns], axis=0)
+        for held in list(stored):
+            stored.pop(held).wait()
+
+    def back_attend(layer, batch):
+        if batch == 0:
+            keys_load(layer).wait()
+        queries, slopes_out = qt[layer, batch], dot_[batch]
+        limits = bounds[batch]
+        log_total = lse[layer, batch, 0:1, :]
+        inner = jnp.sum(
+            mixed[layer, batch] * slopes_out[64:, :].astype(jnp.float32), axis=0, keepdims=True
+        )
+
+        def step(index, sums):
+            spot = (index // 2, pl.ds(index % 2 * 2, 2), slice(None), batch)
+            rows = kvb[spot].reshape(KB, 128)
+            scores = nn(rows, queries) + pair_mask(index * KB, limits)
+            probs = jnp.exp(scores - log_total)
+            slopes = (probs * (nn(rows, slopes_out) - inner)).astype(jnp.bfloat16)
+            both = nt(slopes, queries) + nt(probs.astype(jnp.bfloat16), slopes_out)
+            kvb[spot] = both.astype(jnp.bfloat16).reshape(2, 4, T, 128)
+            return sums + tn(rows, slopes)
+
+        sums = lax.fori_loop(0, steps, step, jnp.zeros((128, QS), jnp.float32))
+
+        def clear(index, nothing):
+            kvb[index // 2, pl.ds(index % 2 * 2, 2), :, batch] = jnp.zeros(
+                (2, 4, T, 128), jnp.bfloat16
             )
-            g[:, :, :, :, pl.ds(start + first, wide)] = total.astype(jnp.bfloat16).reshape(
-                4, 4, 4, 16, wide
-            )
-
-    product(0, 2 * FFH, [(n2, dgu)])
-    product(C_DOWN, FFH, [(dm, hid)])
-    product(C_QK, QS, [(n1, dqk)])
-    product(C_VO, QS, [(n1, dv), (da, att)])
-
-    def spot(j, part):
-        size = THIRDS[j][1]
-        if part is None:
-            return pl.ds(0, size)
-        half = size // 256 * 128
-        return pl.ds(0, half) if part == 0 else pl.ds(0, size - half)
-
-    halves = [
-        lambda j, k, ref=ref: ref.at[(j, k) + (slice(None),) * (ref.ndim - 3) + (spot(j, k),)]
-        for ref in (h0, h1, h2)
-    ]
-    wholes = [
-        lambda j, k, part, ref=ref: ref.at[
-            (j, k) + (slice(None),) * (ref.ndim - 3) + (spot(j, None),)
-        ]
-        for ref in (w0, w1, w2)
-    ]
-
-    def final(j, mine, left, right):
-        out[:, pl.ds(*THIRDS[j])] = (
-            mine[...].astype(jnp.float32)
+            return nothing
+
+        lax.fori_loop(steps, SEQ // KB, clear, 0)
+        dqk[pl.ds(batch * T, T), :] = to_rows(sums[:64, :] * 0.125)
+
+    def back_project(layer):
+        key_grads = own[...].reshape(R, 128)
+        whole = jnp.concatenate([key_grads[:, :64], dqk[:, 64:]], axis=1)
+        turned = turn(whole, tiled(cosine[...]), -tiled(sine[...])).astype(jnp.bfloat16)
+        values = jnp.concatenate(
+            [key_grads[:, 64:], jnp.zeros((R, QS - 64), jnp.float32)], axis=1
+        ).astype(jnp.bfloat16)
+        low[layer] = turned
+        vlow[layer] = values
+        small[layer][2] = jnp.concatenate(
+            [
+                jnp.sum(turned.astype(jnp.float32), axis=0, keepdims=True),
+                jnp.sum(values.astype(jnp.float32), axis=0, keepdims=True),
+            ],
+            axis=1,
+        )
+        mine[1] = nt(turned, wat[:, :, :, :, :QS].reshape(DP, QS)) + nt(
+            values, wat[:, :, :, :, QS:].reshape(DP, QS)
+        )
+        one = swap(1)
+        one.start()
+        one.wait()
+        rows = (x0 if layer == 0 else x1)[...].astype(jnp.float32)
+        back, gain_row = norm_back(mine[1] + theirs[1], rows, gains[layer, 2:3, :])
+        small[layer][0] = gain_row
+        small[layer][3] = squares[layer : layer + 1, :]
+        result = (dmid[...] + back).astype(jnp.bfloat16)
+        if layer == 0:
+            dx[...] = result
+        else:
+            dout[...] = result.astype(jnp.float32)
+
+    def heads_products(layer):
+        first = tn(n1[layer], low[layer])
+        second = tn(n1[layer], vlow[layer]) + tn(da[layer], att[layer])
+        for side, product in enumerate((first, second)):
+            for part in range(2):
+                pool[4 * layer + 2 * side + part] = (
+                    product[:, part * SLOT : (part + 1) * SLOT]
+                    .astype(jnp.bfloat16)
+                    .reshape(4, 4, 4, 16, SLOT)
+                )
+
+    def key_final(j, mine_, left, right):
+        own[j] = (
+            mine_[...].astype(jnp.float32)
             + left[...].astype(jnp.float32)
             + right[...].astype(jnp.float32)
         )
 
-    stages = scatter_stages(weight_view(g), halves, wholes, place, ss, rs, None, final)
-    if sums:
-        sbuf[0] = small[...]
-        for phase, axis in enumerate("xyz"):
-            copies = [
-                send(
-                    sbuf.at[4 * phase],
-                    sbuf.at[4 * phase + k],
-                    as_.at[phase, k - 1],
-                    ar.at[phase, k - 1],
-                    chip_id(moved(place, axis, distance)),
-                )
-                for k, distance in ((1, 1), (2, -1), (3, 2))
-            ]
+    key_halves = [lambda j, k, ref=ref: ref.at[j, k] for ref in (kh0, kh1, kh2)]
+    key_wholes = [lambda j, k, ref=ref: ref.at[j, k] for ref in (kw0, kw1, kw2)]
+    keys = [
+        scatter_stages(
+            token_view(kvb), key_halves, key_wholes, place, ks.at[layer], kr.at[layer], key_final
+        )
+        for layer in range(2)
+    ]
+
+    def feed_final(layer):
+        def final(j, mine_, left, right):
+            outv[layer, :, pl.ds(j * FFH, FFH)] = (
+                mine_[...].astype(jnp.float32)
+                + left[...].astype(jnp.float32)
+                + right[...].astype(jnp.float32)
+            )
+
+        return final
+
+    def lanes(ref, size):
+        return lambda j, k: ref.at[
+            (j, k) + (slice(None),) * (len(ref.shape) - 3) + (pl.ds(0, size(k)),)
+        ]
+
+    inner_halves = [None] + [lanes(ref, lambda k: half_of(FFH, k)[1]) for ref in (mh1, mh2)]
+    inner_wholes = [None] + [lanes(ref, lambda k: FFH) for ref in (mw1, mw2)]
+    feed = [
+        scatter_large_stages(
+            weight_view(grads.at[layer], M_THIRDS), slab, got_half, got_whole, spare,
+            inner_halves, inner_wholes, place, hs.at[layer], hr.at[layer], os_.at[layer],
+            or_.at[layer], ws.at[layer], wr.at[layer], ls.at[layer], ms.at[layer], mr.at[layer],
+            feed_final(layer),
+        )
+        for layer in range(2)
+    ]
+
+    def slots(ref):
+        return lambda j, k: ref.at[j, k, pl.ds(0, A_SLOTS[j][1])]
+
+    def heads_final(j, mine_, left, right):
+        begin, count = A_SLOTS[j]
+        for index in range(count):
+            layer, spot = divmod(begin + index, 4)
+            outv[layer, :, pl.ds(CM + spot * SLOT, SLOT)] = (
+                mine_[index].astype(jnp.float32)
+                + left[index].astype(jnp.float32)
+                + right[index].astype(jnp.float32)
+            )
+
+    heads = scatter_stages(
+        slot_view(pool), [slots(ref) for ref in (ah0, ah1, ah2)],
+        [slots(ref) for ref in (aw0, aw1, aw2)], place, as_, ar, heads_final,
+    )
+
+    def total_small(phase, axis):
+        copies = [
+            send(
+                sbuf.at[4 * phase],
+                sbuf.at[4 * phase + k],
+                bs.at[phase, k - 1],
+                br.at[phase, k - 1],
+                chip_id(moved(place, axis, distance)),
+            )
+            for k, distance in ((1, 1), (2, -1), (3, 2))
+        ]
+
+        def begin():
             for one in copies:
                 one.start()
-            stages[phase]()
+
+        def end():
             for one in copies:
                 one.wait()
             total = (
@@ -930,39 +1028,165 @@
                 sbuf[4 * phase + 4] = total
             else:
                 small_out[...] = total
-        stages = stages[3:]
-    else:
-        small_out[...] = small[...]
-    for stage in stages:
+
+        return begin, end
+
+    back_feed(1, {})
+    feed[1][0]()
+    for batch in range(MB):
+        back_attend(1, batch)
+    for stage in keys[1][:8]:
         stage()
-
-
-def weight_grads(sums, n2, dgu, dm, hid, n1, dqk, dv, da, att, small):
-    kind = jnp.bfloat16
-    wide = THIRDS[0][1]
-    half = THIRDS[0][1] // 2
+    feed[1][1]()
+    keys[1][8]()
+    keys[1][9]()
+    keys_load(0).start()
+    back_project(1)
+    heads_load(0).start()
+    back_feed(
+        0,
+        {
+            3: lambda: (feed[1][2](), feed[1][3]()),
+            5: lambda: feed[1][4](),
+            7: lambda: (feed[1][5](), feed[1][6]()),
+            9: lambda: feed[1][7](),
+        },
+    )
+    feed[1][8]()
+    feed[1][9]()
+    for axis in "xyz":
+        for distance in (1, -1):
+            pl.semaphore_signal(
+                credit, inc=1, device_id=chip_id(moved(place, axis, distance)), device_id_type=MESH
+            )
+    pl.semaphore_wait(credit, 6)
+    feed[0][0]()
+    for batch in range(MB):
+        back_attend(0, batch)
+    heads_products(1)
+    for stage in keys[0][:8]:
+        stage()
+    feed[0][1]()
+    keys[0][8]()
+    keys[0][9]()
+    back_project(0)
+    heads_products(0)
+    sbuf[0] = jnp.concatenate(small[0] + small[1], axis=0)
+    sums = [total_small(phase, axis) for phase, axis in enumerate("xyz")]
+    sums[0][0]()
+    heads[0]()
+    feed[0][2]()
+    feed[0][3]()
+    sums[0][1]()
+    sums[1][0]()
+    heads[1]()
+    feed[0][4]()
+    heads[2]()
+    heads[3]()
+    sums[1][1]()
+    sums[2][0]()
+    feed[0][5]()
+    feed[0][6]()
+    heads[4]()
+    heads[5]()
+    heads[6]()
+    sums[2][1]()
+    feed[0][7]()
+    heads[7]()
+    feed[0][8]()
+    heads[8]()
+    for layer in range(2):
+        outv[layer, 14:15, pl.ds(CM, CA)] = small_out[4 * layer + 2 : 4 * layer + 3, :]
+    trade = send(outv.at[1 - core], other, fs, fr, other_core())
+    trade.start()
+    kept[...] = outv[core]
+    feed[0][9]()
+    heads[9]()
+    trade.wait()
+
+
+def backward(*arrays):
+    low, full = jnp.bfloat16, jnp.float32
+    half = FFH - FFH // 256 * 128
+
+    def ring(last, phase, kind=low):
+        return pltpu.VMEM((3, 2) + (4,) * (2 - phase) + last, kind)
+
     return pl.pallas_call(
-        functools.partial(weight_grads_kernel, sums),
-        out_shape=(shape((16, C), jnp.float32), shape((8, DP), jnp.float32)),
-        in_specs=[VMEM] * 10,
-        out_specs=(VMEM, VMEM),
+        backward_kernel,
+        out_shape=(
+            shape((2, 4, 4, 4, 16, CM), low),
+            shape((R, DP), low),
+            shape((16, C), full),
+            shape((16, C), full),
+            shape((8, DP), full),
+        ),
+        in_specs=[ANY] * 4 + [VMEM] * 15,
+        out_specs=(ANY,) + (VMEM,) * 4,
         scratch_shapes=[
-            pltpu.VMEM((4, 4, 4, 16, C), kind),
-            pltpu.VMEM((3, 2, 4, 4, 16, half), kind),
-            pltpu.VMEM((3, 2, 4, 16, half), kind),
-            pltpu.VMEM((3, 2, 16, half), kind),
-            pltpu.VMEM((3, 2, 4, 4, 16, wide), kind),
-            pltpu.VMEM((3, 2, 4, 16, wide), kind),
-            pltpu.VMEM((3, 2, 16, wide), kind),
-            pltpu.VMEM((12, 8, DP), jnp.float32),
+            pltpu.VMEM((12, 4, 4, 4, 16, SLOT), low),
+            pltpu.VMEM((2, 2, R, SLOT), full),
+            pltpu.VMEM((DP, R), low),
+            pltpu.VMEM((DP, R), low),
+            pltpu.VMEM((4, 4, 4, 16, CA), low),
+            pltpu.VMEM((2, R, DP), full),
+            pltpu.VMEM((2, R, DP), full),
+            pltpu.VMEM((R, DP), full),
+            pltpu.VMEM((R, DP), full),
+            pltpu.VMEM((2, R, DP), low),
+            pltpu.VMEM((MB, 128, QS), low),
+            pltpu.VMEM((R, QS), full),
+            pltpu.VMEM((2, R, QS), low),
+            pltpu.VMEM((2, R, QS), low),
+            pltpu.VMEM((4, 4, 4, MB, T, 128), low),
+            pltpu.VMEM((MB, T, 128), full),
+        ]
+        + [ring((T // 2, 128), phase) for phase in range(3)]
+        + [ring((T, 128), phase) for phase in range(3)]
+        + [
+            pltpu.VMEM((3, 4, 4, 16, FFH), low),
+            pltpu.VMEM((3, 2, 4, 4, 16, half), low),
+            pltpu.VMEM((3, 2, 4, 4, 16, FFH), low),
+            pltpu.VMEM((2, 4, 4, 16, half), low),
+        ]
+        + [ring((16, half), phase) for phase in (1, 2)]
+        + [ring((16, FFH), phase) for phase in (1, 2)]
+        + [
+            pltpu.VMEM((3, 2, 3) + (4,) * (2 - phase) + (16, wide), low)
+            for wide in (128, SLOT)
+            for phase in range(3)
+        ]
+        + [
+            pltpu.VMEM((2, 16, C), full),
+            pltpu.VMEM((12, 8, DP), full),
+            DMA((4,)),
+            DMA((2, 3)),
+            DMA((2, 3)),
+            DMA((2, 2)),
+            DMA((2,)),
+            DMA((2,)),
+            DMA((2, 3, 3, 4)),
+            DMA((2, 3, 3, 4)),
+            DMA((2, 3, 2)),
+            DMA((2, 3, 2)),
+            DMA((2, 3, 2)),
+            DMA((2, 3, 2)),
+            DMA((2, 3, 2)),
+            DMA((2, 3, 2)),
+            DMA((2, 9)),
+            DMA((2, 3, 3, 4)),
+            DMA((2, 3, 3, 4)),
             DMA((3, 3, 4)),
             DMA((3, 3, 4)),
             DMA((3, 3)),
             DMA((3, 3)),
+            DMA,
+            DMA,
+            pltpu.SemaphoreType.REGULAR,
         ],
-        compiler_params=params(9 + int(sums), vmem=60),
-        name="weight_grads",
-    )(n2, dgu, dm, hid, n1, dqk, dv, da, att, small)
+        compiler_params=params(1, vmem=63),
+        name="backward",
+    )(*arrays)
 
 
 def shards(
@@ -1033,9 +1257,6 @@
     finish = jnp.minimum(places[None, :] + 1, lengths[:, None])
     bounds = jnp.stack([starts, finish, jnp.broadcast_to(places[None], (MB, T))], axis=1)
     bounds = jnp.pad(jnp.tile(bounds, (1, 1, 2)), ((0, 0), (0, 5), (0, 0)))
-    last = (chip * T + T + KB - 1) // KB
-    blocks = jnp.stack([starts[:, 0] // KB, jnp.full((MB,), last, jnp.int32)], axis=1)
-
     (
         wa, wm, kv_all, gu_all, ends_all, gains_all, n1_all, qt_all, mixed_all, lse_all, att_all,
         mid_all, n2_all, hid_all, x_all, sq_all,
@@ -1050,66 +1271,14 @@
         sine,
         bounds,
     )
-    wa = wa.reshape(2, 64, 16, CA)
-    wm = wm.reshape(2, 64, 16, CM)
-    kv_all = kv_all.reshape(2, 64, MB, T, 128)
-    final_out = x_all[1]
-    dout = ends_all[1]
-
-    def columns_of(rows):
-        turned = rows.reshape(MB, T, 8, 64).transpose(0, 3, 2, 1)
-        return turned.at[:, :, 0].set(0).reshape(MB, 64, QS)
-
-    def rows_of(columns):
-        return columns.reshape(MB, 64, 8, T).transpose(0, 3, 2, 1).reshape(R, 8, 64)
-
-    grads = [None, None]
-    smalls = [None, None]
-    for layer in (1, 0):
-        gains, n1, kv, qt, mixed, lse, attended, mid, n2, gu, hid, sq = (
-            member[layer]
-            for member in (
-                gains_all, n1_all, kv_all, qt_all, mixed_all, lse_all, att_all, mid_all, n2_all,
-                gu_all, hid_all, sq_all,
-            )
-        )
-        x = x_all[0] if layer == 1 else ends_all[0]
-        dgu, dmid, da, datt, gain_two = mlp_back(layer, dout, gu, mid, gains, wa, wm)
-        dot_ = jnp.pad(columns_of(datt), ((0, 0), (64, 0), (0, 0)))
-        dqt, terms = attend_back(blocks, qt, dot_, kv, bounds, mixed, lse)
-        own = scatter_tokens(terms.reshape(4, 4, 4, MB, T, 128)).reshape(R, 128)
-        dqk = rows_of(dqt).at[:, 0].set(own[:, :64]).reshape(R, QS)
-        dv = jnp.pad(own[:, 64:], ((0, 0), (0, QS - 64)))
-        dx, dqk_low, dv_low, gain_one, bias_sum = project_back(
-            layer, dqk, dv, x, dmid, gains, cosine, sine, wa
-        )
-        valid = lax.dynamic_slice_in_dim(valid_blocks, chip // 2, 1, 1).astype(jnp.float32)
-        squares = jnp.where(valid > 0, sq[:MB, :3], 0.0)
-        smalls[layer] = jnp.stack(
-            [
-                gain_one[0],
-                gain_two[0],
-                bias_sum[0],
-                jnp.pad(squares.reshape(-1), (0, DP - 9)),
-            ]
-        )
-        small = jnp.concatenate(smalls, axis=0) if layer == 0 else jnp.zeros((8, DP), jnp.float32)
-        grads[layer], small_sum = weight_grads(
-            layer == 0, n2, dgu, dout, hid, n1, dqk_low, dv_low, da, attended, small
-        )
-        dout = dx
-
-    def with_bias(layer):
-        return grads[layer].at[14, :QS].set(small_sum[4 * layer + 2, :QS]).at[
-            14, QS : 2 * QS
-        ].set(small_sum[4 * layer + 2, QS:])
-
-    ready = [with_bias(0), with_bias(1)]
-    here = jnp.where(core == 0, ready[0], ready[1])
-    away = lax.ppermute(jnp.where(core == 0, ready[1], ready[0]), "section", [(0, 1), (1, 0)])
-    lower = jnp.where(core == 0, here, away)
-    upper = jnp.where(core == 0, away, here)
-    sides = (lower, upper)
+    valid = lax.dynamic_slice_in_dim(valid_blocks, chip // 2, 1, 1) > 0
+    squares = jnp.where(valid[None], sq_all[:, :MB, :3], 0.0).reshape(2, 9)
+    squares = jnp.pad(squares, ((0, 6), (0, DP - 9)))
+    _, dx, kept, other, small_sum = backward(
+        wa, wm, kv_all, gu_all, ends_all[1], ends_all[0], x_all[0], gains_all, n1_all, qt_all,
+        mixed_all, lse_all, att_all, mid_all, n2_all, squares, cosine, sine, bounds,
+    )
+    sides = (jnp.where(core == 0, kept, other), jnp.where(core == 0, other, kept))
 
     def column(start, size):
         return [side[:14, start : start + size] for side in sides]
@@ -1120,7 +1289,7 @@
         column(C_QK + 64, 448) + column(C_QK, 64) + column(C_VO, 64), axis=1
     )
     grad_out = jnp.concatenate(column(C_VO + 64, 448), axis=1)
-    bias_rows = [side[14] for side in sides]
+    bias_rows = [side[14, CM:] for side in sides]
     grad_bias = jnp.concatenate(
         [row[64:QS] for row in bias_rows]
         + [row[:64] for row in bias_rows]
@@ -1130,7 +1299,7 @@
     grad_gain = own_small[:2].reshape(2, 64, 16)[:, :, :14].reshape(2, D)
     counts = jnp.sum(valid_blocks, axis=1).astype(jnp.float32) * 128 * D
     rms = jnp.sqrt(own_small[3, :9].reshape(MB, 3) / counts[:, None])
-    ends_out = jnp.where(core == 0, dout, final_out)
+    ends_out = jnp.where(core == 0, dx, x_all[1])
     boundary = nt(ends_out, spread).astype(jnp.bfloat16).reshape(1, MB, T, D)
     return (
         boundary,

time: 617 us -> 487 us (0.79)
  Pallas kernels: 514 us -> 446 us
  local copies, waits for them, and re-layouts: 74.6 us -> 21.6 us
  starting transfers between devices: 10.3 us -> 0 us
    pallas_call x10 -> x1, Pallas kernels: 312 us -> 244 us  [backward(): pl.pallas_call(backward_kernel, out_shape=(shape((2, 4, 4, 4, 16, CM), lo...]
    slice x10 -> x0, local copies, waits for them, and re-layouts: 15.7 us -> none  [the longest x1 8.1 us: shards(): member[layer]]
    scatter x10 -> x0, local copies, waits for them, and re-layouts: 14.5 us -> none  [the longest x4 5.34 us: shards(): dqk = rows_of(dqt).at[:, 0].set(own[:, :64]).reshape(R, QS)]
    squeeze x13 -> x2, local copies, waits for them, and re-layouts: 17.7 us -> 3.82 us  [the longest x1 2.05 us: shards(): ends_all[0]]
    ppermute x1 -> x0, starting transfers between devices: 10.3 us -> none  [shards(): lax.ppermute(jnp.where(core == 0, ready[1], ready[0]), 'section', [(0, 1)...]
    reshape x14 -> x1, local copies, waits for them, and re-layouts: 8.66 us -> 0.08 us  [shards(): squares = jnp.where(valid[None], sq_all[:, :MB, :3], 0.0).reshape(2, 9)]
  transfers between devices with their start and end apart: 1 -> 0, of which waited for: 0 -> 0; matrix products, arithmetic and copies ran while one was open for 1% -> 0% of each run, Pallas kernels for 0% -> 0%
where the time goes in v3:
time: 487 us; the launch traced here: 481 us
  Pallas kernels  446 us (92%)
  local copies, waits for them, and re-layouts  21.6 us (4%)
  other arithmetic  7.16 us (1%)
    pallas_call x1, Pallas kernels, backward(): pl.pallas_call(backward_kernel, out_shape=(shape((2, 4, 4, 4, 16, CM), lo...  244 us
    pallas_call x1, Pallas kernels, forward(): pl.pallas_call(forward_kernel, out_shape=(shape((2, 4, 4, 4, 16, CA), low...  202 us

profile of v3, /device:TPU:1, one launch (start us, length us, event | category | flops | bytes accessed | tf_op | source)
XLA Modules:
  0.0 480.8 jit_solution(16886532010801372144)
XLA Ops:
  0.6 0.0 copy-start
  0.7 1.1 dynamic-slice_bitcast_fusion.2
  1.7 0.9 dynamic-slice_bitcast_fusion
  2.7 0.9 fusion.20
  3.5 0.8 fusion.53
  4.4 0.9 dynamic-slice_bitcast_fusion.7
  5.3 0.9 dynamic-slice_bitcast_fusion.6
  6.1 0.7 fusion.36
  6.9 0.8 constant_dynamic-slice_fusion.3
  7.6 1.3 convert_reduce_fusion
  8.9 0.8 reduce_sum.20
  9.7 0.1 broadcast_minimum_fusion
  9.8 0.0 copy-start.3
  9.9 0.1 tile.32
  9.9 0.6 pad.31.bounds
  10.6 0.8 slice_bitcast_fusion.10
  11.4 0.8 slice_reduce_fusion.1
  12.2 0.1 pad_maximum_fusion.2
  12.3 1.4 fusion.10
  13.7 0.6 fusion.41.small
  14.4 0.1 fusion.46
  14.6 0.1 copy.30
  14.7 0.7 tile.30.sine
  15.4 0.7 copy.32.cosine
  16.1 0.0 copy-done
  16.1 1.7 fusion.8.ends
  17.7 201.8 %forward.1 = (bf16[2,4,4,4,16,1024]{5,4,3,2,1,0:T(8,128)(2,1)}, bf16[2,4,4,4,16,7296]{5,4,3,2,1,0:T(8,128)(2,1)}, bf16[2,4,4,4,3,64,128]{6,5,4,3,2,1,0:T(8,128)(...) custom-call(bf16[16,1024]{1,0:T(8,128)(2,1)} %get-tuple-element.117., ...), custom_call_target="tpu_custom_call" | custom-call | tf_op jit(solution)/shard_map/forward/pallas_call | solution.py:683
  219.5 2.0 slice_bitcast_fusion.1
  221.6 1.8 slice_bitcast_fusion.x1
  223.3 0.0 copy-done.3
  223.3 0.2 fusion.58
  223.5 0.8 slice_select_fusion
  224.3 0.1 reshape.206
  224.4 0.6 pad.32.squares
  225.0 244.2 %backward.1 = (bf16[2,4,4,4,16,7296]{5,4,3,2,1,0:T(8,128)(2,1)}, bf16[192,1024]{1,0:T(8,128)(2,1)}, f32[16,8320]{1,0:T(8,128)}, f32[16,8320]{1,0:T(8,128)}, f32[8,1024]{1,0:T(8,128)}) custom-call(bf16[2,4,4,4,16,1024]{5,4,3,2,1,0:T(8,128)(2,1)} %get-tuple-element.27.wa, bf16[2,4,4,4,16,7296]{5,4,3,2,1,0:T(8,128)(2,1)} %get-tuple-element.28.wm, ...), custom_call_target="tpu_custom_call" | custom-call | tf_op jit(solution)/shard_map/backward/pallas_call | solution.py:1115
  469.2 1.3 broadcast_select_fusion
  470.5 0.0 copy-start.2
  470.5 0.0 copy-start.4
  470.6 0.0 copy-start.1
  470.6 1.0 copy.37
  471.7 1.4 copy.36
  473.0 0.1 fusion.63
  473.1 0.1 fusion.64
  473.2 0.1 maximum_bitcast_fusion.2
  473.3 0.7 copy.35
  474.0 0.1 slice.198
  474.0 0.1 slice.199
  474.1 0.1 concatenate.48
  474.2 0.6 broadcast_in_dim.53
  474.8 0.1 concatenate.47
  474.9 0.7 copy.34
  475.6 0.0 copy-done.2
  475.6 0.0 copy-done.4
  475.6 1.7 fusion.7
  477.3 0.8 constant_dynamic-slice_fusion
  478.1 0.1 reshape.208
  478.2 0.7 broadcast_in_dim_reshape.3
  478.9 0.7 fusion.59
  479.6 0.1 reshape_squeeze.7
  479.7 0.1 divide_sqrt_fusion
  479.8 0.6 copy.38
  480.4 0.0 copy-done.1
  (24 shorter events, 0.3 us)
Async XLA Ops:
  0.6 15.5 %copy-start = (bf16[1,3,64,896]{3,2,1,0:T(8,128)(2,1)S(1)}, bf16[1,3,64,896]{3,2,1,0:T(8,128)(2,1)}, u32[]{:S(2)}) copy-start(bf16[1,3,64,896]{3,2,1,0:T(8,128)(2,1)} %param.9) | copy-start | bytes 1032196
  9.8 213.5 %copy-start.3 = (s32[3,32]{1,0:T(4,128)S(1)}, s32[3,32]{1,0:T(4,128)}, u32[]{:S(2)}) copy-start(s32[3,32]{1,0:T(4,128)} %param.11) | copy-start | bytes 1156
  470.5 5.1 %copy-start.2 = (bf16[2,192,1024]{2,1,0:T(8,128)(2,1)S(1)}, bf16[2,192,1024]{2,1,0:T(8,128)(2,1)}, u32[]{:S(2)}) copy-start(bf16[2,192,1024]{2,1,0:T(8,128)(2,1)} %get-tuple-element.32) | copy-start | bytes 2359300
  470.5 5.1 %copy-start.4 = (bf16[192,1024]{1,0:T(8,128)(2,1)S(1)}, bf16[192,1024]{1,0:T(8,128)(2,1)}, u32[]{:S(2)}) copy-start(bf16[192,1024]{1,0:T(8,128)(2,1)} %get-tuple-element.42) | copy-start | bytes 1179652
  470.6 9.8 %copy-start.1 = (bf16[1,3,64,896]{3,2,1,0:T(8,128)(2,1)S(1)}, bf16[1,3,64,896]{3,2,1,0:T(8,128)(2,1)}, u32[]{:S(2)}) copy-start(bf16[1,3,64,896]{3,2,1,0:T(8,128)(2,1)} %param.9) | copy-start | bytes 1032196

commit v4 on v3

v4 whole, which is shorter than its diff:
```python
import functools
import math

import jax
import jax.numpy as jnp
from jax import lax
from jax.experimental import pallas as pl
from jax.experimental.pallas import tpu as pltpu
from jax.sharding import PartitionSpec as P

MESH = pl.DeviceIdType.MESH
EPS = 1e-06
THETA = 1000000.0
MASKED = -1e30

MB = 3
T = 64
R = MB * T
D = 896
DP = 1024
FFH = 2432
QS = 512
C_UP, C_DOWN, C_QK, C_VO, C = FFH, 2 * FFH, 3 * FFH, 3 * FFH + QS, 3 * FFH + 2 * QS
KB = 1024
SEQ = 4096
MIB = 1024 * 1024

BLOCK = 128

THIRDS = ((0, 22 * 128), (22 * 128, 22 * 128), (44 * 128, 21 * 128))
ORDERS = (("z", "y", "x"), ("y", "x", "z"), ("x", "z", "y"))
CM, CA = 3 * FFH, 2 * QS
M_THIRDS = ((0, FFH), (FFH, FFH), (2 * FFH, FFH))
A_THIRDS = ((0, 384), (384, 384), (768, 256))
FF_CHUNKS = ((0, 512), (512, 512), (1024, 512), (1536, 512), (2048, 384))


def position():
    chip = lax.axis_index("dp")
    return {"x": chip // 16, "y": (chip // 4) % 4, "z": chip % 4}


def moved(place, axis, distance):
    other = dict(place)
    other[axis] = (place[axis] + distance + 4) % 4
    return other


def chip_id(place):
    return {"dp": place["x"] * 16 + place["y"] * 4 + place["z"]}


def other_core():
    return {"section": 1 - lax.axis_index("section")}


def greet(place, core=False, chips=True, far=False):
    barrier = pltpu.get_barrier_semaphore()
    count = 0
    if chips:
        for axis in "xyz":
            for distance in (1, -1, 2) if far else (1, -1):
                pl.semaphore_signal(
                    barrier,
                    inc=1,
                    device_id=chip_id(moved(place, axis, distance)),
                    device_id_type=MESH,
                )
                count += 1
    if core:
        pl.semaphore_signal(barrier, inc=1, device_id=other_core(), device_id_type=MESH)
        count += 1
    return count


def settle(count):
    pl.semaphore_wait(pltpu.get_barrier_semaphore(), count)


def send(src, dst, send_sem, recv_sem, device):
    return pltpu.make_async_remote_copy(
        src, dst, send_sem, recv_sem, device_id=device, device_id_type=MESH
    )


def cube(done, place):
    return tuple(slice(None) if axis in done else place[axis] for axis in "xyz")


DIRECT = ((0, 1), (1, -1), (2, 2))


def gather_stages(view, place, send_sems, recv_sems, direct=(0, 1)):
    pending = []

    def copy(j, phase, k, whose, part, distance):
        ref = view(cube(ORDERS[j][:phase], whose), j, part)
        return send(
            ref,
            ref,
            send_sems.at[j, phase, k],
            recv_sems.at[j, phase, k],
            chip_id(moved(place, ORDERS[j][phase], distance)),
        )

    def first(phase):
        for j in range(3):
            for k, distance in DIRECT if phase in direct else DIRECT[:2]:
                one = copy(j, phase, k, place, None, distance)
                one.start()
                pending.append(one)

    def second(phase):
        if phase in direct:
            return
        for j in range(3):
            for k, distance in DIRECT[:2]:
                whose = moved(place, ORDERS[j][phase], -distance)
                copy(j, phase, k, whose, None, distance).wait_recv()
                one = copy(j, phase, 2 + k, whose, k, distance)
                one.start()
                pending.append(one)

    def third(phase):
        for j in range(3):
            if phase in direct:
                for k, distance in DIRECT:
                    whose = moved(place, ORDERS[j][phase], -distance)
                    copy(j, phase, k, whose, None, distance).wait_recv()
            else:
                for k, distance in DIRECT[:2]:
                    whose = moved(place, ORDERS[j][phase], 2)
                    copy(j, phase, 2 + k, whose, k, distance).wait_recv()

    def finish():
        for one in pending:
            one.wait_send()

    stages = []
    for phase in range(3):
        stages.append(functools.partial(first, phase))
        stages.append(functools.partial(second, phase))
        stages.append(functools.partial(third, phase))
    stages.append(finish)
    return stages


PARTS = (
    ((0, 256), (256, 256), (512, 256), (768, 384)),
    ((1152, 256), (1408, 256), (1664, 384), (2048, 384)),
)
ROUNDS = 4
TURNS = tuple((j, k, (1, -1)[k]) for j in range(3) for k in range(2))


class LargeGather:
    def __init__(self, ref, place, send_sems, recv_sems, part_sems, pass_sems):
        self.ref, self.place = ref, place
        self.part_sems, self.pass_sems = part_sems, pass_sems
        stages = gather_stages(
            weight_view(ref, M_THIRDS), place, send_sems, recv_sems, direct=(0,)
        )
        self.phases, self.done = stages[:6], stages[9]
        self.pending = []

    def slab(self, j, whose, half, r):
        start, size = PARTS[half][r]
        chips = cube(ORDERS[j][:2], whose)
        return self.ref.at[chips + (slice(None), pl.ds(j * FFH + start, size))]

    def whose(self, j, distance):
        return moved(self.place, ORDERS[j][2], distance)

    def part(self, j, k, distance, half, r, whose):
        ref = self.slab(j, whose, half, r)
        sems = [side.at[j, k, half, r] for side in self.part_sems]
        return send(ref, ref, *sems, chip_id(self.whose(j, distance)))

    def passed(self, j, k, distance, r, whose):
        ref = self.slab(j, whose, k, r)
        sems = [side.at[j, k, r] for side in self.pass_sems]
        return send(ref, ref, *sems, chip_id(self.whose(j, distance)))

    def start(self, one):
        one.start()
        self.pending.append(one)

    def ahead(self, r):
        for j, k, distance in TURNS:
            self.start(self.part(j, k, distance, k, r, self.place))

    def rest(self, r):
        for j, k, distance in TURNS:
            self.start(self.part(j, k, distance, 1 - k, r, self.place))

    def pass_on(self, r):
        for j, k, distance in TURNS:
            back = self.whose(j, -distance)
            self.part(j, k, distance, k, r, back).wait_recv()
            self.start(self.passed(j, k, distance, r, back))

    def last(self):
        for j, k, distance in TURNS:
            for r in range(ROUNDS):
                self.part(j, k, distance, 1 - k, r, self.whose(j, -distance)).wait_recv()
                self.passed(j, k, distance, r, self.whose(j, 2)).wait_recv()

    def finish(self):
        self.done()
        for one in self.pending:
            one.wait_send()


def scatter_stages(
    view, halves, wholes, place, send_sems, recv_sems, final, begin=0, direct=(1, 2)
):
    pending = []

    def half_copy(j, phase, k, distance):
        far = moved(place, back_axis(j, phase), 2)
        return send(
            view(back_chips(j, phase, far), j, k),
            halves[phase](j, k),
            send_sems.at[j, phase, k],
            recv_sems.at[j, phase, k],
            chip_id(moved(place, back_axis(j, phase), distance)),
        )

    def whole_copy(j, phase, k, distance):
        near = moved(place, back_axis(j, phase), distance)
        slot = k if phase in direct else 2 + k
        return send(
            view(back_chips(j, phase, near), j, None),
            wholes[phase](j, k),
            send_sems.at[j, phase, slot],
            recv_sems.at[j, phase, slot],
            chip_id(near),
        )

    def first(phase):
        for j in range(3):
            for k, distance in DIRECT if phase in direct else DIRECT[:2]:
                one = (whole_copy if phase in direct else half_copy)(j, phase, k, distance)
                one.start()
                pending.append(one)

    def second(phase):
        if phase in direct:
            return
        for j in range(3):
            for k, distance in DIRECT[:2]:
                half_copy(j, phase, k, distance).wait_recv()
                near = moved(place, back_axis(j, phase), distance)
                mine = view(back_chips(j, phase, near), j, k)
                add(mine, mine, halves[phase](j, k))
                one = whole_copy(j, phase, k, distance)
                one.start()
                pending.append(one)

    def third(phase):
        turns = DIRECT if phase in direct else DIRECT[:2]
        for j in range(3):
            for k, distance in turns:
                whole_copy(j, phase, k, distance).wait_recv()
            mine = view(back_chips(j, phase, place), j, None)
            terms = [wholes[phase](j, k) for k, distance in turns]
            if phase < 2:
                add(mine, mine, *terms)
            else:
                final(j, mine, *terms)

    def finish():
        for one in pending:
            one.wait_send()

    stages = []
    for phase in range(begin, 3):
        stages.append(functools.partial(first, phase))
        stages.append(functools.partial(second, phase))
        stages.append(functools.partial(third, phase))
    stages.append(finish)
    return stages


def back_axis(j, phase):
    return ORDERS[j][2 - phase]


def back_chips(j, phase, whose):
    return cube(ORDERS[j][: 2 - phase], whose)


def add(dst, *terms):
    dst[...] = sum(term[...].astype(jnp.float32) for term in terms).astype(dst.dtype)


def half_of(size, part):
    half = size // 256 * 128
    return (0, half) if part == 0 else (half, size - half)


class LargeScatter:
    def __init__(
        self, source, slab, got_half, got_whole, spare, inner_halves, inner_wholes, place,
        half_sems, rest_sems, pass_sems, load_sems, send_sems, recv_sems, final,
    ):
        self.source, self.slab, self.place = source, slab, place
        self.got_half, self.got_whole, self.spare = got_half, got_whole, spare
        self.half_sems, self.rest_sems, self.pass_sems = half_sems, rest_sems, pass_sems
        self.load_sems = load_sems
        self.pending = []

        def view(chips, j, part):
            rest = tuple(index for axis, index in zip("xyz", chips) if axis != back_axis(j, 0))
            cols = slice(None) if part is None else pl.ds(*half_of(FFH, part))
            return slab.at[(j,) + rest + (slice(None), cols)]

        stages = scatter_stages(
            view, inner_halves, inner_wholes, place, send_sems, recv_sems, final, begin=1, direct=(2,)
        )
        self.phases, self.done = stages[:-1], stages[-1]

    def terms(self, j, whose, cols):
        chips = back_chips(j, 0, whose)
        return self.source.at[chips + (slice(None), pl.ds(j * FFH + cols[0], cols[1]))]

    def near(self, j, distance):
        return moved(self.place, back_axis(j, 0), distance)

    def half_ref(self, j, k, r):
        start, size = PARTS[k][r]
        return self.got_half.at[j, k, :, :, :, pl.ds(start - PARTS[k][0][0], size)]

    def copy(self, src, dst, sems, j, k, distance, r):
        return send(
            src, dst, sems[0].at[j, k, r], sems[1].at[j, k, r], chip_id(self.near(j, distance))
        )

    def half_copy(self, j, k, distance, r):
        src = self.terms(j, self.near(j, 2), PARTS[k][r])
        return self.copy(src, self.half_ref(j, k, r), self.half_sems, j, k, distance, r)

    def rest_copy(self, j, k, distance, r):
        cols = PARTS[1 - k][r]
        src = self.terms(j, self.near(j, distance), cols)
        dst = self.got_whole.at[j, k, :, :, :, pl.ds(*cols)]
        return self.copy(src, dst, self.rest_sems, j, k, distance, r)

    def pass_copy(self, j, k, distance, r):
        dst = self.got_whole.at[j, k, :, :, :, pl.ds(*PARTS[k][r])]
        return self.copy(self.half_ref(j, k, r), dst, self.pass_sems, j, k, distance, r)

    def own_load(self, j, k, distance, r):
        return pltpu.make_async_copy(
            self.terms(j, self.near(j, distance), PARTS[k][r]),
            self.spare.at[j, k, :, :, :, pl.ds(0, PARTS[k][r][1])],
            self.load_sems.at[2 * j + k],
        )

    def slab_load(self, j):
        return pltpu.make_async_copy(
            self.terms(j, self.place, (0, FFH)), self.slab.at[j], self.load_sems.at[6 + j]
        )

    def start(self, one):
        one.start()
        self.pending.append(one)

    def ahead(self, r):
        for j, k, distance in TURNS:
            self.start(self.half_copy(j, k, distance, r))
        if r == 0:
            for j, k, distance in TURNS:
                self.own_load(j, k, distance, 0).start()
            for j in range(3):
                self.slab_load(j).start()

    def rest(self, r):
        for j, k, distance in TURNS:
            self.start(self.rest_copy(j, k, distance, r))

    def pass_on(self, r):
        for j, k, distance in TURNS:
            self.half_copy(j, k, distance, r).wait_recv()
            self.own_load(j, k, distance, r).wait()
            own = self.spare.at[j, k, :, :, :, pl.ds(0, PARTS[k][r][1])]
            add(self.half_ref(j, k, r), self.half_ref(j, k, r), own)
            self.start(self.pass_copy(j, k, distance, r))
            if r + 1 < ROUNDS:
                self.own_load(j, k, distance, r + 1).start()

    def third(self):
        for j in range(3):
            self.slab_load(j).wait()
            for k in range(2):
                for r in range(ROUNDS):
                    self.rest_copy(j, k, (1, -1)[k], r).wait_recv()
                    self.pass_copy(j, k, (1, -1)[k], r).wait_recv()
            add(self.slab.at[j], self.slab.at[j], self.got_whole.at[j, 0], self.got_whole.at[j, 1])

    def finish(self):
        self.done()
        for one in self.pending:
            one.wait_send()


def weight_view(ref, thirds=THIRDS):
    def view(chips, j, part):
        start, size = thirds[j]
        if part is not None:
            half = size // 256 * 128
            start, size = (start, half) if part == 0 else (start + half, size - half)
        return ref.at[tuple(chips) + (slice(None), pl.ds(start, size))]

    return view


def token_view(ref):
    def view(chips, j, part):
        rows = slice(None) if part is None else pl.ds(part * 32, 32)
        return ref.at[tuple(chips) + (j, rows, slice(None))]

    return view


def params(collective_id=None, vmem=56):
    if collective_id is None:
        return pltpu.CompilerParams(vmem_limit_bytes=vmem * MIB)
    return pltpu.CompilerParams(
        collective_id=collective_id, has_side_effects=True, vmem_limit_bytes=vmem * MIB
    )


ANY = pl.BlockSpec(memory_space=pl.ANY)
VMEM = pl.BlockSpec(memory_space=pltpu.VMEM)
SMEM = pl.BlockSpec(memory_space=pltpu.SMEM)
DMA = pltpu.SemaphoreType.DMA


def shape(dims, dtype):
    return jax.ShapeDtypeStruct(dims, dtype)


def nn(left, right):
    return jnp.dot(left, right, preferred_element_type=jnp.float32)


def nt(left, right):
    return lax.dot_general(
        left, right, (((1,), (1,)), ((), ())), preferred_element_type=jnp.float32
    )


def tn(left, right):
    return lax.dot_general(
        left, right, (((0,), (0,)), ((), ())), preferred_element_type=jnp.float32
    )


DEAD = 4


def key_marks(segments, lengths, chip):
    rows = lax.broadcasted_iota(jnp.int32, (8, SEQ), 0)
    keys = lax.broadcasted_iota(jnp.int32, (8, SEQ), 1)
    groups = []
    for batch in range(MB):
        same = (rows < DEAD) & (segments[batch : batch + 1, :] == rows)
        dead = (keys >= chip * T) | (keys.astype(jnp.float32) >= lengths[batch])
        groups.append(jnp.where(same | ((rows == DEAD) & dead), 1.0, 0.0))
    groups.append(jnp.zeros((128 - 8 * MB, SEQ), jnp.float32))
    return jnp.concatenate(groups, axis=0).T.astype(jnp.bfloat16)


def query_marks(ids, batch, dead):
    place = lax.broadcasted_iota(jnp.int32, (128, 128), 0) - 8 * batch
    hit = (place >= 0) & (place < DEAD) & (place != ids)
    if dead:
        hit = hit | (place == DEAD)
    return jnp.where(hit, MASKED, 0.0).astype(jnp.bfloat16)


def own_bias(full):
    key = lax.broadcasted_iota(jnp.int32, (T, 128), 0)
    query = lax.broadcasted_iota(jnp.int32, (T, 128), 1) % T
    allowed = (key == query) | ((key <= query) & (full > 0.0))
    return jnp.where(allowed, 0.0, MASKED)


def all_heads(two):
    return jnp.concatenate([two] * 4, axis=1)


def mean_of(values):
    return jnp.sum(values, axis=-1, keepdims=True) * (1.0 / D)


def turn(values, cosine, sine):
    lane = lax.broadcasted_iota(jnp.int32, values.shape, 1) % 64
    swapped = jnp.where(lane < 32, pltpu.roll(values, QS - 32, 1), pltpu.roll(values, 32, 1))
    return values * cosine + swapped * sine


def tiled(table):
    wide = jnp.concatenate([table] * 4, axis=1)
    return jnp.concatenate([wide] * MB, axis=0)


def to_columns(rows):
    turned = rows.T
    return jnp.concatenate([turned[64 * h : 64 * h + 64] for h in range(8)], axis=1)


def to_rows(columns):
    pairs = []
    for pair in range(4):
        turned = columns[:, 128 * pair : 128 * pair + 128].T
        pairs.append(jnp.concatenate([turned[:64], turned[64:]], axis=1))
    return jnp.concatenate(pairs, axis=1)


def without_first_slot(rows):
    lane = lax.broadcasted_iota(jnp.int32, rows.shape, 1)
    return jnp.where(lane < 64, 0.0, rows)


def spread_matrix():
    row = lax.broadcasted_iota(jnp.int32, (D, DP), 0)
    column = lax.broadcasted_iota(jnp.int32, (1, DP), 1)
    spot = column % 16
    target = jnp.where(spot < 14, column // 16 * 14 + spot, -1)
    return jnp.where(row == target, 1.0, 0.0).astype(jnp.bfloat16)


def forward_kernel(
    gate_up, down, qkv, out_w, bias_in, gains_in, ends, segments, valid, cosine, sine,
    wa, wm, kv, gu, cot, gains, n1, qt, mixed, lse, att, mid, n2, hid, xs_, sq, km, qm, ob,
    ends_v, small_v, give_a, give_m, stage_a, stage_m, wat, wml, kvb, gu_v, mine, theirs,
    lsem, ssem, rsem, a_s, a_r, m_s, m_r, mp_s, mp_r, mq_s, mq_r, k_s, k_r, osem, wsem, xsem,
    xrsem,
):
    place = position()
    core = lax.axis_index("section")
    chip = lax.axis_index("dp")
    here = (place["x"], place["y"], place["z"])
    partners = greet(place, core=True, far=True)

    def heads_half(half):
        wide = qkv[...].astype(jnp.float32)
        outs_ = out_w[...].astype(jnp.float32)
        return jnp.concatenate(
            [
                wide[:, D + 64 * half : D + 64 * half + 64],
                wide[:, 448 * half : 448 * half + 448],
                wide[:, D + 128 + 64 * half : D + 192 + 64 * half],
                outs_[:, 448 * half : 448 * half + 448],
            ],
            axis=1,
        )

    def bias_half(half):
        wide = bias_in[...].astype(jnp.float32)
        return jnp.concatenate(
            [
                wide[:, D + 64 * half : D + 64 * half + 64],
                wide[:, 448 * half : 448 * half + 448],
                wide[:, D + 128 + 64 * half : D + 192 + 64 * half],
                jnp.zeros((1, 448), jnp.float32),
            ],
            axis=1,
        )

    halves = [heads_half(0), heads_half(1)]
    for dst, side in ((stage_a.at[core], 0), (give_a, 1)):
        dst[...] = jnp.zeros((16, CA), jnp.bfloat16)
        dst[0:14, :] = jnp.where(core == side, halves[0], halves[1]).astype(jnp.bfloat16)
    for dst, index in ((stage_m.at[core], core), (give_m, 1 - core)):
        dst[...] = jnp.zeros((16, CM), jnp.bfloat16)
        start = pl.multiple_of(index * FFH, 128)
        dst[0:14, 0:FFH] = gate_up[:, pl.ds(start, FFH)]
        dst[0:14, FFH : 2 * FFH] = gate_up[:, pl.ds(pl.multiple_of(start + 2 * FFH, 128), FFH)]
        dst[0:14, 2 * FFH : CM] = down[:, pl.ds(start, FFH)]
    settle(partners)

    trades = []

    def trade(index, give, dst):
        out = send(give, dst.at[core], ssem.at[index], rsem.at[index], other_core())
        back = send(give, dst.at[1 - core], ssem.at[index], rsem.at[index], other_core())
        out.start()
        trades.append((out, back))

    trade(0, give_a, stage_a)
    trade(1, give_m, stage_m)

    def arrive(index):
        out, back = trades[index]
        back.wait_recv()
        out.wait_send()

    arrive(0)
    into = [
        pltpu.make_async_copy(stage_a.at[layer], wat.at[(layer,) + here], lsem.at[layer])
        for layer in range(2)
    ]
    for one in into:
        one.start()
    for one in into:
        one.wait()
    attn = [
        gather_stages(weight_view(wat.at[layer], A_THIRDS), place, a_s.at[layer], a_r.at[layer])
        for layer in range(2)
    ]
    feed = [
        LargeGather(
            ref,
            place,
            m_s.at[layer],
            m_r.at[layer],
            (mp_s.at[layer], mp_r.at[layer]),
            (mq_s.at[layer], mq_r.at[layer]),
        )
        for layer, ref in enumerate((wml, wm.at[1]))
    ]
    early, late = feed
    keys = [
        gather_stages(token_view(kvb.at[layer]), place, k_s.at[layer], k_r.at[layer])
        for layer in range(2)
    ]
    attn[0][0]()
    attn[1][0]()
    arrive(1)
    into = [
        pltpu.make_async_copy(stage_m.at[0], wml.at[here], lsem.at[2]),
        pltpu.make_async_copy(stage_m.at[1], wm.at[(1,) + here], lsem.at[3]),
    ]
    for one in into:
        one.start()
    for one in into:
        one.wait()
    early.phases[0]()
    spread = spread_matrix()
    ends_v[core] = nn(ends[...], spread).astype(jnp.bfloat16)
    small_v[core] = jnp.zeros((8, DP), jnp.float32)
    small_v[core, 0:1, :] = bias_half(0)
    small_v[core, 1:2, :] = bias_half(1)
    small_v[core, 2:4, :] = nn(gains_in[...], spread)
    trade(2, ends_v.at[core], ends_v)
    trade(3, small_v.at[core], small_v)
    attn[0][1]()
    attn[1][1]()
    early.phases[1]()
    lengths = [
        jnp.sum(valid[batch : batch + 1, :].astype(jnp.float32), axis=1, keepdims=True) * BLOCK
        for batch in range(MB)
    ]
    km[...] = key_marks(segments, lengths, chip)
    pair = segments[:, pl.ds(pl.multiple_of(chip // 2 * 128, 128), 128)]
    ids = jnp.where(chip % 2 == 0, pair[:, :64], pair[:, 64:])
    ids = jnp.concatenate([ids, ids], axis=1)
    first_key = (chip * T).astype(jnp.float32)
    for batch in range(MB):
        for kind in range(2):
            qm[kind, batch] = query_marks(ids[batch : batch + 1, :], batch, kind == 0)
        full = jnp.where(first_key < lengths[batch], 1.0, 0.0)
        ob[batch] = own_bias(full)
    for index in range(2, 8):
        attn[0][index]()
        attn[1][index]()
    early.phases[2]()
    early.phases[3]()
    arrive(2)
    arrive(3)
    cot[...] = ends_v[...]
    gains[...] = small_v[...]
    attn[0][8]()

    outs = []

    def store(src, dst, index):
        one = pltpu.make_async_copy(src, dst, osem.at[index])
        one.start()
        outs.append(one)

    def rows_of(layer):
        return ends_v[0] if layer == 0 else xs_[0]

    def project(layer):
        rows = rows_of(layer).astype(jnp.float32)
        gain = gains[layer, 2:3, :]
        bias = jnp.where(core == 0, gains[layer, 0:1, :], gains[layer, 1:2, :])
        normed = (rows * lax.rsqrt(mean_of(rows * rows) + EPS) * gain).astype(jnp.bfloat16)
        n1[layer] = normed
        weights = wat[layer].reshape(DP, CA)
        projected = nn(normed, weights[:, : QS + 128]) + bias[:, : QS + 128]
        turned = turn(projected[:, :QS], tiled(cosine[...]), tiled(sine[...]))
        own = jnp.concatenate([turned[:, :64], projected[:, QS : QS + 64]], axis=1)
        kvb[(layer,) + here] = own.astype(jnp.bfloat16).reshape(MB, T, 128)
        heads = without_first_slot(turned).astype(jnp.bfloat16).astype(jnp.float32) * 0.125
        for batch in range(MB):
            columns = to_columns(heads[batch * T : (batch + 1) * T]).astype(jnp.bfloat16)
            qt[layer, batch] = jnp.concatenate([columns, jnp.zeros_like(columns)], axis=0)

    def attend(layer, batch):
        queries = jnp.concatenate([qt[layer, batch], all_heads(qm[0, batch])], axis=0)
        own_queries = jnp.concatenate([qt[layer, batch], all_heads(qm[1, batch])], axis=0)
        rows = kvb[(layer,) + here + (batch,)]
        marks = km[pl.ds(pl.multiple_of(chip * T, T), T), :]
        scores = nn(jnp.concatenate([rows, marks], axis=1), own_queries) + all_heads(ob[batch])
        top = jnp.max(scores, axis=0, keepdims=True)
        probs = jnp.exp(scores - top)
        total = jnp.sum(probs, axis=0, keepdims=True)
        sums = tn(rows, probs.astype(jnp.bfloat16))

        def step(index, carry):
            top, total, sums = carry
            rows = kvb[layer, index, :, :, batch].reshape(KB, 128)
            marks = km[pl.ds(pl.multiple_of(index * KB, KB), KB), :]
            scores = nn(jnp.concatenate([rows, marks], axis=1), queries)
            new_top = jnp.maximum(top, jnp.max(scores, axis=0, keepdims=True))
            shrink = jnp.exp(top - new_top)
            probs = jnp.exp(scores - new_top)
            total = total * shrink + jnp.sum(probs, axis=0, keepdims=True)
            sums = sums * shrink + tn(rows, probs.astype(jnp.bfloat16))
            return new_top, total, sums

        top, total, sums = lax.fori_loop(0, (chip + 15) // 16, step, (top, total, sums))
        result = (sums / total)[64:, :]
        mixed[layer, batch] = result
        lse[layer, batch] = jnp.broadcast_to(top + jnp.log(total), (8, QS))
        att[layer, pl.ds(batch * T, T), :] = without_first_slot(to_rows(result)).astype(
            jnp.bfloat16
        )

    def swap(slot):
        return send(mine.at[slot], theirs.at[slot], xsem.at[slot], xrsem.at[slot], other_core())

    def branch_of(layer):
        mine[0] = nt(att[layer], wat[layer, :, :, :, :, QS:].reshape(DP, QS))
        one = swap(0)
        one.start()
        one.wait()
        branch = mine[0] + theirs[0]
        middle = rows_of(layer).astype(jnp.float32) + branch
        mid[layer] = middle
        scale = lax.rsqrt(mean_of(middle * middle) + EPS)
        n2[layer] = (middle * scale * gains[layer, 3:4, :]).astype(jnp.bfloat16)
        return branch

    def feed_forward(layer, branch, hooks):
        normed = n2[layer]
        sums = jnp.zeros((R, DP), jnp.float32)
        for index, (start, size) in enumerate(FF_CHUNKS):
            hooks[index]()

            def weights(first, start=start, size=size):
                return wml[:, :, :, :, pl.ds(first + start, size)].reshape(DP, size)

            gate = nn(normed, weights(0))
            up = nn(normed, weights(FFH))
            gu_v[:, pl.ds(start, size)] = gate
            gu_v[:, pl.ds(FFH + start, size)] = up
            hidden = (gate * jax.nn.sigmoid(gate) * up).astype(jnp.bfloat16)
            hid[layer, :, pl.ds(start, size)] = hidden
            sums = sums + nt(hidden, weights(2 * FFH))
        store(gu_v, gu.at[layer], 4 + layer)
        mine[1] = sums
        one = swap(1)
        one.start()
        one.wait()
        result = mine[1] + theirs[1]
        middle = mid[layer]
        xs_[layer] = (middle + result).astype(jnp.bfloat16)
        rows = rows_of(layer).astype(jnp.float32)
        lane = lax.broadcasted_iota(jnp.int32, (8, 128), 1)
        table = jnp.zeros((8, 128), jnp.float32)
        for kind, values in enumerate((rows, branch, result)):
            squares = jnp.sum(values * values, axis=1, keepdims=True)
            for batch in range(MB):
                one = jnp.sum(squares[batch * T : (batch + 1) * T], axis=0, keepdims=True)
                one = jnp.where(first_key < lengths[batch], one, 0.0)
                table = jnp.where(lane == 3 * batch + kind, one, table)
        sq[layer] = table

    def nothing():
        pass

    def beside(stages, rounds):
        rounds = iter(rounds)
        for index in range(8):
            stages[index]()
            if index not in (2, 5):
                next(rounds)()

    def calls(method, *numbers):
        return [functools.partial(method, r) for r in numbers]

    def rounds_of(*methods):
        for method in methods:
            for r in range(ROUNDS):
                method(r)

    project(0)
    beside(
        keys[0],
        [
            early.phases[4],
            nothing,
            lambda: (early.phases[5](), early.ahead(0)),
            *calls(early.ahead, 1, 2, 3),
        ],
    )
    keys[0][8]()
    rounds_of(early.rest)
    store(kvb.at[0], kv.at[0], 0)
    attend(0, 0)
    early.pass_on(0)
    early.pass_on(1)
    attend(0, 1)
    early.pass_on(2)
    early.pass_on(3)
    late.phases[0]()
    attend(0, 2)
    late.phases[1]()
    branch = branch_of(0)
    early.last()
    store(wml, wm.at[0], 2)
    late.phases[2]()
    late.phases[3]()
    feed_forward(0, branch, [nothing] * 3 + [late.phases[4], nothing])
    late.phases[5]()
    late.ahead(0)
    late.ahead(1)
    attn[1][8]()
    store(wat, wa, 1)
    project(1)
    beside(
        keys[1], [nothing, nothing, *calls(late.ahead, 2, 3), *calls(late.rest, 0, 1)]
    )
    keys[1][8]()
    late.rest(2)
    late.rest(3)
    store(kvb.at[1], kv.at[1], 3)
    attend(1, 0)
    late.pass_on(0)
    late.pass_on(1)
    attend(1, 1)
    late.pass_on(2)
    late.pass_on(3)
    attend(1, 2)
    branch = branch_of(1)
    late.last()
    early.finish()
    outs[1].wait()
    outs[2].wait()
    loads = []
    for index, (start, size) in enumerate(FF_CHUNKS):
        for part in range(3):
            cols = pl.ds(part * FFH + start, size)
            loads.append(
                pltpu.make_async_copy(
                    wm.at[1, :, :, :, :, cols],
                    wml.at[:, :, :, :, cols],
                    wsem.at[3 * index + part],
                )
            )
    for one in loads:
        one.start()

    def ready(index):
        for one in loads[3 * index : 3 * index + 3]:
            one.wait()

    feed_forward(1, branch, [functools.partial(ready, index) for index in range(5)])
    for index, one in enumerate(outs):
        if index not in (1, 2):
            one.wait()
    late.finish()
    for stages in attn + keys:
        stages[9]()


def forward(*arrays):
    low, full = jnp.bfloat16, jnp.float32
    return pl.pallas_call(
        forward_kernel,
        out_shape=(
            shape((2, 4, 4, 4, 16, CA), low),
            shape((2, 4, 4, 4, 16, CM), low),
            shape((2, 4, 4, 4, MB, T, 128), low),
            shape((2, R, 2 * FFH), full),
            shape((2, R, DP), low),
            shape((2, 8, DP), full),
            shape((2, R, DP), low),
            shape((2, MB, 128, QS), low),
            shape((2, MB, 64, QS), full),
            shape((2, MB, 8, QS), full),
            shape((2, R, QS), low),
            shape((2, R, DP), full),
            shape((2, R, DP), low),
            shape((2, R, FFH), low),
            shape((2, R, DP), low),
            shape((2, 8, 128), full),
            shape((SEQ, 128), low),
            shape((2, MB, 128, 128), low),
            shape((MB, T, 128), full),
        ),
        in_specs=[VMEM] * 11,
        out_specs=(ANY,) * 4 + (VMEM,) * 15,
        scratch_shapes=[
            pltpu.VMEM((2, R, DP), low),
            pltpu.VMEM((2, 8, DP), full),
            pltpu.VMEM((16, CA), low),
            pltpu.VMEM((16, CM), low),
            pltpu.VMEM((2, 16, CA), low),
            pltpu.VMEM((2, 16, CM), low),
            pltpu.VMEM((2, 4, 4, 4, 16, CA), low),
            pltpu.VMEM((4, 4, 4, 16, CM), low),
            pltpu.VMEM((2, 4, 4, 4, MB, T, 128), low),
            pltpu.VMEM((R, 2 * FFH), full),
            pltpu.VMEM((2, R, DP), full),
            pltpu.VMEM((2, R, DP), full),
            DMA((4,)),
            DMA((4,)),
            DMA((4,)),
            DMA((2, 3, 3, 4)),
            DMA((2, 3, 3, 4)),
            DMA((2, 3, 3, 4)),
            DMA((2, 3, 3, 4)),
            DMA((2, 3, 2, 2, ROUNDS)),
            DMA((2, 3, 2, 2, ROUNDS)),
            DMA((2, 3, 2, ROUNDS)),
            DMA((2, 3, 2, ROUNDS)),
            DMA((2, 3, 3, 4)),
            DMA((2, 3, 3, 4)),
            DMA((6,)),
            DMA((15,)),
            DMA((2,)),
            DMA((2,)),
        ],
        compiler_params=params(0, vmem=60),
        name="forward",
    )(*arrays)


def norm_back(grad, rows, gain):
    scale = lax.rsqrt(mean_of(rows * rows) + EPS)
    scaled = grad * gain
    back = scale * scaled - rows * (scale * scale * scale) * mean_of(scaled * rows)
    return back, jnp.sum(grad * rows * scale, axis=0, keepdims=True)


SLOT = 256
FF_SLOTS = tuple((start, min(SLOT, FFH - start)) for start in range(0, FFH, SLOT))
A_SLOTS = ((0, 3), (3, 3), (6, 2))


def slot_view(pool):
    def view(chips, j, part):
        lanes = slice(None) if part is None else pl.ds(part * 128, 128)
        return pool.at[(pl.ds(*A_SLOTS[j]),) + tuple(chips) + (slice(None), lanes)]

    return view


def backward_kernel(
    wa, wm, kv, gu, ends, xs_, gains, n1, qt, mixed, lse, att, mid, n2, squares, cosine, sine,
    km, qm, ob,
    grads, dx, outv, other, small_out,
    pool, gbuf, n2t, dmt, wat, mine, theirs, dout, dmid, da, dot_, dqk, low, vlow, kvb, own,
    kh0, kw0, kw1, kw2, slab, got_half, got_whole, spare, mh1, mw1, mw2, ah0, aw0, aw1, aw2,
    sbuf,
    lsem, psem, gsem, usem, xsem, xrsem, ks, kr, hs, hr, os_, or_, ws, wr, ls, ms, mr, as_, ar,
    bs, br, fs, fr, credit,
):
    place = position()
    core = lax.axis_index("section")
    chip = lax.axis_index("dp")
    here = (place["x"], place["y"], place["z"])
    partners = greet(place, core=True, far=True)
    steps = (chip + 15) // 16

    def heads_load(layer):
        return pltpu.make_async_copy(wa.at[layer], wat, lsem.at[2 * layer])

    def keys_load(layer):
        return pltpu.make_async_copy(kv.at[layer], kvb, lsem.at[2 * layer + 1])

    heads_load(1).start()
    keys_load(1).start()
    dout[...] = ends[1].astype(jnp.float32)
    settle(partners)
    small = [[None] * 4, [None] * 4]
    stored = {}

    def swap(slot):
        return send(mine.at[slot], theirs.at[slot], xsem.at[slot], xrsem.at[slot], other_core())

    def back_feed(layer, hooks):
        def loads(index):
            start, size = FF_SLOTS[index]
            slot = index % 2
            copies = []
            for part in range(3):
                copies.append(
                    pltpu.make_async_copy(
                        wm.at[layer, :, :, :, :, pl.ds(part * FFH + start, size)],
                        pool.at[3 * slot + part, :, :, :, :, pl.ds(0, size)],
                        psem.at[slot, part],
                    )
                )
            for part in range(2):
                copies.append(
                    pltpu.make_async_copy(
                        gu.at[layer, :, pl.ds(part * FFH + start, size)],
                        gbuf.at[slot, part, :, pl.ds(0, size)],
                        usem.at[slot, part],
                    )
                )
            return copies

        for index in range(2):
            for one in loads(index):
                one.start()
        grad_in = dout[...]
        grad_low = grad_in.astype(jnp.bfloat16)
        n2t[...] = n2[layer].astype(jnp.float32).T.astype(jnp.bfloat16)
        dmt[...] = grad_low.astype(jnp.float32).T.astype(jnp.bfloat16)
        mine[0] = jnp.zeros((R, DP), jnp.float32)
        for index, (start, size) in enumerate(FF_SLOTS):
            slot = index % 2
            hooks.get(index, lambda: None)()
            for one in loads(index):
                one.wait()

            def weights(part, slot=slot, size=size):
                return pool[3 * slot + part, :, :, :, :, :size].reshape(DP, size)

            grad_hidden = nn(grad_low, weights(2))
            gate = gbuf[slot, 0, :, :size]
            up = gbuf[slot, 1, :, :size]
            sigma = jax.nn.sigmoid(gate)
            hidden = (gate * sigma * up).astype(jnp.bfloat16)
            grad_gate = grad_hidden * up * sigma * (1.0 + gate * (1.0 - sigma))
            grad_gate = grad_gate.astype(jnp.bfloat16)
            grad_up = (grad_hidden * gate * sigma).astype(jnp.bfloat16)
            mine[0] += nt(grad_gate, weights(0)) + nt(grad_up, weights(1))
            if index + 2 < len(FF_SLOTS):
                for one in loads(index + 2):
                    one.start()
            products = ((n2t, grad_gate), (n2t, grad_up), (dmt, hidden))
            for part, (left, right) in enumerate(products):
                held = 6 + 3 * slot + part
                if held in stored:
                    stored.pop(held).wait()
                pool[held, :, :, :, :, :size] = (
                    nn(left[...], right).astype(jnp.bfloat16).reshape(4, 4, 4, 16, size)
                )
                stored[held] = pltpu.make_async_copy(
                    pool.at[held, :, :, :, :, pl.ds(0, size)],
                    grads.at[layer, :, :, :, :, pl.ds(part * FFH + start, size)],
                    gsem.at[slot, part],
                )
                stored[held].start()
        one = swap(0)
        one.start()
        one.wait()
        back, gain_row = norm_back(mine[0] + theirs[0], mid[layer], gains[layer, 3:4, :])
        small[layer][1] = gain_row
        middle = grad_in + back
        dmid[...] = middle
        middle_low = middle.astype(jnp.bfloat16)
        da[layer] = middle_low
        heads_load(layer).wait()
        turned = nn(middle_low, wat[:, :, :, :, QS:].reshape(DP, QS))
        turned = without_first_slot(turned.astype(jnp.bfloat16).astype(jnp.float32))
        for batch in range(MB):
            columns = to_columns(turned[batch * T : (batch + 1) * T]).astype(jnp.bfloat16)
            dot_[batch] = jnp.concatenate([jnp.zeros_like(columns), columns], axis=0)
        for held in list(stored):
            stored.pop(held).wait()

    def back_attend(layer, batch):
        if batch == 0:
            keys_load(layer).wait()
        slopes_out = dot_[batch]
        queries = qt[layer, batch]
        marked = jnp.concatenate([queries, all_heads(qm[0, batch])], axis=0)
        log_total = lse[layer, batch, 0:1, :]
        inner = jnp.sum(
            mixed[layer, batch] * slopes_out[64:, :].astype(jnp.float32), axis=0, keepdims=True
        )

        def terms(rows, scores):
            probs = jnp.exp(scores - log_total)
            slopes = (probs * (nn(rows, slopes_out) - inner)).astype(jnp.bfloat16)
            both = nt(slopes, queries) + nt(probs.astype(jnp.bfloat16), slopes_out)
            return both.astype(jnp.bfloat16), tn(rows, slopes)

        own_rows = kvb[here + (batch,)]
        marks = km[pl.ds(pl.multiple_of(chip * T, T), T), :]
        scores = nn(
            jnp.concatenate([own_rows, marks], axis=1),
            jnp.concatenate([queries, all_heads(qm[1, batch])], axis=0),
        )
        own_both, sums = terms(own_rows, scores + all_heads(ob[batch]))

        def step(index, sums):
            rows = kvb[index, :, :, batch].reshape(KB, 128)
            marks = km[pl.ds(pl.multiple_of(index * KB, KB), KB), :]
            both, more = terms(rows, nn(jnp.concatenate([rows, marks], axis=1), marked))
            kvb[index, :, :, batch] = both.reshape(4, 4, T, 128)
            return sums + more

        sums = lax.fori_loop(0, steps, step, sums)

        def clear(index, nothing):
            kvb[index, :, :, batch] = jnp.zeros((4, 4, T, 128), jnp.bfloat16)
            return nothing

        lax.fori_loop(steps, 4, clear, 0)
        kvb[here + (batch,)] = own_both
        dqk[pl.ds(batch * T, T), :] = to_rows(sums[:64, :] * 0.125)

    def back_project(layer):
        key_grads = own[...].reshape(R, 128)
        whole = jnp.concatenate([key_grads[:, :64], dqk[:, 64:]], axis=1)
        turned = turn(whole, tiled(cosine[...]), -tiled(sine[...])).astype(jnp.bfloat16)
        values = jnp.concatenate(
            [key_grads[:, 64:], jnp.zeros((R, QS - 64), jnp.float32)], axis=1
        ).astype(jnp.bfloat16)
        low[layer] = turned
        vlow[layer] = values
        small[layer][2] = jnp.concatenate(
            [
                jnp.sum(turned.astype(jnp.float32), axis=0, keepdims=True),
                jnp.sum(values.astype(jnp.float32), axis=0, keepdims=True),
            ],
            axis=1,
        )
        mine[1] = nt(turned, wat[:, :, :, :, :QS].reshape(DP, QS)) + nt(
            values, wat[:, :, :, :, QS:].reshape(DP, QS)
        )
        one = swap(1)
        one.start()
        one.wait()
        rows = (ends[0] if layer == 0 else xs_[0]).astype(jnp.float32)
        back, gain_row = norm_back(mine[1] + theirs[1], rows, gains[layer, 2:3, :])
        small[layer][0] = gain_row
        small[layer][3] = jnp.concatenate(
            [squares[layer, 0:1, :], jnp.zeros((1, DP - 128), jnp.float32)], axis=1
        )
        result = (dmid[...] + back).astype(jnp.bfloat16)
        if layer == 0:
            dx[...] = result
        else:
            dout[...] = result.astype(jnp.float32)

    def heads_products(layer):
        first = tn(n1[layer], low[layer])
        second = tn(n1[layer], vlow[layer]) + tn(da[layer], att[layer])
        for side, product in enumerate((first, second)):
            for part in range(2):
                pool[4 * layer + 2 * side + part] = (
                    product[:, part * SLOT : (part + 1) * SLOT]
                    .astype(jnp.bfloat16)
                    .reshape(4, 4, 4, 16, SLOT)
                )

    def total(terms):
        return sum(term[...].astype(jnp.float32) for term in terms)

    def key_final(j, *terms):
        own[j] = total(terms)

    key_halves = [lambda j, k, ref=ref: ref.at[j, k] for ref in (kh0,)]
    key_wholes = [lambda j, k, ref=ref: ref.at[j, k] for ref in (kw0, kw1, kw2)]
    keys = [
        scatter_stages(
            token_view(kvb), key_halves, key_wholes, place, ks.at[layer], kr.at[layer], key_final
        )
        for layer in range(2)
    ]

    def feed_final(layer):
        def final(j, *terms):
            outv[layer, :, pl.ds(j * FFH, FFH)] = total(terms)

        return final

    def lanes(ref, size):
        return lambda j, k: ref.at[
            (j, k) + (slice(None),) * (len(ref.shape) - 3) + (pl.ds(0, size(k)),)
        ]

    inner_halves = [None, lanes(mh1, lambda k: half_of(FFH, k)[1])]
    inner_wholes = [None] + [lanes(ref, lambda k: FFH) for ref in (mw1, mw2)]
    feed = [
        LargeScatter(
            grads.at[layer], slab, got_half, got_whole, spare, inner_halves, inner_wholes, place,
            (hs.at[layer], hr.at[layer]), (os_.at[layer], or_.at[layer]),
            (ws.at[layer], wr.at[layer]), ls.at[layer], ms.at[layer], mr.at[layer],
            feed_final(layer),
        )
        for layer in range(2)
    ]
    late, early = feed

    def slots(ref):
        return lambda j, k: ref.at[j, k, pl.ds(0, A_SLOTS[j][1])]

    def heads_final(j, *terms):
        begin, count = A_SLOTS[j]
        for index in range(count):
            layer, spot = divmod(begin + index, 4)
            outv[layer, :, pl.ds(CM + spot * SLOT, SLOT)] = total(
                [term.at[index] for term in terms]
            )

    heads = scatter_stages(
        slot_view(pool), [slots(ah0)],
        [slots(ref) for ref in (aw0, aw1, aw2)], place, as_, ar, heads_final,
    )

    def total_small(phase, axis):
        copies = [
            send(
                sbuf.at[4 * phase],
                sbuf.at[4 * phase + k],
                bs.at[phase, k - 1],
                br.at[phase, k - 1],
                chip_id(moved(place, axis, distance)),
            )
            for k, distance in ((1, 1), (2, -1), (3, 2))
        ]

        def begin():
            for one in copies:
                one.start()

        def end():
            for one in copies:
                one.wait()
            total = (
                sbuf[4 * phase] + sbuf[4 * phase + 1] + sbuf[4 * phase + 2] + sbuf[4 * phase + 3]
            )
            if phase < 2:
                sbuf[4 * phase + 4] = total
            else:
                small_out[...] = total

        return begin, end

    def beside(stages, rounds):
        rounds = iter(rounds)
        for index in range(8):
            stages[index]()
            if index not in (2, 5):
                next(rounds)()

    def calls(method, *numbers):
        return [functools.partial(method, r) for r in numbers]

    def nothing():
        pass

    def rounds_of(*methods):
        for method in methods:
            for r in range(ROUNDS):
                method(r)

    back_feed(1, {})
    rounds_of(early.ahead, early.rest)
    for batch in range(MB):
        back_attend(1, batch)
    for stage in keys[1][:8]:
        stage()
    rounds_of(early.pass_on)
    keys[1][8]()
    keys[1][9]()
    keys_load(0).start()
    back_project(1)
    heads_load(0).start()
    back_feed(
        0,
        {
            2: lambda: (early.third(), early.phases[0]()),
            4: early.phases[1],
            6: lambda: (early.phases[2](), early.phases[3]()),
            9: early.phases[5],
        },
    )
    early.finish()
    for axis in "xyz":
        for distance in (1, -1, 2):
            pl.semaphore_signal(
                credit, inc=1, device_id=chip_id(moved(place, axis, distance)), device_id_type=MESH
            )
    pl.semaphore_wait(credit, 9)
    rounds_of(late.ahead)
    back_attend(0, 0)
    late.pass_on(0)
    late.pass_on(1)
    back_attend(0, 1)
    late.pass_on(2)
    late.pass_on(3)
    late.rest(0)
    back_attend(0, 2)
    beside(
        keys[0],
        [nothing, *calls(late.rest, 1, 2, 3), functools.partial(heads_products, 1), nothing],
    )
    keys[0][8]()
    keys[0][9]()
    late.third()
    late.phases[0]()
    back_project(0)
    heads_products(0)
    sbuf[0] = jnp.concatenate(small[0] + small[1], axis=0)
    sums = [total_small(phase, axis) for phase, axis in enumerate("xyz")]
    sums[0][0]()
    heads[0]()
    late.phases[1]()
    sums[0][1]()
    sums[1][0]()
    heads[1]()
    late.phases[2]()
    late.phases[3]()
    heads[2]()
    heads[3]()
    sums[1][1]()
    sums[2][0]()
    late.phases[5]()
    heads[5]()
    heads[6]()
    sums[2][1]()
    heads[8]()
    for layer in range(2):
        outv[layer, 14:15, pl.ds(CM, CA)] = small_out[4 * layer + 2 : 4 * layer + 3, :]
    trade = send(outv.at[1 - core], other, fs, fr, other_core())
    trade.start()
    late.finish()
    heads[9]()
    trade.wait()


def backward(*arrays):
    low, full = jnp.bfloat16, jnp.float32
    half = FFH - FFH // 256 * 128

    def ring(last, phase, count=2):
        return pltpu.VMEM((3, count) + last[:-2] + (4,) * (2 - phase) + last[-2:], low)

    return pl.pallas_call(
        backward_kernel,
        out_shape=(
            shape((2, 4, 4, 4, 16, CM), low),
            shape((R, DP), low),
            shape((2, 16, C), full),
            shape((16, C), full),
            shape((8, DP), full),
        ),
        in_specs=[ANY] * 4 + [VMEM] * 16,
        out_specs=(ANY,) + (VMEM,) * 4,
        scratch_shapes=[
            pltpu.VMEM((12, 4, 4, 4, 16, SLOT), low),
            pltpu.VMEM((2, 2, R, SLOT), full),
            pltpu.VMEM((DP, R), low),
            pltpu.VMEM((DP, R), low),
            pltpu.VMEM((4, 4, 4, 16, CA), low),
            pltpu.VMEM((2, R, DP), full),
            pltpu.VMEM((2, R, DP), full),
            pltpu.VMEM((R, DP), full),
            pltpu.VMEM((R, DP), full),
            pltpu.VMEM((2, R, DP), low),
            pltpu.VMEM((MB, 128, QS), low),
            pltpu.VMEM((R, QS), full),
            pltpu.VMEM((2, R, QS), low),
            pltpu.VMEM((2, R, QS), low),
            pltpu.VMEM((4, 4, 4, MB, T, 128), low),
            pltpu.VMEM((MB, T, 128), full),
        ]
        + [
            ring((T // 2, 128), 0),
            ring((T, 128), 0),
            ring((T, 128), 1, 3),
            ring((T, 128), 2, 3),
            pltpu.VMEM((3, 4, 4, 16, FFH), low),
            ring((16, half), 0),
            ring((16, FFH), 0),
            ring((16, 384), 0),
            ring((16, half), 1),
            ring((16, FFH), 1),
            ring((16, FFH), 2, 3),
            ring((3, 16, 128), 0),
            ring((3, 16, SLOT), 0),
            ring((3, 16, SLOT), 1, 3),
            ring((3, 16, SLOT), 2, 3),
        ]
        + [
            pltpu.VMEM((12, 8, DP), full),
            DMA((4,)),
            DMA((2, 3)),
            DMA((2, 3)),
            DMA((2, 2)),
            DMA((2,)),
            DMA((2,)),
            DMA((2, 3, 3, 4)),
            DMA((2, 3, 3, 4)),
            DMA((2, 3, 2, ROUNDS)),
            DMA((2, 3, 2, ROUNDS)),
            DMA((2, 3, 2, ROUNDS)),
            DMA((2, 3, 2, ROUNDS)),
            DMA((2, 3, 2, ROUNDS)),
            DMA((2, 3, 2, ROUNDS)),
            DMA((2, 9)),
            DMA((2, 3, 3, 4)),
            DMA((2, 3, 3, 4)),
            DMA((3, 3, 4)),
            DMA((3, 3, 4)),
            DMA((3, 3)),
            DMA((3, 3)),
            DMA,
            DMA,
            pltpu.SemaphoreType.REGULAR,
        ],
        compiler_params=params(1, vmem=63),
        name="backward",
    )(*arrays)


def assemble_kernel(
    kept, other, dx, xs_, sums, valid, boundary, grad_qkv, grad_bias, grad_out, grad_gu, grad_down,
    grad_gain, rms,
):
    core = lax.axis_index("section")
    own, far = jnp.where(core == 0, kept[0], kept[1]), other[...]
    sides = (jnp.where(core == 0, own, far), jnp.where(core == 0, far, own))

    def column(start, size):
        return [side[:, start : start + size] for side in sides]

    qkv = jnp.concatenate(column(CM + 64, 448) + column(CM, 64) + column(CM + QS, 64), axis=1)
    out = jnp.concatenate(column(CM + QS + 64, 448), axis=1)
    gate_up = jnp.concatenate(column(0, FFH) + column(FFH, FFH), axis=1)
    down = jnp.concatenate(column(2 * FFH, FFH), axis=1)
    for row in range(14):
        grad_qkv[row] = qkv[row : row + 1, :]
        grad_out[row] = out[row : row + 1, :]
        grad_gu[row] = gate_up[row : row + 1, :]
        grad_down[row] = down[row : row + 1, :]
    rows = [side[14:15, CM:] for side in sides]
    grad_bias[...] = jnp.concatenate(
        [row[:, 64:QS] for row in rows]
        + [row[:, :64] for row in rows]
        + [row[:, QS : QS + 64] for row in rows],
        axis=1,
    )
    mine = jnp.where(core == 0, sums[0:4, :], sums[4:8, :])
    rest = jnp.concatenate([mine, jnp.zeros((12, DP), jnp.float32)], axis=0)
    terms = []
    for _ in range(3):
        term = rest.astype(jnp.bfloat16)
        rest = rest - term.astype(jnp.float32)
        terms.append(term)
    result = jnp.where(core == 0, dx[...].astype(jnp.float32), xs_[1].astype(jnp.float32))
    narrow = nt(
        jnp.concatenate([result.astype(jnp.bfloat16)] + terms, axis=0), spread_matrix()
    )
    boundary[...] = narrow[:R].astype(jnp.bfloat16)
    grad_gain[...] = narrow[R : R + 2] + narrow[R + 16 : R + 18] + narrow[R + 32 : R + 34]
    for batch in range(MB):
        count = jnp.sum(valid[batch : batch + 1, :].astype(jnp.float32), axis=1, keepdims=True)
        rms[batch] = jnp.sqrt(mine[3:4, 3 * batch : 3 * batch + 3] / (count * float(BLOCK * D)))


def assemble(*arrays):
    full = jnp.float32
    return pl.pallas_call(
        assemble_kernel,
        out_shape=(
            shape((R, D), jnp.bfloat16),
            shape((14, 1, D + 256), full),
            shape((1, D + 256), full),
            shape((14, 1, D), full),
            shape((14, 1, 4 * FFH), full),
            shape((14, 1, 2 * FFH), full),
            shape((2, D), full),
            shape((MB, 1, MB), full),
        ),
        in_specs=[VMEM] * 6,
        out_specs=(VMEM,) * 8,
        compiler_params=params(),
        name="assemble",
    )(*arrays)


def shards(
    ends,
    segment_ids,
    valid_blocks,
    qkv_weight,
    qkv_bias,
    out_weight,
    gate_up_weight,
    down_weight,
    norm_gains,
):
    chip = lax.axis_index("dp")
    places = chip * T + jnp.arange(T, dtype=jnp.int32)
    frequency = THETA ** (-(jnp.arange(128) % 32).astype(jnp.float32) * 2.0 / 64)
    sign = jnp.where(jnp.arange(128) % 64 < 32, -1.0, 1.0)
    angles = places.astype(jnp.float32)[:, None] * frequency[None, :]
    cosine = jnp.cos(angles)
    sine = jnp.sin(angles) * sign[None, :]

    (
        wa, wm, kv, gu, ends_all, gains, n1, qt, mixed, lse, att, mid, n2, _, xs_, sq, km, qm, ob,
    ) = forward(
        gate_up_weight[0],
        down_weight[0],
        qkv_weight[0],
        out_weight[0],
        qkv_bias,
        norm_gains[0],
        ends.reshape(R, D),
        segment_ids,
        valid_blocks,
        cosine,
        sine,
    )
    _, dx, kept, other, sums = backward(
        wa, wm, kv, gu, ends_all, xs_, gains, n1, qt, mixed, lse, att, mid, n2, sq, cosine, sine,
        km, qm, ob,
    )
    boundary, *grads, rms = assemble(kept, other, dx, xs_, sums, valid_blocks)
    grad_qkv, grad_bias, grad_out, grad_gu, grad_down, grad_gain = grads
    return (
        boundary.reshape(1, MB, T, D),
        grad_qkv.transpose(1, 0, 2),
        grad_bias,
        grad_out.transpose(1, 0, 2),
        grad_gu.transpose(1, 0, 2),
        grad_down.transpose(1, 0, 2),
        grad_gain[None],
        rms.transpose(1, 0, 2),
    )


def solution(mesh):
    in_specs = (
        P("section", None, "dp", None),
        P(),
        P(),
        P("section", "dp", None),
        P("section", None),
        P("section", "dp", None),
        P("section", "dp", None),
        P("section", "dp", None),
        P("section", None, None),
    )
    out_specs = (
        P("section", None, "dp", None),
        P("section", "dp", None),
        P("section", None),
        P("section", "dp", None),
        P("section", "dp", None),
        P("section", "dp", None),
        P("section", None, None),
        P("section", None, None),
    )
    return jax.shard_map(shards, mesh=mesh, in_specs=in_specs, out_specs=out_specs, check_vma=False)
```

time: 487 us -> 435 us (0.89)
  local copies, waits for them, and re-layouts: 21.6 us -> 0 us
  Pallas kernels: 446 us -> 427 us
  other arithmetic: 7.16 us -> 0.84 us
    pallas_call x1, Pallas kernels: 244 us -> 228 us  [backward(): pl.pallas_call(backward_kernel, out_shape=(shape((2, 4, 4, 4, 16, CM), lo...]
    pallas_call x1, Pallas kernels: 202 us -> 196 us  [forward(): pl.pallas_call(forward_kernel, out_shape=(shape((2, 4, 4, 4, 16, CA), low...]
    dynamic_slice x6 -> x0, local copies, waits for them, and re-layouts: 5.37 us -> none  [the longest x1 1.08 us: feed_half(): lax.dynamic_slice_in_dim(gate_up_weight[0], index * FFH, FFH, 1)]
where the time goes in v4:
time: 435 us; the launch traced here: 429 us
  Pallas kernels  427 us (98%)
    pallas_call x1, Pallas kernels, backward(): pl.pallas_call(backward_kernel, out_shape=(shape((2, 4, 4, 4, 16, CM), lo...  228 us
    pallas_call x1, Pallas kernels, forward(): pl.pallas_call(forward_kernel, out_shape=(shape((2, 4, 4, 4, 16, CA), low...  196 us

profile of v4, /device:TPU:1, one launch (start us, length us, event | category | flops | bytes accessed | tf_op | source)
XLA Modules:
  0.0 428.5 jit_solution(10407956800612426928)
XLA Ops:
  0.7 0.8 fusion
  1.5 195.8 %forward.1 = (bf16[2,4,4,4,16,1024]{5,4,3,2,1,0:T(8,128)(2,1)}, bf16[2,4,4,4,16,7296]{5,4,3,2,1,0:T(8,128)(2,1)}, bf16[2,4,4,4,3,64,128]{6,5,4,3,2,1,0:T(8,128)(...) custom-call(bf16[14,9728]{1,0:T(8,128)(2,1)} %bitcast.14, ...), custom_call_target="tpu_custom_call" | custom-call | tf_op jit(solution)/shard_map/forward/pallas_call | solution.py:885
  197.3 227.5 %backward.1 = (bf16[2,4,4,4,16,7296]{5,4,3,2,1,0:T(8,128)(2,1)}, bf16[192,1024]{1,0:T(8,128)(2,1)}, f32[2,16,8320]{2,1,0:T(8,128)}, f32[16,8320]{1,0:T(8,128)}, f32[8,1024]{1,0:T(8,128)}) custom-call(bf16[2,4,4,4,16,1024]{5,4,3,2,1,0:T(8,128)(2,1)} %get-tuple-element.38.wa, bf16[2,4,4,4,16,7296]{5,4,3,2,1,0:T(8,128)(2,1)} %get-tuple-element.39.wm, ...), custom_call_target="tpu_custom_call" | custom-call | tf_op jit(solution)/shard_map/backward/pallas_call | solution.py:1354
  424.8 3.5 assemble.1
  (2 shorter events, 0.0 us)

commit v5 on v4

--- a/solution.py
+++ b/solution.py
@@ -366,18 +366,16 @@
         one.start()
         self.pending.append(one)
 
-    def ahead(self, r):
+    def group(self, half, r):
+        for j in range(3):
+            self.start(self.half_copy(j, half, (1, -1)[half], r))
+            self.start(self.rest_copy(j, 1 - half, (1, -1)[1 - half], r))
+
+    def load(self):
         for j, k, distance in TURNS:
-            self.start(self.half_copy(j, k, distance, r))
-        if r == 0:
-            for j, k, distance in TURNS:
-                self.own_load(j, k, distance, 0).start()
-            for j in range(3):
-                self.slab_load(j).start()
-
-    def rest(self, r):
-        for j, k, distance in TURNS:
-            self.start(self.rest_copy(j, k, distance, r))
+            self.own_load(j, k, distance, 0).start()
+        for j in range(3):
+            self.slab_load(j).start()
 
     def pass_on(self, r):
         for j, k, distance in TURNS:
@@ -469,7 +467,8 @@
         dead = (keys >= chip * T) | (keys.astype(jnp.float32) >= lengths[batch])
         groups.append(jnp.where(same | ((rows == DEAD) & dead), 1.0, 0.0))
     groups.append(jnp.zeros((128 - 8 * MB, SEQ), jnp.float32))
-    return jnp.concatenate(groups, axis=0).T.astype(jnp.bfloat16)
+    marks = jnp.concatenate(groups, axis=0).T.astype(jnp.bfloat16)
+    return marks.reshape(4, 4, 4, T, 128)
 
 
 def query_marks(ids, batch, dead):
@@ -496,14 +495,19 @@
 
 
 def turn(values, cosine, sine):
+    width = values.shape[1]
     lane = lax.broadcasted_iota(jnp.int32, values.shape, 1) % 64
-    swapped = jnp.where(lane < 32, pltpu.roll(values, QS - 32, 1), pltpu.roll(values, 32, 1))
+    swapped = jnp.where(lane < 32, pltpu.roll(values, width - 32, 1), pltpu.roll(values, 32, 1))
     return values * cosine + swapped * sine
 
 
-def tiled(table):
-    wide = jnp.concatenate([table] * 4, axis=1)
+def tiled(table, columns=QS):
+    wide = jnp.concatenate([table] * (columns // 128), axis=1)
     return jnp.concatenate([wide] * MB, axis=0)
+
+
+def plane(batch, index):
+    return tuple(index if axis == ORDERS[batch][2] else slice(None) for axis in "xyz")
 
 
 def to_columns(rows):
@@ -536,7 +540,7 @@
     gate_up, down, qkv, out_w, bias_in, gains_in, ends, segments, valid, cosine, sine,
     wa, wm, kv, gu, cot, gains, n1, qt, mixed, lse, att, mid, n2, hid, xs_, sq, km, qm, ob,
     ends_v, small_v, give_a, give_m, stage_a, stage_m, wat, wml, kvb, gu_v, mine, theirs,
-    lsem, ssem, rsem, a_s, a_r, m_s, m_r, mp_s, mp_r, mq_s, mq_r, k_s, k_r, osem, wsem, xsem,
+    state, acc, lsem, ssem, rsem, a_s, a_r, m_s, m_r, mp_s, mp_r, mq_s, mq_r, k_s, k_r, osem, wsem, xsem,
     xrsem,
 ):
     place = position()
@@ -685,46 +689,67 @@
     def rows_of(layer):
         return ends_v[0] if layer == 0 else xs_[0]
 
-    def project(layer):
+    def bias_of(layer):
+        return jnp.where(core == 0, gains[layer, 0:1, :], gains[layer, 1:2, :])
+
+    def project_keys(layer):
         rows = rows_of(layer).astype(jnp.float32)
         gain = gains[layer, 2:3, :]
-        bias = jnp.where(core == 0, gains[layer, 0:1, :], gains[layer, 1:2, :])
         normed = (rows * lax.rsqrt(mean_of(rows * rows) + EPS) * gain).astype(jnp.bfloat16)
         n1[layer] = normed
-        weights = wat[layer].reshape(DP, CA)
-        projected = nn(normed, weights[:, : QS + 128]) + bias[:, : QS + 128]
-        turned = turn(projected[:, :QS], tiled(cosine[...]), tiled(sine[...]))
-        own = jnp.concatenate([turned[:, :64], projected[:, QS : QS + 64]], axis=1)
+        bias = bias_of(layer)
+        first = nn(normed, wat[layer, :, :, :, :, 0:128].reshape(DP, 128)) + bias[:, 0:128]
+        values = nn(normed, wat[layer, :, :, :, :, QS : QS + 128].reshape(DP, 128))
+        values = values + bias[:, QS : QS + 128]
+        turned = turn(first, tiled(cosine[...], 128), tiled(sine[...], 128))
+        own = jnp.concatenate([turned[:, :64], values[:, :64]], axis=1)
         kvb[(layer,) + here] = own.astype(jnp.bfloat16).reshape(MB, T, 128)
+
+    def project_queries(layer):
+        projected = nn(n1[layer], wat[layer, :, :, :, :, 0:QS].reshape(DP, QS))
+        projected = projected + bias_of(layer)[:, 0:QS]
+        turned = turn(projected, tiled(cosine[...]), tiled(sine[...]))
         heads = without_first_slot(turned).astype(jnp.bfloat16).astype(jnp.float32) * 0.125
         for batch in range(MB):
             columns = to_columns(heads[batch * T : (batch + 1) * T]).astype(jnp.bfloat16)
             qt[layer, batch] = jnp.concatenate([columns, jnp.zeros_like(columns)], axis=0)
 
-    def attend(layer, batch):
-        queries = jnp.concatenate([qt[layer, batch], all_heads(qm[0, batch])], axis=0)
-        own_queries = jnp.concatenate([qt[layer, batch], all_heads(qm[1, batch])], axis=0)
+    def attend_own(layer, batch):
+        queries = jnp.concatenate([qt[layer, batch], all_heads(qm[1, batch])], axis=0)
         rows = kvb[(layer,) + here + (batch,)]
-        marks = km[pl.ds(pl.multiple_of(chip * T, T), T), :]
-        scores = nn(jnp.concatenate([rows, marks], axis=1), own_queries) + all_heads(ob[batch])
+        scores = nn(jnp.concatenate([rows, km[here]], axis=1), queries) + all_heads(ob[batch])
         top = jnp.max(scores, axis=0, keepdims=True)
         probs = jnp.exp(scores - top)
-        total = jnp.sum(probs, axis=0, keepdims=True)
-        sums = tn(rows, probs.astype(jnp.bfloat16))
-
+        state[batch, 0:1, :] = top
+        state[batch, 1:2, :] = jnp.sum(probs, axis=0, keepdims=True)
+        acc[batch] = tn(rows, probs.astype(jnp.bfloat16))
+
+    def fold(layer, batch, index, carry):
+        top, total, sums = carry
+        queries = jnp.concatenate([qt[layer, batch], all_heads(qm[0, batch])], axis=0)
+        spot = plane(batch, index)
+        rows = kvb[(layer,) + spot + (batch,)].reshape(KB, 128)
+        scores = nn(jnp.concatenate([rows, km[spot].reshape(KB, 128)], axis=1), queries)
+        new_top = jnp.maximum(top, jnp.max(scores, axis=0, keepdims=True))
+        shrink = jnp.exp(top - new_top)
+        probs = jnp.exp(scores - new_top)
+        total = total * shrink + jnp.sum(probs, axis=0, keepdims=True)
+        return new_top, total, sums * shrink + tn(rows, probs.astype(jnp.bfloat16))
+
+    def held(batch):
+        return state[batch, 0:1, :], state[batch, 1:2, :], acc[batch]
+
+    def attend_near(layer, batch):
+        top, total, sums = fold(layer, batch, place[ORDERS[batch][2]], held(batch))
+        state[batch, 0:1, :] = top
+        state[batch, 1:2, :] = total
+        acc[batch] = sums
+
+    def attend_far(layer, batch):
         def step(index, carry):
-            top, total, sums = carry
-            rows = kvb[layer, index, :, :, batch].reshape(KB, 128)
-            marks = km[pl.ds(pl.multiple_of(index * KB, KB), KB), :]
-            scores = nn(jnp.concatenate([rows, marks], axis=1), queries)
-            new_top = jnp.maximum(top, jnp.max(scores, axis=0, keepdims=True))
-            shrink = jnp.exp(top - new_top)
-            probs = jnp.exp(scores - new_top)
-            total = total * shrink + jnp.sum(probs, axis=0, keepdims=True)
-            sums = sums * shrink + tn(rows, probs.astype(jnp.bfloat16))
-            return new_top, total, sums
-
-        top, total, sums = lax.fori_loop(0, (chip + 15) // 16, step, (top, total, sums))
+            return fold(layer, batch, (place[ORDERS[batch][2]] + index) % 4, carry)
+
+        top, total, sums = lax.fori_loop(1, 4, step, held(batch))
         result = (sums / total)[64:, :]
         mixed[layer, batch] = result
         lse[layer, batch] = jnp.broadcast_to(top + jnp.log(total), (8, QS))
@@ -785,13 +810,6 @@
     def nothing():
         pass
 
-    def beside(stages, rounds):
-        rounds = iter(rounds)
-        for index in range(8):
-            stages[index]()
-            if index not in (2, 5):
-                next(rounds)()
-
     def calls(method, *numbers):
         return [functools.partial(method, r) for r in numbers]
 
@@ -800,27 +818,36 @@
             for r in range(ROUNDS):
                 method(r)
 
-    project(0)
-    beside(
-        keys[0],
-        [
-            early.phases[4],
-            nothing,
-            lambda: (early.phases[5](), early.ahead(0)),
-            *calls(early.ahead, 1, 2, 3),
-        ],
-    )
+    project_keys(0)
+    keys[0][0]()
+    project_queries(0)
+    early.phases[4]()
+    keys[0][2]()
+    keys[0][3]()
+    for batch in range(MB):
+        attend_own(0, batch)
+    early.phases[5]()
+    early.ahead(0)
+    keys[0][5]()
+    keys[0][6]()
+    early.ahead(1)
+    attend_near(0, 0)
+    attend_near(0, 1)
+    keys[0][7]()
+    early.ahead(2)
+    attend_near(0, 2)
     keys[0][8]()
+    early.ahead(3)
     rounds_of(early.rest)
     store(kvb.at[0], kv.at[0], 0)
-    attend(0, 0)
     early.pass_on(0)
+    attend_far(0, 0)
     early.pass_on(1)
-    attend(0, 1)
     early.pass_on(2)
+    attend_far(0, 1)
     early.pass_on(3)
     late.phases[0]()
-    attend(0, 2)
+    attend_far(0, 2)
     late.phases[1]()
     branch = branch_of(0)
     early.last()
@@ -830,24 +857,37 @@
     feed_forward(0, branch, [nothing] * 3 + [late.phases[4], nothing])
     late.phases[5]()
     late.ahead(0)
-    late.ahead(1)
     attn[1][8]()
     store(wat, wa, 1)
-    project(1)
-    beside(
-        keys[1], [nothing, nothing, *calls(late.ahead, 2, 3), *calls(late.rest, 0, 1)]
-    )
+    project_keys(1)
+    keys[1][0]()
+    late.ahead(1)
+    project_queries(1)
+    keys[1][2]()
+    keys[1][3]()
+    late.ahead(2)
+    for batch in range(MB):
+        attend_own(1, batch)
+    keys[1][5]()
+    keys[1][6]()
+    late.ahead(3)
+    attend_near(1, 0)
+    attend_near(1, 1)
+    keys[1][7]()
+    late.rest(0)
+    attend_near(1, 2)
     keys[1][8]()
+    late.rest(1)
     late.rest(2)
     late.rest(3)
     store(kvb.at[1], kv.at[1], 3)
-    attend(1, 0)
     late.pass_on(0)
+    attend_far(1, 0)
     late.pass_on(1)
-    attend(1, 1)
     late.pass_on(2)
+    attend_far(1, 1)
     late.pass_on(3)
-    attend(1, 2)
+    attend_far(1, 2)
     branch = branch_of(1)
     late.last()
     early.finish()
@@ -901,7 +941,7 @@
             shape((2, R, FFH), low),
             shape((2, R, DP), low),
             shape((2, 8, 128), full),
-            shape((SEQ, 128), low),
+            shape((4, 4, 4, T, 128), low),
             shape((2, MB, 128, 128), low),
             shape((MB, T, 128), full),
         ),
@@ -920,6 +960,8 @@
             pltpu.VMEM((R, 2 * FFH), full),
             pltpu.VMEM((2, R, DP), full),
             pltpu.VMEM((2, R, DP), full),
+            pltpu.VMEM((MB, 8, QS), full),
+            pltpu.VMEM((MB, 128, QS), full),
             DMA((4,)),
             DMA((4,)),
             DMA((4,)),
@@ -967,7 +1009,7 @@
     wa, wm, kv, gu, ends, xs_, gains, n1, qt, mixed, lse, att, mid, n2, squares, cosine, sine,
     km, qm, ob,
     grads, dx, outv, other, small_out,
-    pool, gbuf, n2t, dmt, wat, mine, theirs, dout, dmid, da, dot_, dqk, low, vlow, kvb, own,
+    pool, gbuf, n2t, dmt, wat, mine, theirs, dout, dmid, da, dot_, acc, low, vlow, kvb, own,
     kh0, kw0, kw1, kw2, slab, got_half, got_whole, spare, mh1, mw1, mw2, ah0, aw0, aw1, aw2,
     sbuf,
     lsem, psem, gsem, usem, xsem, xrsem, ks, kr, hs, hr, os_, or_, ws, wr, ls, ms, mr, as_, ar,
@@ -978,7 +1020,6 @@
     chip = lax.axis_index("dp")
     here = (place["x"], place["y"], place["z"])
     partners = greet(place, core=True, far=True)
-    steps = (chip + 15) // 16
 
     def heads_load(layer):
         return pltpu.make_async_copy(wa.at[layer], wat, lsem.at[2 * layer])
@@ -989,39 +1030,51 @@
     heads_load(1).start()
     keys_load(1).start()
     dout[...] = ends[1].astype(jnp.float32)
-    settle(partners)
     small = [[None] * 4, [None] * 4]
     stored = {}
 
     def swap(slot):
         return send(mine.at[slot], theirs.at[slot], xsem.at[slot], xrsem.at[slot], other_core())
 
-    def back_feed(layer, hooks):
-        def loads(index):
-            start, size = FF_SLOTS[index]
-            slot = index % 2
-            copies = []
-            for part in range(3):
-                copies.append(
-                    pltpu.make_async_copy(
-                        wm.at[layer, :, :, :, :, pl.ds(part * FFH + start, size)],
-                        pool.at[3 * slot + part, :, :, :, :, pl.ds(0, size)],
-                        psem.at[slot, part],
-                    )
+    def feed_loads(layer, index):
+        start, size = FF_SLOTS[index]
+        slot = index % 2
+        copies = []
+        for part in range(3):
+            copies.append(
+                pltpu.make_async_copy(
+                    wm.at[layer, :, :, :, :, pl.ds(part * FFH + start, size)],
+                    pool.at[3 * slot + part, :, :, :, :, pl.ds(0, size)],
+                    psem.at[slot, part],
                 )
-            for part in range(2):
-                copies.append(
-                    pltpu.make_async_copy(
-                        gu.at[layer, :, pl.ds(part * FFH + start, size)],
-                        gbuf.at[slot, part, :, pl.ds(0, size)],
-                        usem.at[slot, part],
-                    )
+            )
+        for part in range(2):
+            copies.append(
+                pltpu.make_async_copy(
+                    gu.at[layer, :, pl.ds(part * FFH + start, size)],
+                    gbuf.at[slot, part, :, pl.ds(0, size)],
+                    usem.at[slot, part],
                 )
-            return copies
-
+            )
+        return copies
+
+    def feed_start(layer):
         for index in range(2):
-            for one in loads(index):
+            for one in feed_loads(layer, index):
                 one.start()
+
+    feed_start(1)
+
+    def back_feed(layer, stream, hooks):
+        sends = {
+            2: ((0, 0),),
+            3: ((0, 1),),
+            4: ((0, 2),),
+            6: ((0, 3),),
+            7: ((1, 0),),
+            8: ((1, 1),),
+            9: ((1, 2),),
+        }
         grad_in = dout[...]
         grad_low = grad_in.astype(jnp.bfloat16)
         n2t[...] = n2[layer].astype(jnp.float32).T.astype(jnp.bfloat16)
@@ -1030,7 +1083,7 @@
         for index, (start, size) in enumerate(FF_SLOTS):
             slot = index % 2
             hooks.get(index, lambda: None)()
-            for one in loads(index):
+            for one in feed_loads(layer, index):
                 one.wait()
 
             def weights(part, slot=slot, size=size):
@@ -1046,7 +1099,7 @@
             grad_up = (grad_hidden * gate * sigma).astype(jnp.bfloat16)
             mine[0] += nt(grad_gate, weights(0)) + nt(grad_up, weights(1))
             if index + 2 < len(FF_SLOTS):
-                for one in loads(index + 2):
+                for one in feed_loads(layer, index + 2):
                     one.start()
             products = ((n2t, grad_gate), (n2t, grad_up), (dmt, hidden))
             for part, (left, right) in enumerate(products):
@@ -1062,6 +1115,12 @@
                     gsem.at[slot, part],
                 )
                 stored[held].start()
+            for half, r in sends.get(index, ()):
+                stream.group(half, r)
+        for held in list(stored):
+            stored.pop(held).wait()
+        stream.group(1, 3)
+        stream.load()
         one = swap(0)
         one.start()
         one.wait()
@@ -1077,69 +1136,62 @@
         for batch in range(MB):
             columns = to_columns(turned[batch * T : (batch + 1) * T]).astype(jnp.bfloat16)
             dot_[batch] = jnp.concatenate([jnp.zeros_like(columns), columns], axis=0)
-        for held in list(stored):
-            stored.pop(held).wait()
-
-    def back_attend(layer, batch):
-        if batch == 0:
-            keys_load(layer).wait()
+
+    def terms(layer, batch, rows, scores):
         slopes_out = dot_[batch]
-        queries = qt[layer, batch]
-        marked = jnp.concatenate([queries, all_heads(qm[0, batch])], axis=0)
-        log_total = lse[layer, batch, 0:1, :]
         inner = jnp.sum(
             mixed[layer, batch] * slopes_out[64:, :].astype(jnp.float32), axis=0, keepdims=True
         )
-
-        def terms(rows, scores):
-            probs = jnp.exp(scores - log_total)
-            slopes = (probs * (nn(rows, slopes_out) - inner)).astype(jnp.bfloat16)
-            both = nt(slopes, queries) + nt(probs.astype(jnp.bfloat16), slopes_out)
-            return both.astype(jnp.bfloat16), tn(rows, slopes)
-
-        own_rows = kvb[here + (batch,)]
-        marks = km[pl.ds(pl.multiple_of(chip * T, T), T), :]
-        scores = nn(
-            jnp.concatenate([own_rows, marks], axis=1),
-            jnp.concatenate([queries, all_heads(qm[1, batch])], axis=0),
-        )
-        own_both, sums = terms(own_rows, scores + all_heads(ob[batch]))
-
-        def step(index, sums):
-            rows = kvb[index, :, :, batch].reshape(KB, 128)
-            marks = km[pl.ds(pl.multiple_of(index * KB, KB), KB), :]
-            both, more = terms(rows, nn(jnp.concatenate([rows, marks], axis=1), marked))
-            kvb[index, :, :, batch] = both.reshape(4, 4, T, 128)
-            return sums + more
-
-        sums = lax.fori_loop(0, steps, step, sums)
-
-        def clear(index, nothing):
-            kvb[index, :, :, batch] = jnp.zeros((4, 4, T, 128), jnp.bfloat16)
-            return nothing
-
-        lax.fori_loop(steps, 4, clear, 0)
-        kvb[here + (batch,)] = own_both
-        dqk[pl.ds(batch * T, T), :] = to_rows(sums[:64, :] * 0.125)
-
-    def back_project(layer):
+        probs = jnp.exp(scores - lse[layer, batch, 0:1, :])
+        slopes = (probs * (nn(rows, slopes_out) - inner)).astype(jnp.bfloat16)
+        both = nt(slopes, qt[layer, batch]) + nt(probs.astype(jnp.bfloat16), slopes_out)
+        return both.astype(jnp.bfloat16), tn(rows[:, :64], slopes)
+
+    def back_plane(layer, batch, offset, begin=False):
+        spot = plane(batch, (place[ORDERS[batch][2]] + offset) % 4)
+        rows = kvb[spot + (batch,)].reshape(KB, 128)
+        marked = jnp.concatenate([qt[layer, batch], all_heads(qm[0, batch])], axis=0)
+        scores = nn(jnp.concatenate([rows, km[spot].reshape(KB, 128)], axis=1), marked)
+        both, more = terms(layer, batch, rows, scores)
+        kvb[spot + (batch,)] = both.reshape(4, 4, T, 128)
+        acc[batch] = more if begin else acc[batch] + more
+
+    def back_own(layer, batch):
+        rows = kvb[here + (batch,)]
+        back_plane(layer, batch, 0)
+        marked = jnp.concatenate([qt[layer, batch], all_heads(qm[1, batch])], axis=0)
+        scores = nn(jnp.concatenate([rows, km[here]], axis=1), marked) + all_heads(ob[batch])
+        both, more = terms(layer, batch, rows, scores)
+        kvb[here + (batch,)] = both
+        acc[batch] += more
+
+    def back_queries(layer):
+        whole = jnp.concatenate([to_rows(acc[batch] * 0.125) for batch in range(MB)], axis=0)
+        turned = turn(whole, tiled(cosine[...]), -tiled(sine[...])).astype(jnp.bfloat16)
+        low[layer] = turned
+        mine[1] = nt(turned, wat[:, :, :, :, 0:QS].reshape(DP, QS))
+
+    def back_keys(layer):
         key_grads = own[...].reshape(R, 128)
-        whole = jnp.concatenate([key_grads[:, :64], dqk[:, 64:]], axis=1)
-        turned = turn(whole, tiled(cosine[...]), -tiled(sine[...])).astype(jnp.bfloat16)
-        values = jnp.concatenate(
-            [key_grads[:, 64:], jnp.zeros((R, QS - 64), jnp.float32)], axis=1
+        none = jnp.zeros((R, 64), jnp.float32)
+        turned = turn(
+            jnp.concatenate([key_grads[:, :64], none], axis=1),
+            tiled(cosine[...], 128),
+            -tiled(sine[...], 128),
         ).astype(jnp.bfloat16)
-        low[layer] = turned
+        values = jnp.concatenate([key_grads[:, 64:], none], axis=1).astype(jnp.bfloat16)
+        low[layer, :, 0:128] = low[layer, :, 0:128] + turned
         vlow[layer] = values
         small[layer][2] = jnp.concatenate(
             [
-                jnp.sum(turned.astype(jnp.float32), axis=0, keepdims=True),
+                jnp.sum(low[layer].astype(jnp.float32), axis=0, keepdims=True),
                 jnp.sum(values.astype(jnp.float32), axis=0, keepdims=True),
+                jnp.zeros((1, QS - 128), jnp.float32),
             ],
             axis=1,
         )
-        mine[1] = nt(turned, wat[:, :, :, :, :QS].reshape(DP, QS)) + nt(
-            values, wat[:, :, :, :, QS:].reshape(DP, QS)
+        mine[1] += nt(turned, wat[:, :, :, :, 0:128].reshape(DP, 128)) + nt(
+            values, wat[:, :, :, :, QS : QS + 128].reshape(DP, 128)
         )
         one = swap(1)
         one.start()
@@ -1156,16 +1208,26 @@
         else:
             dout[...] = result.astype(jnp.float32)
 
-    def heads_products(layer):
+    def put(slot, start, product):
+        wide = product.shape[1]
+        pool[slot, :, :, :, :, pl.ds(start, wide)] = product.astype(jnp.bfloat16).reshape(
+            4, 4, 4, 16, wide
+        )
+
+    def query_products(layer):
         first = tn(n1[layer], low[layer])
-        second = tn(n1[layer], vlow[layer]) + tn(da[layer], att[layer])
+        second = tn(da[layer], att[layer])
         for side, product in enumerate((first, second)):
-            for part in range(2):
-                pool[4 * layer + 2 * side + part] = (
-                    product[:, part * SLOT : (part + 1) * SLOT]
-                    .astype(jnp.bfloat16)
-                    .reshape(4, 4, 4, 16, SLOT)
-                )
+            put(4 * layer + 2 * side, 128, product[:, 128:SLOT])
+            put(4 * layer + 2 * side + 1, 0, product[:, SLOT:])
+
+    def key_products(layer):
+        put(4 * layer, 0, tn(n1[layer], low[layer, :, 0:128]))
+        put(
+            4 * layer + 2,
+            0,
+            tn(n1[layer], vlow[layer]) + tn(da[layer], att[layer, :, 0:128]),
+        )
 
     def total(terms):
         return sum(term[...].astype(jnp.float32) for term in terms)
@@ -1251,71 +1313,73 @@
 
         return begin, end
 
-    def beside(stages, rounds):
-        rounds = iter(rounds)
-        for index in range(8):
-            stages[index]()
-            if index not in (2, 5):
-                next(rounds)()
-
-    def calls(method, *numbers):
-        return [functools.partial(method, r) for r in numbers]
-
-    def nothing():
-        pass
-
     def rounds_of(*methods):
         for method in methods:
             for r in range(ROUNDS):
                 method(r)
 
-    back_feed(1, {})
-    rounds_of(early.ahead, early.rest)
-    for batch in range(MB):
-        back_attend(1, batch)
-    for stage in keys[1][:8]:
-        stage()
-    rounds_of(early.pass_on)
+    def back_attend(layer, stream):
+        keys_load(layer).wait()
+        for batch in range(MB):
+            back_plane(layer, batch, 2, True)
+        keys[layer][0]()
+        stream.pass_on(0)
+        for batch in range(MB):
+            back_plane(layer, batch, 1)
+        stream.pass_on(1)
+        for batch in range(MB):
+            back_plane(layer, batch, 3)
+        keys[layer][1]()
+        stream.pass_on(2)
+        for batch in range(MB):
+            back_own(layer, batch)
+        keys[layer][2]()
+        keys[layer][3]()
+        stream.pass_on(3)
+        back_queries(layer)
+        keys[layer][5]()
+        keys[layer][6]()
+        stream.third()
+        stream.phases[0]()
+
+    def settle_early():
+        early.phases[5]()
+        early.finish()
+        for axis in "xyz":
+            for distance in (1, -1, 2):
+                pl.semaphore_signal(
+                    credit,
+                    inc=1,
+                    device_id=chip_id(moved(place, axis, distance)),
+                    device_id_type=MESH,
+                )
+        pl.semaphore_wait(credit, 9)
+
+    back_feed(1, early, {1: lambda: settle(partners)})
+    back_attend(1, early)
+    feed_start(0)
     keys[1][8]()
     keys[1][9]()
     keys_load(0).start()
-    back_project(1)
+    back_keys(1)
     heads_load(0).start()
     back_feed(
         0,
+        late,
         {
-            2: lambda: (early.third(), early.phases[0]()),
-            4: early.phases[1],
-            6: lambda: (early.phases[2](), early.phases[3]()),
-            9: early.phases[5],
+            0: early.phases[1],
+            1: lambda: (early.phases[2](), early.phases[3]()),
+            2: settle_early,
         },
     )
-    early.finish()
-    for axis in "xyz":
-        for distance in (1, -1, 2):
-            pl.semaphore_signal(
-                credit, inc=1, device_id=chip_id(moved(place, axis, distance)), device_id_type=MESH
-            )
-    pl.semaphore_wait(credit, 9)
-    rounds_of(late.ahead)
-    back_attend(0, 0)
-    late.pass_on(0)
-    late.pass_on(1)
-    back_attend(0, 1)
-    late.pass_on(2)
-    late.pass_on(3)
-    late.rest(0)
-    back_attend(0, 2)
-    beside(
-        keys[0],
-        [nothing, *calls(late.rest, 1, 2, 3), functools.partial(heads_products, 1), nothing],
-    )
+    back_attend(0, late)
+    query_products(1)
+    key_products(1)
+    query_products(0)
     keys[0][8]()
     keys[0][9]()
-    late.third()
-    late.phases[0]()
-    back_project(0)
-    heads_products(0)
+    back_keys(0)
+    key_products(0)
     sbuf[0] = jnp.concatenate(small[0] + small[1], axis=0)
     sums = [total_small(phase, axis) for phase, axis in enumerate("xyz")]
     sums[0][0]()
@@ -1374,9 +1438,9 @@
             pltpu.VMEM((R, DP), full),
             pltpu.VMEM((2, R, DP), low),
             pltpu.VMEM((MB, 128, QS), low),
-            pltpu.VMEM((R, QS), full),
+            pltpu.VMEM((MB, 64, QS), full),
             pltpu.VMEM((2, R, QS), low),
-            pltpu.VMEM((2, R, QS), low),
+            pltpu.VMEM((2, R, 128), low),
             pltpu.VMEM((4, 4, 4, MB, T, 128), low),
             pltpu.VMEM((MB, T, 128), full),
         ]

time: 435 us -> 412 us (0.947)
  Pallas kernels: 427 us -> 403 us
    pallas_call x1, Pallas kernels: 228 us -> 205 us  [backward(): pl.pallas_call(backward_kernel, out_shape=(shape((2, 4, 4, 4, 16, CM), lo...]
where the time goes in v5:
time: 412 us; the launch traced here: 405 us
  Pallas kernels  403 us (98%)
    pallas_call x1, Pallas kernels, backward(): pl.pallas_call(backward_kernel, out_shape=(shape((2, 4, 4, 4, 16, CM), lo...  205 us
    pallas_call x1, Pallas kernels, forward(): pl.pallas_call(forward_kernel, out_shape=(shape((2, 4, 4, 4, 16, CA), low...  194 us

profile of v5, /device:TPU:1, one launch (start us, length us, event | category | flops | bytes accessed | tf_op | source)
XLA Modules:
  0.0 404.9 jit_solution(7921159579530320887)
XLA Ops:
  0.7 0.8 fusion
  1.5 194.4 %forward.1 = (bf16[2,4,4,4,16,1024]{5,4,3,2,1,0:T(8,128)(2,1)}, bf16[2,4,4,4,16,7296]{5,4,3,2,1,0:T(8,128)(2,1)}, bf16[2,4,4,4,3,64,128]{6,5,4,3,2,1,0:T(8,128)(...) custom-call(bf16[14,9728]{1,0:T(8,128)(2,1)} %bitcast.14, ...), custom_call_target="tpu_custom_call" | custom-call | tf_op jit(solution)/shard_map/forward/pallas_call | solution.py:925
  195.9 205.0 %backward.1 = (bf16[2,4,4,4,16,7296]{5,4,3,2,1,0:T(8,128)(2,1)}, bf16[192,1024]{1,0:T(8,128)(2,1)}, f32[2,16,8320]{2,1,0:T(8,128)}, f32[16,8320]{1,0:T(8,128)}, f32[8,1024]{1,0:T(8,128)}) custom-call(bf16[2,4,4,4,16,1024]{5,4,3,2,1,0:T(8,128)(2,1)} %get-tuple-element.38.wa, bf16[2,4,4,4,16,7296]{5,4,3,2,1,0:T(8,128)(2,1)} %get-tuple-element.39.wm, ...), custom_call_target="tpu_custom_call" | custom-call | tf_op jit(solution)/shard_map/backward/pallas_call | solution.py:1418
  400.9 3.5 assemble.1
  (2 shorter events, 0.0 us)

commit v6 on v5

--- a/solution.py
+++ b/solution.py
@@ -32,7 +32,6 @@
 CM, CA = 3 * FFH, 2 * QS
 M_THIRDS = ((0, FFH), (FFH, FFH), (2 * FFH, FFH))
 A_THIRDS = ((0, 384), (384, 384), (768, 256))
-FF_CHUNKS = ((0, 512), (512, 512), (1024, 512), (1536, 512), (2048, 384))
 
 
 def position():
@@ -185,25 +184,22 @@
         one.start()
         self.pending.append(one)
 
-    def ahead(self, r):
+    def group(self, half, r):
         for j, k, distance in TURNS:
-            self.start(self.part(j, k, distance, k, r, self.place))
-
-    def rest(self, r):
-        for j, k, distance in TURNS:
-            self.start(self.part(j, k, distance, 1 - k, r, self.place))
-
-    def pass_on(self, r):
-        for j, k, distance in TURNS:
+            self.start(self.part(j, k, distance, half, r, self.place))
+
+    def pass_on(self, half, r):
+        distance = (1, -1)[half]
+        for j in range(3):
             back = self.whose(j, -distance)
-            self.part(j, k, distance, k, r, back).wait_recv()
-            self.start(self.passed(j, k, distance, r, back))
-
-    def last(self):
-        for j, k, distance in TURNS:
-            for r in range(ROUNDS):
-                self.part(j, k, distance, 1 - k, r, self.whose(j, -distance)).wait_recv()
-                self.passed(j, k, distance, r, self.whose(j, 2)).wait_recv()
+            self.part(j, half, distance, half, r, back).wait_recv()
+            self.start(self.passed(j, half, distance, r, back))
+
+    def ready(self, half, r):
+        for j in range(3):
+            distance = (1, -1)[1 - half]
+            self.part(j, 1 - half, distance, half, r, self.whose(j, -distance)).wait_recv()
+            self.passed(j, half, (1, -1)[half], r, self.whose(j, 2)).wait_recv()
 
     def finish(self):
         self.done()
@@ -538,7 +534,7 @@
 
 def forward_kernel(
     gate_up, down, qkv, out_w, bias_in, gains_in, ends, segments, valid, cosine, sine,
-    wa, wm, kv, gu, cot, gains, n1, qt, mixed, lse, att, mid, n2, hid, xs_, sq, km, qm, ob,
+    wa, wm, kv, gu, cot, gains, n1, qt, mixed, lse, att, mid, n2, xs_, sq, km, qm, ob,
     ends_v, small_v, give_a, give_m, stage_a, stage_m, wat, wml, kvb, gu_v, mine, theirs,
     state, acc, lsem, ssem, rsem, a_s, a_r, m_s, m_r, mp_s, mp_r, mq_s, mq_r, k_s, k_r, osem, wsem, xsem,
     xrsem,
@@ -671,20 +667,20 @@
     for index in range(2, 8):
         attn[0][index]()
         attn[1][index]()
-    early.phases[2]()
-    early.phases[3]()
+        if index == 3:
+            early.phases[2]()
+            early.phases[3]()
     arrive(2)
     arrive(3)
     cot[...] = ends_v[...]
     gains[...] = small_v[...]
     attn[0][8]()
 
-    outs = []
+    outs = {}
 
     def store(src, dst, index):
-        one = pltpu.make_async_copy(src, dst, osem.at[index])
-        one.start()
-        outs.append(one)
+        outs[index] = pltpu.make_async_copy(src, dst, osem.at[index])
+        outs[index].start()
 
     def rows_of(layer):
         return ends_v[0] if layer == 0 else xs_[0]
@@ -775,7 +771,7 @@
     def feed_forward(layer, branch, hooks):
         normed = n2[layer]
         sums = jnp.zeros((R, DP), jnp.float32)
-        for index, (start, size) in enumerate(FF_CHUNKS):
+        for index, (start, size) in enumerate(PARTS[0] + PARTS[1]):
             hooks[index]()
 
             def weights(first, start=start, size=size):
@@ -786,7 +782,6 @@
             gu_v[:, pl.ds(start, size)] = gate
             gu_v[:, pl.ds(FFH + start, size)] = up
             hidden = (gate * jax.nn.sigmoid(gate) * up).astype(jnp.bfloat16)
-            hid[layer, :, pl.ds(start, size)] = hidden
             sums = sums + nt(hidden, weights(2 * FFH))
         store(gu_v, gu.at[layer], 4 + layer)
         mine[1] = sums
@@ -810,13 +805,15 @@
     def nothing():
         pass
 
-    def calls(method, *numbers):
-        return [functools.partial(method, r) for r in numbers]
-
-    def rounds_of(*methods):
-        for method in methods:
-            for r in range(ROUNDS):
-                method(r)
+    def chain(*steps):
+        def run():
+            for step in steps:
+                step()
+
+        return run
+
+    def do(method, *numbers):
+        return functools.partial(method, *numbers)
 
     project_keys(0)
     keys[0][0]()
@@ -827,93 +824,118 @@
     for batch in range(MB):
         attend_own(0, batch)
     early.phases[5]()
-    early.ahead(0)
+    early.group(0, 0)
     keys[0][5]()
     keys[0][6]()
-    early.ahead(1)
+    early.group(0, 1)
     attend_near(0, 0)
     attend_near(0, 1)
     keys[0][7]()
-    early.ahead(2)
+    early.group(0, 2)
     attend_near(0, 2)
     keys[0][8]()
-    early.ahead(3)
-    rounds_of(early.rest)
+    early.group(0, 3)
+    early.pass_on(0, 0)
+    early.pass_on(0, 1)
+    early.group(1, 0)
     store(kvb.at[0], kv.at[0], 0)
-    early.pass_on(0)
     attend_far(0, 0)
-    early.pass_on(1)
-    early.pass_on(2)
+    early.pass_on(0, 2)
+    early.group(1, 1)
     attend_far(0, 1)
-    early.pass_on(3)
+    early.pass_on(0, 3)
+    early.group(1, 2)
+    early.pass_on(1, 0)
+    attend_far(0, 2)
+    early.group(1, 3)
+    early.pass_on(1, 1)
     late.phases[0]()
-    attend_far(0, 2)
-    late.phases[1]()
     branch = branch_of(0)
-    early.last()
+    early.pass_on(1, 2)
+    feed_forward(
+        0,
+        branch,
+        [
+            do(early.ready, 0, 0),
+            chain(do(early.ready, 0, 1), do(early.pass_on, 1, 3), late.phases[2], late.phases[3]),
+            do(early.ready, 0, 2),
+            do(early.ready, 0, 3),
+            do(early.ready, 1, 0),
+            do(early.ready, 1, 1),
+            do(early.ready, 1, 2),
+            chain(do(early.ready, 1, 3), late.phases[4]),
+        ],
+    )
     store(wml, wm.at[0], 2)
-    late.phases[2]()
-    late.phases[3]()
-    feed_forward(0, branch, [nothing] * 3 + [late.phases[4], nothing])
     late.phases[5]()
-    late.ahead(0)
+    late.group(0, 0)
     attn[1][8]()
     store(wat, wa, 1)
     project_keys(1)
     keys[1][0]()
-    late.ahead(1)
+    late.group(0, 1)
     project_queries(1)
     keys[1][2]()
     keys[1][3]()
-    late.ahead(2)
+    late.group(0, 2)
     for batch in range(MB):
         attend_own(1, batch)
     keys[1][5]()
     keys[1][6]()
-    late.ahead(3)
+    late.group(0, 3)
     attend_near(1, 0)
     attend_near(1, 1)
     keys[1][7]()
-    late.rest(0)
+    late.pass_on(0, 0)
     attend_near(1, 2)
     keys[1][8]()
-    late.rest(1)
-    late.rest(2)
-    late.rest(3)
+    late.pass_on(0, 1)
+    late.pass_on(0, 2)
+    late.pass_on(0, 3)
+    late.group(1, 0)
     store(kvb.at[1], kv.at[1], 3)
-    late.pass_on(0)
     attend_far(1, 0)
-    late.pass_on(1)
-    late.pass_on(2)
+    late.group(1, 1)
+    late.group(1, 2)
+    late.pass_on(1, 0)
     attend_far(1, 1)
-    late.pass_on(3)
+    late.group(1, 3)
+    late.pass_on(1, 1)
     attend_far(1, 2)
+    early.finish()
+    outs[2].wait()
+    outs[4].wait()
     branch = branch_of(1)
-    late.last()
-    early.finish()
-    outs[1].wait()
-    outs[2].wait()
-    loads = []
-    for index, (start, size) in enumerate(FF_CHUNKS):
+    late.pass_on(1, 2)
+    late.pass_on(1, 3)
+
+    def loads(index):
+        start, size = (PARTS[0] + PARTS[1])[index]
+        copies = []
         for part in range(3):
             cols = pl.ds(part * FFH + start, size)
-            loads.append(
+            copies.append(
                 pltpu.make_async_copy(
-                    wm.at[1, :, :, :, :, cols],
-                    wml.at[:, :, :, :, cols],
-                    wsem.at[3 * index + part],
+                    wm.at[1, :, :, :, :, cols], wml.at[:, :, :, :, cols], wsem.at[3 * index + part]
                 )
             )
-    for one in loads:
-        one.start()
-
-    def ready(index):
-        for one in loads[3 * index : 3 * index + 3]:
+        return copies
+
+    def fetch(index):
+        late.ready(index // ROUNDS, index % ROUNDS)
+        for one in loads(index):
+            one.start()
+
+    def fetched(index):
+        if index + 1 < 2 * ROUNDS:
+            fetch(index + 1)
+        for one in loads(index):
             one.wait()
 
-    feed_forward(1, branch, [functools.partial(ready, index) for index in range(5)])
-    for index, one in enumerate(outs):
-        if index not in (1, 2):
+    fetch(0)
+    feed_forward(1, branch, [do(fetched, index) for index in range(2 * ROUNDS)])
+    for index, one in outs.items():
+        if index not in (2, 4):
             one.wait()
     late.finish()
     for stages in attn + keys:
@@ -938,7 +960,6 @@
             shape((2, R, QS), low),
             shape((2, R, DP), full),
             shape((2, R, DP), low),
-            shape((2, R, FFH), low),
             shape((2, R, DP), low),
             shape((2, 8, 128), full),
             shape((4, 4, 4, T, 128), low),
@@ -946,7 +967,7 @@
             shape((MB, T, 128), full),
         ),
         in_specs=[VMEM] * 11,
-        out_specs=(ANY,) * 4 + (VMEM,) * 15,
+        out_specs=(ANY,) * 4 + (VMEM,) * 14,
         scratch_shapes=[
             pltpu.VMEM((2, R, DP), low),
             pltpu.VMEM((2, 8, DP), full),
@@ -976,7 +997,7 @@
             DMA((2, 3, 3, 4)),
             DMA((2, 3, 3, 4)),
             DMA((6,)),
-            DMA((15,)),
+            DMA((24,)),
             DMA((2,)),
             DMA((2,)),
         ],
@@ -1065,7 +1086,7 @@
 
     feed_start(1)
 
-    def back_feed(layer, stream, hooks):
+    def back_feed(layer, stream, hooks, free=2):
         sends = {
             2: ((0, 0),),
             3: ((0, 1),),
@@ -1115,8 +1136,13 @@
                     gsem.at[slot, part],
                 )
                 stored[held].start()
-            for half, r in sends.get(index, ()):
-                stream.group(half, r)
+            if index == free:
+                for earlier in range(2, index):
+                    for half, r in sends.get(earlier, ()):
+                        stream.group(half, r)
+            if index >= free:
+                for half, r in sends.get(index, ()):
+                    stream.group(half, r)
         for held in list(stored):
             stored.pop(held).wait()
         stream.group(1, 3)
@@ -1368,9 +1394,10 @@
         late,
         {
             0: early.phases[1],
-            1: lambda: (early.phases[2](), early.phases[3]()),
-            2: settle_early,
+            2: lambda: (early.phases[2](), early.phases[3]()),
+            4: settle_early,
         },
+        4,
     )
     back_attend(0, late)
     query_products(1)
@@ -1579,7 +1606,7 @@
     sine = jnp.sin(angles) * sign[None, :]
 
     (
-        wa, wm, kv, gu, ends_all, gains, n1, qt, mixed, lse, att, mid, n2, _, xs_, sq, km, qm, ob,
+        wa, wm, kv, gu, ends_all, gains, n1, qt, mixed, lse, att, mid, n2, xs_, sq, km, qm, ob,
     ) = forward(
         gate_up_weight[0],
         down_weight[0],

time: 412 us -> 400 us (0.971)
  Pallas kernels: 403 us -> 391 us
    pallas_call x1, Pallas kernels: 194 us -> 186 us  [forward(): pl.pallas_call(forward_kernel, out_shape=(shape((2, 4, 4, 4, 16, CA), low...]
where the time goes in v6:
time: 400 us; the launch traced here: 393 us
  Pallas kernels  391 us (98%)
    pallas_call x1, Pallas kernels, backward(): pl.pallas_call(backward_kernel, out_shape=(shape((2, 4, 4, 4, 16, CM), lo...  201 us
    pallas_call x1, Pallas kernels, forward(): pl.pallas_call(forward_kernel, out_shape=(shape((2, 4, 4, 4, 16, CA), low...  186 us

profile of v6, /device:TPU:1, one launch (start us, length us, event | category | flops | bytes accessed | tf_op | source)
XLA Modules:
  0.0 392.9 jit_solution(6979508173384952258)
XLA Ops:
  0.7 0.8 fusion
  1.5 186.3 %forward.1 = (bf16[2,4,4,4,16,1024]{5,4,3,2,1,0:T(8,128)(2,1)}, bf16[2,4,4,4,16,7296]{5,4,3,2,1,0:T(8,128)(2,1)}, bf16[2,4,4,4,3,64,128]{6,5,4,3,2,1,0:T(8,128)(...) custom-call(bf16[14,9728]{1,0:T(8,128)(2,1)} %bitcast.14, ...), custom_call_target="tpu_custom_call" | custom-call | tf_op jit(solution)/shard_map/forward/pallas_call | solution.py:947
  187.8 201.1 %backward.1 = (bf16[2,4,4,4,16,7296]{5,4,3,2,1,0:T(8,128)(2,1)}, bf16[192,1024]{1,0:T(8,128)(2,1)}, f32[2,16,8320]{2,1,0:T(8,128)}, f32[16,8320]{1,0:T(8,128)}, f32[8,1024]{1,0:T(8,128)}) custom-call(bf16[2,4,4,4,16,1024]{5,4,3,2,1,0:T(8,128)(2,1)} %get-tuple-element.38.wa, bf16[2,4,4,4,16,7296]{5,4,3,2,1,0:T(8,128)(2,1)} %get-tuple-element.39.wm, ...), custom_call_target="tpu_custom_call" | custom-call | tf_op jit(solution)/shard_map/backward/pallas_call | solution.py:1445
  388.9 3.5 assemble.1
  (2 shorter events, 0.0 us)
